TPU v7x, 32 devices: a whole 2x2x4 slice. The times are simulated.
32 devices in a mesh: col: 4 (over z), tm: 8 (over y, x, core).
Axes of the slice: x: 2, y: 2, z: 4, core: 2. Of those that a mesh axis runs over, the one named last changes fastest.
Arguments:
- record: float32 [8192, 1024], P('tm', 'col'), as said below
- plan: int32 [3, 4], P(None, 'col'), may hold values 0 or 1
Outputs:
- rotated: float32 [8192, 1024], P('tm', 'col')
- column_rms: float32 [1024], P('col')
Inputs may be any that keep to these rules, and one draw needn't show every extreme that they name: `record`: each column is independent noise scaled by a column factor and a time factor, plus a shared wave with a loading per column.
All inputs are finite; a program needn't handle non-finite values. No bound on the sum of `plan` on one device may be relied on, other than what follows from the above.
Results may differ from a plain program's by a relative error of at most 0.0003.
Values sent between devices are 32-bit elements; how exact they have to be, the bound alone decides.
No kernel may reach another device: no remote copies, remote signals or barrier semaphores. Data moves between devices by JAX's collectives and lax.ppermute only.
A program may use at most 64 MiB of HBM per device.

v0:
```python
import functools
import jax
import jax.numpy as jnp
from jax import lax
from jax.experimental import pallas as pl
from jax.experimental.pallas import tpu as pltpu
from jax.sharding import PartitionSpec as P

epsilon = 1e-06
F32 = jnp.float32
BF16 = jnp.bfloat16
NN = (((1,), (0,)), ((), ()))
NT = (((1,), (1,)), ((), ()))
TN = (((0,), (0,)), ((), ()))
VMEM = pl.BlockSpec(memory_space=pltpu.VMEM)
SMEM = pl.BlockSpec(memory_space=pltpu.SMEM)


def split(x):
    high = x.astype(BF16)
    return high, (x - high.astype(F32)).astype(BF16)


def dot3(a, b, dims=NN):
    one = functools.partial(lax.dot_general, dimension_numbers=dims, preferred_element_type=F32)
    return one(a[0], b[0]) + (one(a[0], b[1]) + one(a[1], b[0]))


def identity_of(width):
    shape = (width, width)
    return (lax.broadcasted_iota(jnp.int32, shape, 0) == lax.broadcasted_iota(jnp.int32, shape, 1)).astype(F32)


def gram_of(first, second):
    width = first.shape[1]
    cross = dot3(split(first), split(second), TN)
    tail = [
        jnp.sum(first * first, axis=0, keepdims=True),
        jnp.sum(second * second, axis=0, keepdims=True),
        jnp.zeros((6, width), F32),
    ]
    return jnp.concatenate([cross] + tail, axis=0)


def inverse(skew, error_ref, total_ref):
    width = skew[0].shape[0]
    square = dot3(skew, skew, NT)
    bound = jnp.minimum(jnp.max(jnp.sum(jnp.abs(square), axis=0)), jnp.sqrt(jnp.sum(square * square)))
    identity = identity_of(width)
    scale = 2.0 / (bound + 2.0)
    error_ref[...] = (1.0 - scale) * identity - scale * square
    total_ref[...] = scale * identity

    def step(error_bound):
        grow = 2.0 / (2.0 - error_bound * error_bound)
        error, total = error_ref[...], total_ref[...]
        both = dot3(split(jnp.concatenate([error, total], axis=0)), split(error))
        total_ref[...] = grow * (total + both[width:])
        error_ref[...] = (1.0 - grow) * identity + grow * both[:width]
        return error_bound * error_bound / (2.0 - error_bound * error_bound)

    lax.while_loop(lambda error_bound: error_bound > 1e-3, step, bound / (bound + 2.0))
    total = total_ref[...]
    parts = split(total)
    residual = identity - total - dot3(split(square), parts)
    return total + dot3(parts, split(residual))


def rotated_halves(s_ref, first, second, error_ref, total_ref):
    skew = split(s_ref[...])
    inner = inverse(skew, error_ref, total_ref)
    mixed = dot3(split(first + dot3(split(second), skew, NT)), split(inner))
    return 2.0 * mixed - first, second - 2.0 * dot3(split(mixed), skew)


def gram_kernel(pair_ref, gram_ref):
    width = pair_ref.shape[1] // 2
    gram_ref[...] = gram_of(pair_ref[:, :width], pair_ref[:, width:])


def ratio_kernel(*refs):
    parts, s_ref = refs[:-1], refs[-1]
    gram = functools.reduce(lambda x, y: x + y, [ref[...] for ref in parts])
    width = gram.shape[1]
    cross, second_diag = gram[:width], gram[width + 1 : width + 2]
    first_diag = jnp.sum(identity_of(width) * gram[width : width + 1], axis=1, keepdims=True)
    difference = first_diag - second_diag
    s_ref[...] = (
        cross * difference / (2.0 * (difference * difference + 4.0 * cross * cross + 0.01 * first_diag * second_diag))
    )


def own_kernel(plan_ref, s_ref, pair_ref, staying_ref, error_ref, total_ref):
    width = s_ref.shape[0]
    first, second = rotated_halves(s_ref, pair_ref[:, :width], pair_ref[:, width:], error_ref, total_ref)
    staying_ref[...] = jnp.where(plan_ref[0] == 1, first, second)


def neighbour_kernel(last, halves, plan_ref, s_ref, staying_ref, *refs):
    width = s_ref.shape[0]
    if halves == 2:
        first, second = refs[0][...], refs[1][...]
        refs = refs[2:]
    else:
        first, second = refs[0][:, :width], refs[0][:, width:]
        refs = refs[1:]
    *outs, error_ref, total_ref = refs
    first, second = rotated_halves(s_ref, first, second, error_ref, total_ref)
    moves_second = plan_ref[0] == 1
    moving = jnp.where(moves_second, second, first)
    staying = staying_ref[...]
    pair_ref, gram_ref = outs[:2]
    pair_ref[:, :width] = staying
    pair_ref[:, width:] = moving
    if last:
        gram_ref[...] = jnp.concatenate(
            [
                jnp.sum(staying * staying, axis=0, keepdims=True),
                jnp.sum(moving * moving, axis=0, keepdims=True),
                jnp.zeros((6, width), F32),
            ],
            axis=0,
        )
    else:
        gram_ref[...] = gram_of(staying, moving)
        outs[2][...] = moving
        outs[3][...] = jnp.where(moves_second, first, second)


def call(kernel, operands, outs, scratch=(), plan=None, name=None):
    specs = [SMEM] * (plan is not None) + [VMEM] * len(operands)
    return pl.pallas_call(
        kernel,
        out_shape=[jax.ShapeDtypeStruct(shape, F32) for shape in outs],
        in_specs=specs,
        out_specs=[VMEM] * len(outs),
        scratch_shapes=list(scratch),
        compiler_params=pltpu.CompilerParams(vmem_limit_bytes=48 * 1024 * 1024),
        name=name,
    )(*([plan] if plan is not None else []), *operands)


def passed_along(block, axis):
    size = lax.axis_size(axis)
    return lax.ppermute(block, axis, [(i, (i + 1) % size) for i in range(size)])


def parts_of_sum(term, axis):
    size = lax.axis_size(axis)
    if size & (size - 1):
        return [lax.psum(term, axis)]
    parts, bit = [term], 1
    while bit < size:
        term = functools.reduce(lambda x, y: x + y, parts)
        masks = [bit] if bit == 1 or 2 * bit >= size else [bit, 2 * bit, 3 * bit]
        parts = [term] + [lax.ppermute(term, axis, [(i, i ^ mask) for i in range(size)]) for mask in masks]
        bit *= 2 if len(masks) == 1 else 4
    return parts


def body(record, plan):
    rows, width = record.shape[0], record.shape[1] // 2
    rounds = plan.shape[0]
    total_rows = rows * lax.axis_size("tm")
    square, block, gram = (width, width), (rows, width), (width + 8, width)
    scratch = [pltpu.VMEM(square, F32)] * 2
    pair = record
    neighbour = [passed_along(record, "col")]
    neighbour_plan = passed_along(plan, "col")
    (terms,) = call(gram_kernel, [pair], [gram], name="gram")
    for step in range(rounds):
        last = step + 1 == rounds
        (ratio,) = call(ratio_kernel, parts_of_sum(terms, "tm"), [square], name="ratio")
        neighbour_ratio = passed_along(ratio, "col")
        (staying,) = call(own_kernel, [ratio, pair], [block], scratch, plan[step], name="own")
        operands = [neighbour_ratio, staying] + neighbour
        if last:
            pair, terms = call(
                functools.partial(neighbour_kernel, True, len(neighbour)), operands, [record.shape, (8, width)], scratch, neighbour_plan[step], name="last"
            )
        else:
            pair, terms, moving, neighbour_staying = call(
                functools.partial(neighbour_kernel, False, len(neighbour)), operands, [record.shape, gram, block, block], scratch, neighbour_plan[step], name="both"
            )
            neighbour = [neighbour_staying, passed_along(moving, "col")]
    energy = functools.reduce(lambda x, y: x + y, parts_of_sum(terms, "tm"))[:2].reshape(2 * width)
    return (pair, jnp.sqrt(energy / total_rows + epsilon))


def solution(mesh):
    in_specs = (P("tm", "col"), P(None, "col"))
    out_specs = (P("tm", "col"), P("col"))
    return jax.shard_map(body, mesh=mesh, in_specs=in_specs, out_specs=out_specs, check_vma=False)
```

profile of v0, /device:TPU:0, one launch (start us, length us, event | category | flops | bytes accessed | tf_op | source)
XLA Modules:
  0.0 85.3 jit_solution(3907240946440592102)
XLA Ops:
  0.6 3.1 %collective-permute-start.6 = (f32[1024,256]{1,0:T(8,128)}, f32[1024,256]{1,0:T(8,128)S(1)}, u32[]{:S(2)}, u32[]{:S(2)}) collective-permute-start(f32[1024,256]{1,0:T(8,128)} %pair_ref.3), channel_id=1, source_target_pairs={{0,8},{8,16},{16,24},{24,0},{1,9},{9,17},{17,25},{25,1},{2,10},{10... | collective-permute-start | bytes 3145736 | tf_op jit(solution)/shard_map/ppermute | solution.py:145
  3.7 1.3 %copy-done = f32[1024,256]{1,0:T(8,128)S(1)} copy-done((f32[1024,256]{1,0:T(8,128)S(1)}, f32[1024,256]{1,0:T(8,128)}, u32[]{:S(2)}) %copy-start) | copy-done | bytes 1048600
  5.0 0.4 gram.1
  5.5 0.1 copy-done.2
  5.6 1.6 %collective-permute-start = (s32[3,1]{0,1:T(1,128)S(1)}, s32[3,1]{0,1:T(1,128)S(1)}, u32[]{:S(2)}, u32[]{:S(2)}) collective-permute-start(s32[3,1]{0,1:T(1,128)S(1)} %copy-done.2), channel_id=1, source_target_pairs={{0,8},{8,16},{16,24},{24,0},{1,9},{9,17},{17,25},{25,1},{2,10},{10... | collective-permute-start | bytes 44 | tf_op jit(solution)/shard_map/ppermute | solution.py:145
  7.2 2.5 %collective-permute-start.4 = (f32[136,128]{1,0:T(8,128)S(1)}, f32[136,128]{1,0:T(8,128)S(1)}, u32[]{:S(2)}, u32[]{:S(2)}) collective-permute-start(f32[136,128]{1,0:T(8,128)S(1)} %add.28.refs_0_), channel_id=1, source_target_pairs={{0,6},{1,7},{2,4},{3,5},{4,2},{5,3},{6,0},{7,1},{8,14},{9,15},{10,... | collective-permute-start | bytes 208904 | tf_op jit(solution)/shard_map/ppermute | solution.py:156
  9.7 0.5 collective-permute-start.3
  10.2 0.5 collective-permute-start.2
  10.8 0.7 fusion
  11.4 1.1 %collective-permute-done.4.refs_3_ = f32[136,128]{1,0:T(8,128)S(1)} collective-permute-done((f32[136,128]{1,0:T(8,128)S(1)}, f32[136,128]{1,0:T(8,128)S(1)}, u32[]{:S(2)}, u32[]{:S(2)}) %collective-permute-start.4) | collective-permute-done | bytes 69664 | tf_op jit(solution)/shard_map/ppermute | solution.py:156
  12.5 1.5 %collective-permute-done.3.refs_2_ = f32[136,128]{1,0:T(8,128)S(1)} collective-permute-done((f32[136,128]{1,0:T(8,128)S(1)}, f32[136,128]{1,0:T(8,128)S(1)}, u32[]{:S(2)}, u32[]{:S(2)}) %collective-permute-start.3) | collective-permute-done | bytes 69664 | tf_op jit(solution)/shard_map/ppermute | solution.py:156
  14.1 0.5 collective-permute-done.2.refs_1_
  14.6 0.1 ratio.3.s_ref
  14.7 1.6 %collective-permute-start.5 = (f32[128,128]{1,0:T(8,128)S(1)}, f32[128,128]{1,0:T(8,128)S(1)}, u32[]{:S(2)}, u32[]{:S(2)}) collective-permute-start(f32[128,128]{1,0:T(8,128)S(1)} %ratio.3.s_ref), channel_id=1, source_target_pairs={{0,8},{8,16},{16,24},{24,0},{1,9},{9,17},{17,25},{25,1},{2,10},{10... | collective-permute-start | bytes 196616 | tf_op jit(solution)/shard_map/ppermute | solution.py:145
  16.3 13.6 %collective-permute-done = s32[3,1]{0,1:T(1,128)S(1)} collective-permute-done((s32[3,1]{0,1:T(1,128)S(1)}, s32[3,1]{0,1:T(1,128)S(1)}, u32[]{:S(2)}, u32[]{:S(2)}) %collective-permute-start) | collective-permute-done | bytes 44 | tf_op jit(solution)/shard_map/ppermute | solution.py:145
  29.9 0.6 fusion.1
  30.5 3.2 %own.3.staying_ref = f32[1024,128]{1,0:T(8,128)S(1)} custom-call(s32[1]{0:T(128)} %bitcast.3.plan_ref, f32[128,128]{1,0:T(8,128)S(1)} %ratio.3.s_ref, f32[1024,256]{1,0:T(8,128)S(1)} %copy-done.1), custom_call_target="tpu_custom_call" | custom-call | tf_op jit(solution)/shard_map/own/pallas_call | solution.py:132
  33.7 3.9 %both.2 = (f32[1024,256]{1,0:T(8,128)S(1)}, f32[136,128]{1,0:T(8,128)S(1)}, f32[1024,128]{1,0:T(8,128)S(1)}, f32[1024,128]{1,0:T(8,128)S(1)}) custom-call(s32[1]{0:T(128)} %bitcast.2.plan_ref, f32[128,128]{1,0:T(8,128)S(1)} %collective-permute-done.5.s_ref, f32[1024,128]{1,0:T(8,128)S(1)} %own.3.staying_ref, f32[1024,256]{1,0:T(8,128)S(1)} %collective-permute-done.6.refs_0_), custom_call_target="tpu_custom_call" | custom-call | tf_op jit(solution)/shard_map/both/pallas_call | solution.py:132
  37.7 1.2 %collective-permute-done.7 = f32[136,128]{1,0:T(8,128)S(1)} collective-permute-done((f32[136,128]{1,0:T(8,128)S(1)}, f32[136,128]{1,0:T(8,128)S(1)}, u32[]{:S(2)}, u32[]{:S(2)}) %collective-permute-start.7) | collective-permute-done | bytes 69664 | tf_op jit(solution)/shard_map/ppermute | solution.py:156
  39.0 2.5 %collective-permute-start.10 = (f32[136,128]{1,0:T(8,128)S(1)}, f32[136,128]{1,0:T(8,128)S(1)}, u32[]{:S(2)}, u32[]{:S(2)}) collective-permute-start(f32[136,128]{1,0:T(8,128)S(1)} %add.29.refs_0_), channel_id=1, source_target_pairs={{0,6},{1,7},{2,4},{3,5},{4,2},{5,3},{6,0},{7,1},{8,14},{9,15},{10,... | collective-permute-start | bytes 208904 | tf_op jit(solution)/shard_map/ppermute | solution.py:156
  41.5 0.5 collective-permute-start.9
  42.0 0.5 collective-permute-start.8
  42.5 1.7 %collective-permute-done.10.refs_3_ = f32[136,128]{1,0:T(8,128)S(1)} collective-permute-done((f32[136,128]{1,0:T(8,128)S(1)}, f32[136,128]{1,0:T(8,128)S(1)}, u32[]{:S(2)}, u32[]{:S(2)}) %collective-permute-start.10) | collective-permute-done | bytes 69664 | tf_op jit(solution)/shard_map/ppermute | solution.py:156
  44.3 1.5 %collective-permute-done.9.refs_2_ = f32[136,128]{1,0:T(8,128)S(1)} collective-permute-done((f32[136,128]{1,0:T(8,128)S(1)}, f32[136,128]{1,0:T(8,128)S(1)}, u32[]{:S(2)}, u32[]{:S(2)}) %collective-permute-start.9) | collective-permute-done | bytes 69664 | tf_op jit(solution)/shard_map/ppermute | solution.py:156
  45.8 0.5 collective-permute-done.8.refs_1_
  46.4 1.3 %collective-permute-start.11 = (f32[128,128]{1,0:T(8,128)S(1)}, f32[128,128]{1,0:T(8,128)S(1)}, u32[]{:S(2)}, u32[]{:S(2)}) collective-permute-start(f32[128,128]{1,0:T(8,128)S(1)} %ratio.4.s_ref), channel_id=1, source_target_pairs={{0,8},{8,16},{16,24},{24,0},{1,9},{9,17},{17,25},{25,1},{2,10},{10... | collective-permute-start | bytes 196616 | tf_op jit(solution)/shard_map/ppermute | solution.py:145
  47.7 3.2 %own.4.staying_ref = f32[1024,128]{1,0:T(8,128)S(1)} custom-call(s32[1]{0:T(128)} %bitcast.4.plan_ref, f32[128,128]{1,0:T(8,128)S(1)} %ratio.4.s_ref, f32[1024,256]{1,0:T(8,128)S(1)} %get-tuple-element.13.pair_ref), custom_call_target="tpu_custom_call" | custom-call | tf_op jit(solution)/shard_map/own/pallas_call | solution.py:132
  50.9 2.2 %collective-permute-done.11.s_ref = f32[128,128]{1,0:T(8,128)S(1)} collective-permute-done((f32[128,128]{1,0:T(8,128)S(1)}, f32[128,128]{1,0:T(8,128)S(1)}, u32[]{:S(2)}, u32[]{:S(2)}) %collective-permute-start.11) | collective-permute-done | bytes 65568 | tf_op jit(solution)/shard_map/ppermute | solution.py:145
  53.2 3.9 %both.3 = (f32[1024,256]{1,0:T(8,128)S(1)}, f32[136,128]{1,0:T(8,128)S(1)}, f32[1024,128]{1,0:T(8,128)S(1)}, f32[1024,128]{1,0:T(8,128)S(1)}) custom-call(s32[1]{0:T(128)} %bitcast.1.plan_ref, f32[128,128]{1,0:T(8,128)S(1)} %collective-permute-done.11.s_ref, f32[1024,128]{1,0:T(8,128)S(1)} %own.4.staying_ref, f32[1024,128]{1,0:T(8,128)S(1)} %get-tuple-element.14.refs_0_, ...), custom_call_target="tpu_custom_call" | custom-call | tf_op jit(solution)/shard_map/both/pallas_call | solution.py:132
  57.2 1.2 %collective-permute-done.13 = f32[136,128]{1,0:T(8,128)S(1)} collective-permute-done((f32[136,128]{1,0:T(8,128)S(1)}, f32[136,128]{1,0:T(8,128)S(1)}, u32[]{:S(2)}, u32[]{:S(2)}) %collective-permute-start.13) | collective-permute-done | bytes 69664 | tf_op jit(solution)/shard_map/ppermute | solution.py:156
  58.4 2.3 %collective-permute-start.16 = (f32[136,128]{1,0:T(8,128)S(1)}, f32[136,128]{1,0:T(8,128)S(1)}, u32[]{:S(2)}, u32[]{:S(2)}) collective-permute-start(f32[136,128]{1,0:T(8,128)S(1)} %add.30.refs_0_), channel_id=1, source_target_pairs={{0,6},{1,7},{2,4},{3,5},{4,2},{5,3},{6,0},{7,1},{8,14},{9,15},{10,... | collective-permute-start | bytes 208904 | tf_op jit(solution)/shard_map/ppermute | solution.py:156
  60.7 0.5 collective-permute-start.15
  61.2 0.8 collective-permute-start.14
  62.0 1.8 %collective-permute-done.16.refs_3_ = f32[136,128]{1,0:T(8,128)S(1)} collective-permute-done((f32[136,128]{1,0:T(8,128)S(1)}, f32[136,128]{1,0:T(8,128)S(1)}, u32[]{:S(2)}, u32[]{:S(2)}) %collective-permute-start.16) | collective-permute-done | bytes 69664 | tf_op jit(solution)/shard_map/ppermute | solution.py:156
  63.8 1.4 %collective-permute-done.15.refs_2_ = f32[136,128]{1,0:T(8,128)S(1)} collective-permute-done((f32[136,128]{1,0:T(8,128)S(1)}, f32[136,128]{1,0:T(8,128)S(1)}, u32[]{:S(2)}, u32[]{:S(2)}) %collective-permute-start.15) | collective-permute-done | bytes 69664 | tf_op jit(solution)/shard_map/ppermute | solution.py:156
  65.2 0.3 collective-permute-done.14.refs_1_
  65.5 0.1 ratio.5.s_ref
  65.6 1.2 %collective-permute-start.17 = (f32[128,128]{1,0:T(8,128)S(1)}, f32[128,128]{1,0:T(8,128)S(1)}, u32[]{:S(2)}, u32[]{:S(2)}) collective-permute-start(f32[128,128]{1,0:T(8,128)S(1)} %ratio.5.s_ref), channel_id=1, source_target_pairs={{0,8},{8,16},{16,24},{24,0},{1,9},{9,17},{17,25},{25,1},{2,10},{10... | collective-permute-start | bytes 196616 | tf_op jit(solution)/shard_map/ppermute | solution.py:145
  66.8 3.1 %own.5.staying_ref = f32[1024,128]{1,0:T(8,128)S(1)} custom-call(s32[1]{0:T(128)} %bitcast.5.plan_ref, f32[128,128]{1,0:T(8,128)S(1)} %ratio.5.s_ref, f32[1024,256]{1,0:T(8,128)S(1)} %get-tuple-element.17.pair_ref), custom_call_target="tpu_custom_call" | custom-call | tf_op jit(solution)/shard_map/own/pallas_call | solution.py:132
  69.9 2.6 %collective-permute-done.17.s_ref = f32[128,128]{1,0:T(8,128)S(1)} collective-permute-done((f32[128,128]{1,0:T(8,128)S(1)}, f32[128,128]{1,0:T(8,128)S(1)}, u32[]{:S(2)}, u32[]{:S(2)}) %collective-permute-start.17) | collective-permute-done | bytes 65568 | tf_op jit(solution)/shard_map/ppermute | solution.py:145
  72.5 4.0 %last.1 = (f32[1024,256]{1,0:T(8,128)}, f32[8,128]{1,0:T(8,128)S(1)}) custom-call(s32[1]{0:T(128)} %bitcast.plan_ref, f32[128,128]{1,0:T(8,128)S(1)} %collective-permute-done.17.s_ref, f32[1024,128]{1,0:T(8,128)S(1)} %own.5.staying_ref, f32[1024,128]{1,0:T(8,128)S(1)} %get-tuple-element.18.refs_0_, f32[1024,128]{1,0:T(8,128)S(1)} %collective-permute-done.18.refs_1_), custom_call_target="tpu_custom_call" | custom-call | tf_op jit(solution)/shard_map/last/pallas_call | solution.py:132
  76.5 1.2 %collective-permute-done.19 = f32[8,128]{1,0:T(8,128)S(1)} collective-permute-done((f32[8,128]{1,0:T(8,128)S(1)}, f32[8,128]{1,0:T(8,128)S(1)}, u32[]{:S(2)}, u32[]{:S(2)}) %collective-permute-start.19) | collective-permute-done | bytes 4128 | tf_op jit(solution)/shard_map/ppermute | solution.py:156
  77.7 1.4 %collective-permute-start.22 = (f32[8,128]{1,0:T(8,128)S(1)}, f32[8,128]{1,0:T(8,128)S(1)}, u32[]{:S(2)}, u32[]{:S(2)}) collective-permute-start(f32[8,128]{1,0:T(8,128)S(1)} %add.31), channel_id=1, source_target_pairs={{0,6},{1,7},{2,4},{3,5},{4,2},{5,3},{6,0},{7,1},{8,14},{9,15},{10,... | collective-permute-start | bytes 12296 | tf_op jit(solution)/shard_map/ppermute | solution.py:156
  79.1 2.0 %collective-permute-start.21 = (f32[8,128]{1,0:T(8,128)S(1)}, f32[8,128]{1,0:T(8,128)S(1)}, u32[]{:S(2)}, u32[]{:S(2)}) collective-permute-start(f32[8,128]{1,0:T(8,128)S(1)} %add.31), channel_id=1, source_target_pairs={{0,4},{1,5},{2,6},{3,7},{4,0},{5,1},{6,2},{7,3},{8,12},{9,13},{10,... | collective-permute-start | bytes 12296 | tf_op jit(solution)/shard_map/ppermute | solution.py:156
  81.1 1.0 %collective-permute-done.22 = f32[8,128]{1,0:T(8,128)S(1)} collective-permute-done((f32[8,128]{1,0:T(8,128)S(1)}, f32[8,128]{1,0:T(8,128)S(1)}, u32[]{:S(2)}, u32[]{:S(2)}) %collective-permute-start.22) | collective-permute-done | bytes 4128 | tf_op jit(solution)/shard_map/ppermute | solution.py:156
  82.2 0.5 collective-permute-done.21
  82.7 2.0 %collective-permute-done.20 = f32[8,128]{1,0:T(8,128)S(1)} collective-permute-done((f32[8,128]{1,0:T(8,128)S(1)}, f32[8,128]{1,0:T(8,128)S(1)}, u32[]{:S(2)}, u32[]{:S(2)}) %collective-permute-start.20) | collective-permute-done | bytes 4128 | tf_op jit(solution)/shard_map/ppermute | solution.py:156
  84.7 0.6 sqrt_bitcast_fusion
  (22 shorter events, 0.5 us)
Async XLA Ops:
  0.6 33.1 %collective-permute-start.6 = (f32[1024,256]{1,0:T(8,128)}, f32[1024,256]{1,0:T(8,128)S(1)}, u32[]{:S(2)}, u32[]{:S(2)}) collective-permute-start(f32[1024,256]{1,0:T(8,128)} %pair_ref.3), channel_id=1, source_target_pairs={{0,8},{8,16},{16,24},{24,0},{1,9},{9,17},{17,25},{25,1},{2,10},{10... | collective-permute-start | bytes 3145736 | tf_op jit(solution)/shard_map/ppermute | solution.py:145
  3.7 1.3 %copy-start = (f32[1024,256]{1,0:T(8,128)S(1)}, f32[1024,256]{1,0:T(8,128)}, u32[]{:S(2)}) copy-start(f32[1024,256]{1,0:T(8,128)} %pair_ref.3) | copy-start | bytes 3145732
  5.0 0.7 copy-start.2
  5.0 25.5 %copy-start.1 = (f32[1024,256]{1,0:T(8,128)S(1)}, f32[1024,256]{1,0:T(8,128)}, u32[]{:S(2)}) copy-start(f32[1024,256]{1,0:T(8,128)} %pair_ref.3) | copy-start | bytes 3145732
  5.4 1.8 %collective-permute-start.1 = (f32[136,128]{1,0:T(8,128)S(1)}, f32[136,128]{1,0:T(8,128)S(1)}, u32[]{:S(2)}, u32[]{:S(2)}) collective-permute-start(f32[136,128]{1,0:T(8,128)S(1)} %gram.1), channel_id=1, source_target_pairs={{0,1},{1,0},{2,3},{3,2},{4,5},{5,4},{6,7},{7,6},{8,9},{9,8},{10,11... | collective-permute-start | bytes 208904 | tf_op jit(solution)/shard_map/ppermute | solution.py:156
  5.6 24.2 %collective-permute-start = (s32[3,1]{0,1:T(1,128)S(1)}, s32[3,1]{0,1:T(1,128)S(1)}, u32[]{:S(2)}, u32[]{:S(2)}) collective-permute-start(s32[3,1]{0,1:T(1,128)S(1)} %copy-done.2), channel_id=1, source_target_pairs={{0,8},{8,16},{16,24},{24,0},{1,9},{9,17},{17,25},{25,1},{2,10},{10... | collective-permute-start | bytes 44 | tf_op jit(solution)/shard_map/ppermute | solution.py:145
  7.2 5.3 %collective-permute-start.4 = (f32[136,128]{1,0:T(8,128)S(1)}, f32[136,128]{1,0:T(8,128)S(1)}, u32[]{:S(2)}, u32[]{:S(2)}) collective-permute-start(f32[136,128]{1,0:T(8,128)S(1)} %add.28.refs_0_), channel_id=1, source_target_pairs={{0,6},{1,7},{2,4},{3,5},{4,2},{5,3},{6,0},{7,1},{8,14},{9,15},{10,... | collective-permute-start | bytes 208904 | tf_op jit(solution)/shard_map/ppermute | solution.py:156
  9.7 4.3 %collective-permute-start.3 = (f32[136,128]{1,0:T(8,128)S(1)}, f32[136,128]{1,0:T(8,128)S(1)}, u32[]{:S(2)}, u32[]{:S(2)}) collective-permute-start(f32[136,128]{1,0:T(8,128)S(1)} %add.28.refs_0_), channel_id=1, source_target_pairs={{0,4},{1,5},{2,6},{3,7},{4,0},{5,1},{6,2},{7,3},{8,12},{9,13},{10,... | collective-permute-start | bytes 208904 | tf_op jit(solution)/shard_map/ppermute | solution.py:156
  10.2 4.3 %collective-permute-start.2 = (f32[136,128]{1,0:T(8,128)S(1)}, f32[136,128]{1,0:T(8,128)S(1)}, u32[]{:S(2)}, u32[]{:S(2)}) collective-permute-start(f32[136,128]{1,0:T(8,128)S(1)} %add.28.refs_0_), channel_id=1, source_target_pairs={{0,2},{1,3},{2,0},{3,1},{4,6},{5,7},{6,4},{7,5},{8,10},{9,11},{10,... | collective-permute-start | bytes 208904 | tf_op jit(solution)/shard_map/ppermute | solution.py:156
  14.7 19.0 %collective-permute-start.5 = (f32[128,128]{1,0:T(8,128)S(1)}, f32[128,128]{1,0:T(8,128)S(1)}, u32[]{:S(2)}, u32[]{:S(2)}) collective-permute-start(f32[128,128]{1,0:T(8,128)S(1)} %ratio.3.s_ref), channel_id=1, source_target_pairs={{0,8},{8,16},{16,24},{24,0},{1,9},{9,17},{17,25},{25,1},{2,10},{10... | collective-permute-start | bytes 196616 | tf_op jit(solution)/shard_map/ppermute | solution.py:145
  37.6 15.6 %collective-permute-start.12 = (f32[1024,128]{1,0:T(8,128)S(1)}, f32[1024,128]{1,0:T(8,128)S(1)}, u32[]{:S(2)}, u32[]{:S(2)}) collective-permute-start(f32[1024,128]{1,0:T(8,128)S(1)} %get-tuple-element.15), channel_id=1, source_target_pairs={{0,8},{8,16},{16,24},{24,0},{1,9},{9,17},{17,25},{25,1},{2,10},{10... | collective-permute-start | bytes 1572872 | tf_op jit(solution)/shard_map/ppermute | solution.py:145
  37.6 1.3 %collective-permute-start.7 = (f32[136,128]{1,0:T(8,128)S(1)}, f32[136,128]{1,0:T(8,128)S(1)}, u32[]{:S(2)}, u32[]{:S(2)}) collective-permute-start(f32[136,128]{1,0:T(8,128)S(1)} %get-tuple-element.12), channel_id=1, source_target_pairs={{0,1},{1,0},{2,3},{3,2},{4,5},{5,4},{6,7},{7,6},{8,9},{9,8},{10,11... | collective-permute-start | bytes 208904 | tf_op jit(solution)/shard_map/ppermute | solution.py:156
  39.0 5.3 %collective-permute-start.10 = (f32[136,128]{1,0:T(8,128)S(1)}, f32[136,128]{1,0:T(8,128)S(1)}, u32[]{:S(2)}, u32[]{:S(2)}) collective-permute-start(f32[136,128]{1,0:T(8,128)S(1)} %add.29.refs_0_), channel_id=1, source_target_pairs={{0,6},{1,7},{2,4},{3,5},{4,2},{5,3},{6,0},{7,1},{8,14},{9,15},{10,... | collective-permute-start | bytes 208904 | tf_op jit(solution)/shard_map/ppermute | solution.py:156
  41.5 4.3 %collective-permute-start.9 = (f32[136,128]{1,0:T(8,128)S(1)}, f32[136,128]{1,0:T(8,128)S(1)}, u32[]{:S(2)}, u32[]{:S(2)}) collective-permute-start(f32[136,128]{1,0:T(8,128)S(1)} %add.29.refs_0_), channel_id=1, source_target_pairs={{0,4},{1,5},{2,6},{3,7},{4,0},{5,1},{6,2},{7,3},{8,12},{9,13},{10,... | collective-permute-start | bytes 208904 | tf_op jit(solution)/shard_map/ppermute | solution.py:156
  42.0 4.3 %collective-permute-start.8 = (f32[136,128]{1,0:T(8,128)S(1)}, f32[136,128]{1,0:T(8,128)S(1)}, u32[]{:S(2)}, u32[]{:S(2)}) collective-permute-start(f32[136,128]{1,0:T(8,128)S(1)} %add.29.refs_0_), channel_id=1, source_target_pairs={{0,2},{1,3},{2,0},{3,1},{4,6},{5,7},{6,4},{7,5},{8,10},{9,11},{10,... | collective-permute-start | bytes 208904 | tf_op jit(solution)/shard_map/ppermute | solution.py:156
  46.4 6.7 %collective-permute-start.11 = (f32[128,128]{1,0:T(8,128)S(1)}, f32[128,128]{1,0:T(8,128)S(1)}, u32[]{:S(2)}, u32[]{:S(2)}) collective-permute-start(f32[128,128]{1,0:T(8,128)S(1)} %ratio.4.s_ref), channel_id=1, source_target_pairs={{0,8},{8,16},{16,24},{24,0},{1,9},{9,17},{17,25},{25,1},{2,10},{10... | collective-permute-start | bytes 196616 | tf_op jit(solution)/shard_map/ppermute | solution.py:145
  57.0 15.4 %collective-permute-start.18 = (f32[1024,128]{1,0:T(8,128)S(1)}, f32[1024,128]{1,0:T(8,128)S(1)}, u32[]{:S(2)}, u32[]{:S(2)}) collective-permute-start(f32[1024,128]{1,0:T(8,128)S(1)} %get-tuple-element.19), channel_id=1, source_target_pairs={{0,8},{8,16},{16,24},{24,0},{1,9},{9,17},{17,25},{25,1},{2,10},{10... | collective-permute-start | bytes 1572872 | tf_op jit(solution)/shard_map/ppermute | solution.py:145
  57.1 1.3 %collective-permute-start.13 = (f32[136,128]{1,0:T(8,128)S(1)}, f32[136,128]{1,0:T(8,128)S(1)}, u32[]{:S(2)}, u32[]{:S(2)}) collective-permute-start(f32[136,128]{1,0:T(8,128)S(1)} %get-tuple-element.16), channel_id=1, source_target_pairs={{0,1},{1,0},{2,3},{3,2},{4,5},{5,4},{6,7},{7,6},{8,9},{9,8},{10,11... | collective-permute-start | bytes 208904 | tf_op jit(solution)/shard_map/ppermute | solution.py:156
  58.4 5.3 %collective-permute-start.16 = (f32[136,128]{1,0:T(8,128)S(1)}, f32[136,128]{1,0:T(8,128)S(1)}, u32[]{:S(2)}, u32[]{:S(2)}) collective-permute-start(f32[136,128]{1,0:T(8,128)S(1)} %add.30.refs_0_), channel_id=1, source_target_pairs={{0,6},{1,7},{2,4},{3,5},{4,2},{5,3},{6,0},{7,1},{8,14},{9,15},{10,... | collective-permute-start | bytes 208904 | tf_op jit(solution)/shard_map/ppermute | solution.py:156
  60.7 4.5 %collective-permute-start.15 = (f32[136,128]{1,0:T(8,128)S(1)}, f32[136,128]{1,0:T(8,128)S(1)}, u32[]{:S(2)}, u32[]{:S(2)}) collective-permute-start(f32[136,128]{1,0:T(8,128)S(1)} %add.30.refs_0_), channel_id=1, source_target_pairs={{0,4},{1,5},{2,6},{3,7},{4,0},{5,1},{6,2},{7,3},{8,12},{9,13},{10,... | collective-permute-start | bytes 208904 | tf_op jit(solution)/shard_map/ppermute | solution.py:156
  61.2 4.3 %collective-permute-start.14 = (f32[136,128]{1,0:T(8,128)S(1)}, f32[136,128]{1,0:T(8,128)S(1)}, u32[]{:S(2)}, u32[]{:S(2)}) collective-permute-start(f32[136,128]{1,0:T(8,128)S(1)} %add.30.refs_0_), channel_id=1, source_target_pairs={{0,2},{1,3},{2,0},{3,1},{4,6},{5,7},{6,4},{7,5},{8,10},{9,11},{10,... | collective-permute-start | bytes 208904 | tf_op jit(solution)/shard_map/ppermute | solution.py:156
  65.6 6.8 %collective-permute-start.17 = (f32[128,128]{1,0:T(8,128)S(1)}, f32[128,128]{1,0:T(8,128)S(1)}, u32[]{:S(2)}, u32[]{:S(2)}) collective-permute-start(f32[128,128]{1,0:T(8,128)S(1)} %ratio.5.s_ref), channel_id=1, source_target_pairs={{0,8},{8,16},{16,24},{24,0},{1,9},{9,17},{17,25},{25,1},{2,10},{10... | collective-permute-start | bytes 196616 | tf_op jit(solution)/shard_map/ppermute | solution.py:145
  76.5 1.2 %collective-permute-start.19 = (f32[8,128]{1,0:T(8,128)S(1)}, f32[8,128]{1,0:T(8,128)S(1)}, u32[]{:S(2)}, u32[]{:S(2)}) collective-permute-start(f32[8,128]{1,0:T(8,128)S(1)} %get-tuple-element.21), channel_id=1, source_target_pairs={{0,1},{1,0},{2,3},{3,2},{4,5},{5,4},{6,7},{7,6},{8,9},{9,8},{10,11... | collective-permute-start | bytes 12296 | tf_op jit(solution)/shard_map/ppermute | solution.py:156
  77.7 4.5 %collective-permute-start.22 = (f32[8,128]{1,0:T(8,128)S(1)}, f32[8,128]{1,0:T(8,128)S(1)}, u32[]{:S(2)}, u32[]{:S(2)}) collective-permute-start(f32[8,128]{1,0:T(8,128)S(1)} %add.31), channel_id=1, source_target_pairs={{0,6},{1,7},{2,4},{3,5},{4,2},{5,3},{6,0},{7,1},{8,14},{9,15},{10,... | collective-permute-start | bytes 12296 | tf_op jit(solution)/shard_map/ppermute | solution.py:156
  79.1 3.6 %collective-permute-start.21 = (f32[8,128]{1,0:T(8,128)S(1)}, f32[8,128]{1,0:T(8,128)S(1)}, u32[]{:S(2)}, u32[]{:S(2)}) collective-permute-start(f32[8,128]{1,0:T(8,128)S(1)} %add.31), channel_id=1, source_target_pairs={{0,4},{1,5},{2,6},{3,7},{4,0},{5,1},{6,2},{7,3},{8,12},{9,13},{10,... | collective-permute-start | bytes 12296 | tf_op jit(solution)/shard_map/ppermute | solution.py:156
  81.1 3.6 %collective-permute-start.20 = (f32[8,128]{1,0:T(8,128)S(1)}, f32[8,128]{1,0:T(8,128)S(1)}, u32[]{:S(2)}, u32[]{:S(2)}) collective-permute-start(f32[8,128]{1,0:T(8,128)S(1)} %add.31), channel_id=1, source_target_pairs={{0,2},{1,3},{2,0},{3,1},{4,6},{5,7},{6,4},{7,5},{8,10},{9,11},{10,... | collective-permute-start | bytes 12296 | tf_op jit(solution)/shard_map/ppermute | solution.py:156
where the time goes:
time: 85.5 us; the launch traced here: 85.3 us
  waiting for transfers between devices  36 us (42%)
  starting transfers between devices  23.2 us (27%)
  Pallas kernels  22 us (26%)
  local copies, waits for them, and re-layouts  2.68 us (3%)
    pallas_call x10, Pallas kernels, call(): pl.pallas_call(kernel, out_shape=[jax.ShapeDtypeStruct(shape, F32) for sh...  22 us
    ppermute x7, waiting for transfers between devices, passed_along(): return lax.ppermute(block, axis, [(i, (i + 1) % size) for i in range(size)])  18.3 us
    ppermute x16, waiting for transfers between devices, parts_of_sum(): lax.ppermute(term, axis, [(i, i ^ mask) for i in range(size)])  17.6 us
    ppermute x16, starting transfers between devices, parts_of_sum(): lax.ppermute(term, axis, [(i, i ^ mask) for i in range(size)])  14.4 us
    ppermute x7, starting transfers between devices, passed_along(): return lax.ppermute(block, axis, [(i, (i + 1) % size) for i in range(size)])  8.85 us
  transfers between devices with their start and end apart: 23, of which 18 were waited for; matrix products, arithmetic and copies ran while one was open for 2% of the time, Pallas kernels for 12%

commit v1 on v0

v1 whole, which is shorter than its diff:
```python
import functools
import jax
import jax.numpy as jnp
from jax import lax
from jax.experimental import pallas as pl
from jax.experimental.pallas import tpu as pltpu
from jax.sharding import PartitionSpec as P

epsilon = 1e-06
MICROS = {"own": 1.0, "inverse": 2.0, "turn": 1.0, "join": 0.5}
F32 = jnp.float32
BF16 = jnp.bfloat16
NN = (((1,), (0,)), ((), ()))
NT = (((1,), (1,)), ((), ()))
TN = (((0,), (0,)), ((), ()))
VMEM = pl.BlockSpec(memory_space=pltpu.VMEM)


def split(x):
    high = x.astype(BF16)
    return high, (x - high.astype(F32)).astype(BF16)


def dot3(a, b, dims=NN):
    one = functools.partial(lax.dot_general, dimension_numbers=dims, preferred_element_type=F32)
    return one(a[0], b[0]) + (one(a[0], b[1]) + one(a[1], b[0]))


def identity_of(width):
    shape = (width, width)
    return (lax.broadcasted_iota(jnp.int32, shape, 0) == lax.broadcasted_iota(jnp.int32, shape, 1)).astype(F32)


def gram_of(first, second):
    width = first.shape[1]
    cross = dot3(split(first), split(second), TN)
    tail = [
        jnp.sum(first * first, axis=0, keepdims=True),
        jnp.sum(second * second, axis=0, keepdims=True),
        jnp.zeros((6, width), F32),
    ]
    return jnp.concatenate([cross] + tail, axis=0)


def inverse(skew, error_ref, total_ref):
    width = skew[0].shape[0]
    square = dot3(skew, skew, NT)
    bound = jnp.minimum(jnp.max(jnp.sum(jnp.abs(square), axis=0)), jnp.sqrt(jnp.sum(square * square)))
    identity = identity_of(width)
    scale = 2.0 / (bound + 2.0)
    error_ref[...] = (1.0 - scale) * identity - scale * square
    total_ref[...] = scale * identity

    def step(error_bound):
        grow = 2.0 / (2.0 - error_bound * error_bound)
        error, total = error_ref[...], total_ref[...]
        both = dot3(split(jnp.concatenate([error, total], axis=0)), split(error))
        total_ref[...] = grow * (total + both[width:])
        error_ref[...] = (1.0 - grow) * identity + grow * both[:width]
        return error_bound * error_bound / (2.0 - error_bound * error_bound)

    lax.while_loop(lambda error_bound: error_bound > 1e-3, step, bound / (bound + 2.0))
    total = total_ref[...]
    parts = split(total)
    residual = identity - total - dot3(split(square), parts)
    return total + dot3(parts, split(residual))


def rotated_halves(skew, inner, first, second):
    mixed = dot3(split(first + dot3(split(second), skew, NT)), split(inner))
    return 2.0 * mixed - first, second - 2.0 * dot3(split(mixed), skew)


def gram_kernel(pair_ref, gram_ref, head_ref):
    width = pair_ref.shape[1] // 2
    gram_ref[...] = gram_of(pair_ref[:, :width], pair_ref[:, width:])
    head_ref[...] = pair_ref[: head_ref.shape[0]]


def ratio_kernel(row, plan_ref, *refs):
    parts, s_ref = refs[:-1], refs[-1]
    gram = functools.reduce(lambda x, y: x + y, [ref[...] for ref in parts])
    width = gram.shape[1]
    cross, second_diag = gram[:width], gram[width + 1 : width + 2]
    first_diag = jnp.sum(identity_of(width) * gram[width : width + 1], axis=1, keepdims=True)
    difference = first_diag - second_diag
    s_ref[:width] = (
        cross * difference / (2.0 * (difference * difference + 4.0 * cross * cross + 0.01 * first_diag * second_diag))
    )
    s_ref[width:] = plan_ref[row : row + 8]


def own_kernel(known, kept, s_ref, pair_ref, staying_ref, *refs):
    *outs, error_ref, total_ref = refs
    width = s_ref.shape[1]
    skew = split(s_ref[:width])
    inner = inverse(skew, error_ref, total_ref)
    first, second = rotated_halves(skew, inner, pair_ref[:, :width], pair_ref[:, width:])
    moves_second = s_ref[width : width + 1] > 0.5
    staying = jnp.where(moves_second, first, second)
    staying_ref[...] = staying
    if known < pair_ref.shape[0]:
        outs[0][...] = jnp.where(moves_second, second[known:], first[known:])
    if known < kept:
        outs[-1][...] = staying[known:kept]


def inverse_kernel(s_ref, inner_ref, error_ref, total_ref):
    inner_ref[...] = inverse(split(s_ref[: s_ref.shape[1]]), error_ref, total_ref)


def turned(s_ref, inner_ref, refs):
    width = s_ref.shape[1]
    if len(refs) == 1:
        first, second = refs[0][:, :width], refs[0][:, width:]
    else:
        second = refs[1][...]
        first = jnp.concatenate([refs[0][...]] + [ref[...] for ref in refs[2:]], axis=0)
    first, second = rotated_halves(split(s_ref[:width]), inner_ref[...], first, second)
    moves_second = s_ref[width : width + 1] > 0.5
    return jnp.where(moves_second, second, first), jnp.where(moves_second, first, second)


def joined(staying, moving, pair_ref, gram_ref, kept):
    width = staying.shape[1]
    pair_ref[:, :width] = staying
    pair_ref[:, width:] = moving
    if kept:
        gram_ref[...] = gram_of(staying, moving)
    else:
        gram_ref[...] = jnp.concatenate(
            [
                jnp.sum(staying * staying, axis=0, keepdims=True),
                jnp.sum(moving * moving, axis=0, keepdims=True),
                jnp.zeros((6, width), F32),
            ],
            axis=0,
        )


def turn_kernel(parts, s_ref, inner_ref, *refs):
    moving, staying = turned(s_ref, inner_ref, refs[:parts])
    refs[parts][...] = moving
    if len(refs) > parts + 1:
        refs[parts + 1][...] = staying[: refs[parts + 1].shape[0]]


def join_kernel(kept, staying_ref, moving_ref, tail_ref, pair_ref, gram_ref, *outs):
    moving = jnp.concatenate([moving_ref[...], tail_ref[...]], axis=0)
    joined(staying_ref[...], moving, pair_ref, gram_ref, kept)
    if kept:
        outs[0][...] = moving[:kept]


def turn_join_kernel(kept, parts, s_ref, inner_ref, staying_ref, *refs):
    moving, neighbour_staying = turned(s_ref, inner_ref, refs[:parts])
    pair_ref, gram_ref, *outs = refs[parts:]
    joined(staying_ref[...], moving, pair_ref, gram_ref, kept)
    if kept:
        outs[0][...] = moving[:kept]
        outs[1][...] = neighbour_staying[: outs[1].shape[0]]


def call(kernel, operands, outs, scratch=(), name=""):
    micros = MICROS.get(name, 0.0)
    return pl.pallas_call(
        kernel,
        out_shape=[jax.ShapeDtypeStruct(shape, F32) for shape in outs],
        in_specs=[VMEM] * len(operands),
        out_specs=[VMEM] * len(outs),
        scratch_shapes=list(scratch),
        compiler_params=pltpu.CompilerParams(vmem_limit_bytes=48 * 1024 * 1024),
        cost_estimate=pl.CostEstimate(flops=int(micros * 1e9) + 1, bytes_accessed=int(micros * 3.5e6) + 1, transcendentals=0),
        name=name,
    )(*operands)


def passed_along(block, axis):
    size = lax.axis_size(axis)
    return lax.ppermute(block, axis, [(i, (i + 1) % size) for i in range(size)])


def parts_of_sum(term, axis):
    size = lax.axis_size(axis)
    if size & (size - 1):
        return [lax.psum(term, axis)]
    parts, bit = [term], 1
    while bit < size:
        term = functools.reduce(lambda x, y: x + y, parts)
        masks = [bit] if bit == 1 or 2 * bit >= size else [bit, 2 * bit, 3 * bit]
        parts = [term] + [lax.ppermute(term, axis, [(i, i ^ mask) for i in range(size)]) for mask in masks]
        bit *= 2 if len(masks) == 1 else 4
    return parts


def known_rows(rows, rounds):
    eighths = [5] + [6] * rounds
    return [rows * part // 128 * 16 for part in eighths[:rounds]] + [0]


def body(record, plan):
    rows, width = record.shape[0], record.shape[1] // 2
    rounds = plan.shape[0]
    total_rows = rows * lax.axis_size("tm")
    square, gram = (width, width), (width + 8, width)
    scratch = [pltpu.VMEM(square, F32)] * 2
    heads = known_rows(rows, rounds)
    pair = record
    terms, raw_head = call(gram_kernel, [pair], [gram, (heads[0], 2 * width)], name="gram")
    neighbour = [passed_along(raw_head, "col")]
    plan_rows = jnp.repeat(jnp.broadcast_to(plan.astype(F32), (rounds, width)), 8, axis=0)
    for step in range(rounds):
        known, kept = heads[step], heads[step + 1]
        parts = parts_of_sum(terms, "tm")
        (ratio,) = call(functools.partial(ratio_kernel, 8 * step), [plan_rows] + parts, [gram], name="ratio")
        neighbour_ratio = passed_along(ratio, "col")
        outs = [(rows, width)] + [(rows - known, width)] * (known < rows) + [(kept - known, width)] * (known < kept)
        staying, *sent = call(functools.partial(own_kernel, known, kept), [ratio, pair], outs, scratch, name="own")
        (inner,) = call(inverse_kernel, [neighbour_ratio], [square], scratch, name="inverse")
        turn = [neighbour_ratio, inner]
        sums = gram if kept else (8, width)
        kept_outs = [(kept, width)] * (kept > 0)
        known_outs = [(min(known, kept), width)] * (kept > 0)
        if known < rows:
            tail = passed_along(sent[0], "col")
            kernel = functools.partial(turn_kernel, len(neighbour))
            moving, *kept_staying = call(kernel, turn + neighbour, [(known, width)] + known_outs, name="turn")
            kernel = functools.partial(join_kernel, kept)
            pair, terms, *moving = call(kernel, [staying, moving, tail], [record.shape, sums] + kept_outs, name="join")
        else:
            tail = None
            kernel = functools.partial(turn_join_kernel, kept, len(neighbour))
            outs = [record.shape, sums] + kept_outs + known_outs
            pair, terms, *rest = call(kernel, turn + [staying] + neighbour, outs, name="both")
            moving, kept_staying = rest[:1], rest[1:]
        if kept:
            neighbour = kept_staying + [passed_along(moving[0], "col")]
        if known < kept:
            more = sent[-1]
            if tail is not None:
                more, _ = lax.optimization_barrier((more, tail))
            neighbour.append(passed_along(more, "col"))
    energy = functools.reduce(lambda x, y: x + y, parts_of_sum(terms, "tm"))[:2].reshape(2 * width)
    return (pair, jnp.sqrt(energy / total_rows + epsilon))


def solution(mesh):
    in_specs = (P("tm", "col"), P(None, "col"))
    out_specs = (P("tm", "col"), P("col"))
    return jax.shard_map(body, mesh=mesh, in_specs=in_specs, out_specs=out_specs, check_vma=False)
```

time: 85.5 us -> 75.7 us (0.89)
  waiting for transfers between devices: 36 us -> 31.7 us
  Pallas kernels: 22 us -> 17.9 us
  local copies, waits for them, and re-layouts: 2.68 us -> 1.45 us
    ppermute x7 -> x10, waiting for transfers between devices: 18.3 us -> 13 us  [passed_along(): return lax.ppermute(block, axis, [(i, (i + 1) % size) for i in range(size)])]
    pallas_call x10 -> x16, Pallas kernels: 22 us -> 17.9 us  [call(): pl.pallas_call(kernel, out_shape=[jax.ShapeDtypeStruct(shape, F32) for sh...]
    slice x2 -> x0, local copies, waits for them, and re-layouts: 1.28 us -> none  [the longest x1 0.66 us: body(): plan[step]]
    ppermute x16, waiting for transfers between devices: 17.6 us -> 18.7 us  [parts_of_sum(): lax.ppermute(term, axis, [(i, i ^ mask) for i in range(size)])]
    ppermute x7 -> x10, starting transfers between devices: 8.85 us -> 8.7 us  [passed_along(): return lax.ppermute(block, axis, [(i, (i + 1) % size) for i in range(size)])]
  transfers between devices with their start and end apart: 23 -> 26, of which waited for: 18 -> 21; matrix products, arithmetic and copies ran while one was open for 2% -> 0% of each run, Pallas kernels for 12% -> 20%
where the time goes in v1:
time: 75.7 us; the launch traced here: 75.5 us
  waiting for transfers between devices  31.7 us (42%)
  starting transfers between devices  23 us (30%)
  Pallas kernels  17.9 us (24%)
  local copies, waits for them, and re-layouts  1.45 us (2%)
  between operations  0.84 us (1%)
    ppermute x16, waiting for transfers between devices, parts_of_sum(): lax.ppermute(term, axis, [(i, i ^ mask) for i in range(size)])  18.7 us
    pallas_call x16, Pallas kernels, call(): pl.pallas_call(kernel, out_shape=[jax.ShapeDtypeStruct(shape, F32) for sh...  17.9 us
    ppermute x16, starting transfers between devices, parts_of_sum(): lax.ppermute(term, axis, [(i, i ^ mask) for i in range(size)])  14.3 us
    ppermute x10, waiting for transfers between devices, passed_along(): return lax.ppermute(block, axis, [(i, (i + 1) % size) for i in range(size)])  13 us
    ppermute x10, starting transfers between devices, passed_along(): return lax.ppermute(block, axis, [(i, (i + 1) % size) for i in range(size)])  8.7 us
  transfers between devices with their start and end apart: 26, of which 21 were waited for; matrix products, arithmetic and copies ran while one was open for 0% of the time, Pallas kernels for 20%

profile of v1, /device:TPU:0, one launch (start us, length us, event | category | flops | bytes accessed | tf_op | source)
XLA Modules:
  0.0 75.5 jit_solution(16860282376619051877)
XLA Ops:
  0.6 1.2 %copy-done = f32[1024,256]{1,0:T(8,128)S(1)} copy-done((f32[1024,256]{1,0:T(8,128)S(1)}, f32[1024,256]{1,0:T(8,128)}, u32[]{:S(2)}) %copy-start) | copy-done | bytes 1048600
  2.3 3.1 %collective-permute-start.5 = (f32[640,256]{1,0:T(8,128)S(1)}, f32[640,256]{1,0:T(8,128)S(1)}, u32[]{:S(2)}, u32[]{:S(2)}) collective-permute-start(f32[640,256]{1,0:T(8,128)S(1)} %get-tuple-element.26), channel_id=1, source_target_pairs={{0,8},{8,16},{16,24},{24,0},{1,9},{9,17},{17,25},{25,1},{2,10},{10... | collective-permute-start | bytes 1966088 | tf_op jit(solution)/shard_map/ppermute | solution.py:180
  5.4 1.3 %collective-permute-done = f32[136,128]{1,0:T(8,128)S(1)} collective-permute-done((f32[136,128]{1,0:T(8,128)S(1)}, f32[136,128]{1,0:T(8,128)S(1)}, u32[]{:S(2)}, u32[]{:S(2)}) %collective-permute-start) | collective-permute-done | bytes 69664 | tf_op jit(solution)/shard_map/ppermute | solution.py:191
  6.6 2.5 %collective-permute-start.3 = (f32[136,128]{1,0:T(8,128)S(1)}, f32[136,128]{1,0:T(8,128)S(1)}, u32[]{:S(2)}, u32[]{:S(2)}) collective-permute-start(f32[136,128]{1,0:T(8,128)S(1)} %add.28.refs_0_), channel_id=1, source_target_pairs={{0,6},{1,7},{2,4},{3,5},{4,2},{5,3},{6,0},{7,1},{8,14},{9,15},{10,... | collective-permute-start | bytes 208904 | tf_op jit(solution)/shard_map/ppermute | solution.py:191
  9.2 0.5 collective-permute-start.2
  9.7 0.5 collective-permute-start.1
  10.4 1.6 %collective-permute-done.3.refs_3_ = f32[136,128]{1,0:T(8,128)S(1)} collective-permute-done((f32[136,128]{1,0:T(8,128)S(1)}, f32[136,128]{1,0:T(8,128)S(1)}, u32[]{:S(2)}, u32[]{:S(2)}) %collective-permute-start.3) | collective-permute-done | bytes 69664 | tf_op jit(solution)/shard_map/ppermute | solution.py:191
  11.9 1.5 %collective-permute-done.2.refs_2_ = f32[136,128]{1,0:T(8,128)S(1)} collective-permute-done((f32[136,128]{1,0:T(8,128)S(1)}, f32[136,128]{1,0:T(8,128)S(1)}, u32[]{:S(2)}, u32[]{:S(2)}) %collective-permute-start.2) | collective-permute-done | bytes 69664 | tf_op jit(solution)/shard_map/ppermute | solution.py:191
  13.5 0.5 collective-permute-done.1.refs_1_
  14.2 1.6 %collective-permute-start.4 = (f32[136,128]{1,0:T(8,128)S(1)}, f32[136,128]{1,0:T(8,128)S(1)}, u32[]{:S(2)}, u32[]{:S(2)}) collective-permute-start(f32[136,128]{1,0:T(8,128)S(1)} %ratio.3.s_ref), channel_id=1, source_target_pairs={{0,8},{8,16},{16,24},{24,0},{1,9},{9,17},{17,25},{25,1},{2,10},{10... | collective-permute-start | bytes 208904 | tf_op jit(solution)/shard_map/ppermute | solution.py:180
  15.8 2.5 %own.3 = (f32[1024,128]{1,0:T(8,128)S(1)}, f32[384,128]{1,0:T(8,128)S(1)}, f32[128,128]{1,0:T(8,128)S(1)}) custom-call(f32[136,128]{1,0:T(8,128)S(1)} %ratio.3.s_ref, f32[1024,256]{1,0:T(8,128)S(1)} %copy-done.1), custom_call_target="tpu_custom_call" | custom-call | flops 1000000000 | bytes 3500001 | tf_op jit(solution)/shard_map/own/pallas_call | solution.py:166
  18.4 1.6 %collective-permute-start.6 = (f32[384,128]{1,0:T(8,128)S(1)}, f32[384,128]{1,0:T(8,128)S(1)}, u32[]{:S(2)}, u32[]{:S(2)}) collective-permute-start(f32[384,128]{1,0:T(8,128)S(1)} %get-tuple-element.28), channel_id=1, source_target_pairs={{0,8},{8,16},{16,24},{24,0},{1,9},{9,17},{17,25},{25,1},{2,10},{10... | collective-permute-start | bytes 589832 | tf_op jit(solution)/shard_map/ppermute | solution.py:180
  20.0 4.5 %collective-permute-done.4.s_ref = f32[136,128]{1,0:T(8,128)S(1)} collective-permute-done((f32[136,128]{1,0:T(8,128)S(1)}, f32[136,128]{1,0:T(8,128)S(1)}, u32[]{:S(2)}, u32[]{:S(2)}) %collective-permute-start.4) | collective-permute-done | bytes 69664 | tf_op jit(solution)/shard_map/ppermute | solution.py:180
  24.4 1.6 %inverse.3.inner_ref = f32[128,128]{1,0:T(8,128)S(1)} custom-call(f32[136,128]{1,0:T(8,128)S(1)} %collective-permute-done.4.s_ref), custom_call_target="tpu_custom_call" | custom-call | flops 2000000000 | bytes 7000001 | tf_op jit(solution)/shard_map/inverse/pallas_call | solution.py:166
  26.1 0.9 %turn.3 = (f32[640,128]{1,0:T(8,128)S(1)}, f32[640,128]{1,0:T(8,128)S(1)}) custom-call(f32[136,128]{1,0:T(8,128)S(1)} %collective-permute-done.4.s_ref, f32[128,128]{1,0:T(8,128)S(1)} %inverse.3.inner_ref, f32[640,256]{1,0:T(8,128)S(1)} %collective-permute-done.5.refs_0_), custom_call_target="tpu_custom_call" | custom-call | flops 1000000000 | bytes 3500001 | tf_op jit(solution)/shard_map/turn/pallas_call | solution.py:166
  27.0 0.8 %collective-permute-done.6.tail_ref = f32[384,128]{1,0:T(8,128)S(1)} collective-permute-done((f32[384,128]{1,0:T(8,128)S(1)}, f32[384,128]{1,0:T(8,128)S(1)}, u32[]{:S(2)}, u32[]{:S(2)}) %collective-permute-start.6) | collective-permute-done | bytes 196640 | tf_op jit(solution)/shard_map/ppermute | solution.py:180
  28.5 1.2 %collective-permute-done.7 = f32[136,128]{1,0:T(8,128)S(1)} collective-permute-done((f32[136,128]{1,0:T(8,128)S(1)}, f32[136,128]{1,0:T(8,128)S(1)}, u32[]{:S(2)}, u32[]{:S(2)}) %collective-permute-start.7) | collective-permute-done | bytes 69664 | tf_op jit(solution)/shard_map/ppermute | solution.py:191
  29.7 2.5 %collective-permute-start.10 = (f32[136,128]{1,0:T(8,128)S(1)}, f32[136,128]{1,0:T(8,128)S(1)}, u32[]{:S(2)}, u32[]{:S(2)}) collective-permute-start(f32[136,128]{1,0:T(8,128)S(1)} %add.29.refs_0_), channel_id=1, source_target_pairs={{0,6},{1,7},{2,4},{3,5},{4,2},{5,3},{6,0},{7,1},{8,14},{9,15},{10,... | collective-permute-start | bytes 208904 | tf_op jit(solution)/shard_map/ppermute | solution.py:191
  32.2 0.5 collective-permute-start.9
  32.7 0.5 collective-permute-start.8
  33.3 1.6 %collective-permute-done.10.refs_3_ = f32[136,128]{1,0:T(8,128)S(1)} collective-permute-done((f32[136,128]{1,0:T(8,128)S(1)}, f32[136,128]{1,0:T(8,128)S(1)}, u32[]{:S(2)}, u32[]{:S(2)}) %collective-permute-start.10) | collective-permute-done | bytes 69664 | tf_op jit(solution)/shard_map/ppermute | solution.py:191
  35.0 1.5 %collective-permute-done.9.refs_2_ = f32[136,128]{1,0:T(8,128)S(1)} collective-permute-done((f32[136,128]{1,0:T(8,128)S(1)}, f32[136,128]{1,0:T(8,128)S(1)}, u32[]{:S(2)}, u32[]{:S(2)}) %collective-permute-start.9) | collective-permute-done | bytes 69664 | tf_op jit(solution)/shard_map/ppermute | solution.py:191
  36.5 0.5 collective-permute-done.8.refs_1_
  37.3 2.5 %own.4 = (f32[1024,128]{1,0:T(8,128)S(1)}, f32[256,128]{1,0:T(8,128)S(1)}) custom-call(f32[136,128]{1,0:T(8,128)S(1)} %ratio.4.s_ref, f32[1024,256]{1,0:T(8,128)S(1)} %get-tuple-element.30.pair_ref), custom_call_target="tpu_custom_call" | custom-call | flops 1000000000 | bytes 3500001 | tf_op jit(solution)/shard_map/own/pallas_call | solution.py:166
  39.8 1.6 %collective-permute-start.14 = (f32[256,128]{1,0:T(8,128)S(1)}, f32[256,128]{1,0:T(8,128)S(1)}, u32[]{:S(2)}, u32[]{:S(2)}) collective-permute-start(f32[256,128]{1,0:T(8,128)S(1)} %get-tuple-element.37), channel_id=1, source_target_pairs={{0,8},{8,16},{16,24},{24,0},{1,9},{9,17},{17,25},{25,1},{2,10},{10... | collective-permute-start | bytes 393224 | tf_op jit(solution)/shard_map/ppermute | solution.py:180
  41.5 3.6 %collective-permute-done.11.s_ref = f32[136,128]{1,0:T(8,128)S(1)} collective-permute-done((f32[136,128]{1,0:T(8,128)S(1)}, f32[136,128]{1,0:T(8,128)S(1)}, u32[]{:S(2)}, u32[]{:S(2)}) %collective-permute-start.11) | collective-permute-done | bytes 69664 | tf_op jit(solution)/shard_map/ppermute | solution.py:180
  45.1 1.6 %inverse.4.inner_ref = f32[128,128]{1,0:T(8,128)S(1)} custom-call(f32[136,128]{1,0:T(8,128)S(1)} %collective-permute-done.11.s_ref), custom_call_target="tpu_custom_call" | custom-call | flops 2000000000 | bytes 7000001 | tf_op jit(solution)/shard_map/inverse/pallas_call | solution.py:166
  46.7 1.0 %turn.4 = (f32[768,128]{1,0:T(8,128)S(1)}, f32[768,128]{1,0:T(8,128)S(1)}) custom-call(f32[136,128]{1,0:T(8,128)S(1)} %collective-permute-done.11.s_ref, f32[128,128]{1,0:T(8,128)S(1)} %inverse.4.inner_ref, f32[640,128]{1,0:T(8,128)S(1)} %get-tuple-element.32.refs_0_, f32[768,128]{1,0:T(8,128)S(1)} %collective-permute-done.12.refs_1_, ...), custom_call_target="tpu_custom_call" | custom-call | flops 1000000000 | bytes 3500001 | tf_op jit(solution)/shard_map/turn/pallas_call | solution.py:166
  48.4 1.2 %collective-permute-done.15 = f32[136,128]{1,0:T(8,128)S(1)} collective-permute-done((f32[136,128]{1,0:T(8,128)S(1)}, f32[136,128]{1,0:T(8,128)S(1)}, u32[]{:S(2)}, u32[]{:S(2)}) %collective-permute-start.15) | collective-permute-done | bytes 69664 | tf_op jit(solution)/shard_map/ppermute | solution.py:191
  49.6 2.5 %collective-permute-start.18 = (f32[136,128]{1,0:T(8,128)S(1)}, f32[136,128]{1,0:T(8,128)S(1)}, u32[]{:S(2)}, u32[]{:S(2)}) collective-permute-start(f32[136,128]{1,0:T(8,128)S(1)} %add.30.refs_0_), channel_id=1, source_target_pairs={{0,6},{1,7},{2,4},{3,5},{4,2},{5,3},{6,0},{7,1},{8,14},{9,15},{10,... | collective-permute-start | bytes 208904 | tf_op jit(solution)/shard_map/ppermute | solution.py:191
  52.1 0.5 collective-permute-start.17
  52.6 0.5 collective-permute-start.16
  53.1 1.7 %collective-permute-done.18.refs_3_ = f32[136,128]{1,0:T(8,128)S(1)} collective-permute-done((f32[136,128]{1,0:T(8,128)S(1)}, f32[136,128]{1,0:T(8,128)S(1)}, u32[]{:S(2)}, u32[]{:S(2)}) %collective-permute-start.18) | collective-permute-done | bytes 69664 | tf_op jit(solution)/shard_map/ppermute | solution.py:191
  54.9 1.5 %collective-permute-done.17.refs_2_ = f32[136,128]{1,0:T(8,128)S(1)} collective-permute-done((f32[136,128]{1,0:T(8,128)S(1)}, f32[136,128]{1,0:T(8,128)S(1)}, u32[]{:S(2)}, u32[]{:S(2)}) %collective-permute-start.17) | collective-permute-done | bytes 69664 | tf_op jit(solution)/shard_map/ppermute | solution.py:191
  56.4 0.5 collective-permute-done.16.refs_1_
  57.1 2.3 %own.5 = (f32[1024,128]{1,0:T(8,128)S(1)}, f32[256,128]{1,0:T(8,128)S(1)}) custom-call(f32[136,128]{1,0:T(8,128)S(1)} %ratio.5.s_ref, f32[1024,256]{1,0:T(8,128)S(1)} %get-tuple-element.39.pair_ref), custom_call_target="tpu_custom_call" | custom-call | flops 1000000000 | bytes 3500001 | tf_op jit(solution)/shard_map/own/pallas_call | solution.py:166
  59.8 3.9 %collective-permute-done.19.s_ref = f32[136,128]{1,0:T(8,128)S(1)} collective-permute-done((f32[136,128]{1,0:T(8,128)S(1)}, f32[136,128]{1,0:T(8,128)S(1)}, u32[]{:S(2)}, u32[]{:S(2)}) %collective-permute-start.19) | collective-permute-done | bytes 69664 | tf_op jit(solution)/shard_map/ppermute | solution.py:180
  63.6 1.4 %inverse.5.inner_ref = f32[128,128]{1,0:T(8,128)S(1)} custom-call(f32[136,128]{1,0:T(8,128)S(1)} %collective-permute-done.19.s_ref), custom_call_target="tpu_custom_call" | custom-call | flops 2000000000 | bytes 7000001 | tf_op jit(solution)/shard_map/inverse/pallas_call | solution.py:166
  65.0 1.0 %turn.5.moving_ref = f32[768,128]{1,0:T(8,128)S(1)} custom-call(f32[136,128]{1,0:T(8,128)S(1)} %collective-permute-done.19.s_ref, f32[128,128]{1,0:T(8,128)S(1)} %inverse.5.inner_ref, f32[768,128]{1,0:T(8,128)S(1)} %get-tuple-element.41.refs_0_, f32[768,128]{1,0:T(8,128)S(1)} %collective-permute-done.20.refs_1_), custom_call_target="tpu_custom_call" | custom-call | flops 1000000000 | bytes 3500001 | tf_op jit(solution)/shard_map/turn/pallas_call | solution.py:166
  66.3 1.1 %join.5 = (f32[1024,256]{1,0:T(8,128)}, f32[8,128]{1,0:T(8,128)S(1)}) custom-call(f32[1024,128]{1,0:T(8,128)S(1)} %get-tuple-element.40.staying_ref, f32[768,128]{1,0:T(8,128)S(1)} %turn.5.moving_ref, f32[256,128]{1,0:T(8,128)S(1)} %collective-permute-done.21.tail_ref), custom_call_target="tpu_custom_call" | custom-call | flops 500000000 | bytes 1750001 | tf_op jit(solution)/shard_map/join/pallas_call | solution.py:166
  67.4 1.2 %collective-permute-done.22 = f32[8,128]{1,0:T(8,128)S(1)} collective-permute-done((f32[8,128]{1,0:T(8,128)S(1)}, f32[8,128]{1,0:T(8,128)S(1)}, u32[]{:S(2)}, u32[]{:S(2)}) %collective-permute-start.22) | collective-permute-done | bytes 4128 | tf_op jit(solution)/shard_map/ppermute | solution.py:191
  68.5 2.2 %collective-permute-start.25 = (f32[8,128]{1,0:T(8,128)S(1)}, f32[8,128]{1,0:T(8,128)S(1)}, u32[]{:S(2)}, u32[]{:S(2)}) collective-permute-start(f32[8,128]{1,0:T(8,128)S(1)} %add.31), channel_id=1, source_target_pairs={{0,6},{1,7},{2,4},{3,5},{4,2},{5,3},{6,0},{7,1},{8,14},{9,15},{10,... | collective-permute-start | bytes 12296 | tf_op jit(solution)/shard_map/ppermute | solution.py:191
  70.7 0.5 collective-permute-start.24
  71.3 0.7 collective-permute-start.23
  72.0 1.0 %collective-permute-done.25 = f32[8,128]{1,0:T(8,128)S(1)} collective-permute-done((f32[8,128]{1,0:T(8,128)S(1)}, f32[8,128]{1,0:T(8,128)S(1)}, u32[]{:S(2)}, u32[]{:S(2)}) %collective-permute-start.25) | collective-permute-done | bytes 4128 | tf_op jit(solution)/shard_map/ppermute | solution.py:191
  73.0 1.3 %collective-permute-done.24 = f32[8,128]{1,0:T(8,128)S(1)} collective-permute-done((f32[8,128]{1,0:T(8,128)S(1)}, f32[8,128]{1,0:T(8,128)S(1)}, u32[]{:S(2)}, u32[]{:S(2)}) %collective-permute-start.24) | collective-permute-done | bytes 4128 | tf_op jit(solution)/shard_map/ppermute | solution.py:191
  74.4 0.5 collective-permute-done.23
  74.9 0.6 sqrt_bitcast_fusion
  (36 shorter events, 3.1 us)
Async XLA Ops:
  0.6 1.2 %copy-start = (f32[1024,256]{1,0:T(8,128)S(1)}, f32[1024,256]{1,0:T(8,128)}, u32[]{:S(2)}) copy-start(f32[1024,256]{1,0:T(8,128)} %pair_ref.3) | copy-start | bytes 3145732
  1.9 13.9 %copy-start.1 = (f32[1024,256]{1,0:T(8,128)S(1)}, f32[1024,256]{1,0:T(8,128)}, u32[]{:S(2)}) copy-start(f32[1024,256]{1,0:T(8,128)} %pair_ref.3) | copy-start | bytes 3145732
  2.3 23.8 %collective-permute-start.5 = (f32[640,256]{1,0:T(8,128)S(1)}, f32[640,256]{1,0:T(8,128)S(1)}, u32[]{:S(2)}, u32[]{:S(2)}) collective-permute-start(f32[640,256]{1,0:T(8,128)S(1)} %get-tuple-element.26), channel_id=1, source_target_pairs={{0,8},{8,16},{16,24},{24,0},{1,9},{9,17},{17,25},{25,1},{2,10},{10... | collective-permute-start | bytes 1966088 | tf_op jit(solution)/shard_map/ppermute | solution.py:180
  5.4 4.8 %copy-start.2 = (s32[3,1]{0,1:T(1,128)S(1)}, s32[3,1]{0,1:T(1,128)}, u32[]{:S(2)}) copy-start(s32[3,1]{0,1:T(1,128)} %param.3) | copy-start | bytes 40
  5.4 1.3 %collective-permute-start = (f32[136,128]{1,0:T(8,128)S(1)}, f32[136,128]{1,0:T(8,128)S(1)}, u32[]{:S(2)}, u32[]{:S(2)}) collective-permute-start(f32[136,128]{1,0:T(8,128)S(1)} %get-tuple-element.24), channel_id=1, source_target_pairs={{0,1},{1,0},{2,3},{3,2},{4,5},{5,4},{6,7},{7,6},{8,9},{9,8},{10,11... | collective-permute-start | bytes 208904 | tf_op jit(solution)/shard_map/ppermute | solution.py:191
  6.6 5.3 %collective-permute-start.3 = (f32[136,128]{1,0:T(8,128)S(1)}, f32[136,128]{1,0:T(8,128)S(1)}, u32[]{:S(2)}, u32[]{:S(2)}) collective-permute-start(f32[136,128]{1,0:T(8,128)S(1)} %add.28.refs_0_), channel_id=1, source_target_pairs={{0,6},{1,7},{2,4},{3,5},{4,2},{5,3},{6,0},{7,1},{8,14},{9,15},{10,... | collective-permute-start | bytes 208904 | tf_op jit(solution)/shard_map/ppermute | solution.py:191
  9.2 4.3 %collective-permute-start.2 = (f32[136,128]{1,0:T(8,128)S(1)}, f32[136,128]{1,0:T(8,128)S(1)}, u32[]{:S(2)}, u32[]{:S(2)}) collective-permute-start(f32[136,128]{1,0:T(8,128)S(1)} %add.28.refs_0_), channel_id=1, source_target_pairs={{0,4},{1,5},{2,6},{3,7},{4,0},{5,1},{6,2},{7,3},{8,12},{9,13},{10,... | collective-permute-start | bytes 208904 | tf_op jit(solution)/shard_map/ppermute | solution.py:191
  9.7 4.3 %collective-permute-start.1 = (f32[136,128]{1,0:T(8,128)S(1)}, f32[136,128]{1,0:T(8,128)S(1)}, u32[]{:S(2)}, u32[]{:S(2)}) collective-permute-start(f32[136,128]{1,0:T(8,128)S(1)} %add.28.refs_0_), channel_id=1, source_target_pairs={{0,2},{1,3},{2,0},{3,1},{4,6},{5,7},{6,4},{7,5},{8,10},{9,11},{10,... | collective-permute-start | bytes 208904 | tf_op jit(solution)/shard_map/ppermute | solution.py:191
  14.2 10.3 %collective-permute-start.4 = (f32[136,128]{1,0:T(8,128)S(1)}, f32[136,128]{1,0:T(8,128)S(1)}, u32[]{:S(2)}, u32[]{:S(2)}) collective-permute-start(f32[136,128]{1,0:T(8,128)S(1)} %ratio.3.s_ref), channel_id=1, source_target_pairs={{0,8},{8,16},{16,24},{24,0},{1,9},{9,17},{17,25},{25,1},{2,10},{10... | collective-permute-start | bytes 208904 | tf_op jit(solution)/shard_map/ppermute | solution.py:180
  18.4 9.5 %collective-permute-start.6 = (f32[384,128]{1,0:T(8,128)S(1)}, f32[384,128]{1,0:T(8,128)S(1)}, u32[]{:S(2)}, u32[]{:S(2)}) collective-permute-start(f32[384,128]{1,0:T(8,128)S(1)} %get-tuple-element.28), channel_id=1, source_target_pairs={{0,8},{8,16},{16,24},{24,0},{1,9},{9,17},{17,25},{25,1},{2,10},{10... | collective-permute-start | bytes 589832 | tf_op jit(solution)/shard_map/ppermute | solution.py:180
  28.3 1.3 %collective-permute-start.7 = (f32[136,128]{1,0:T(8,128)S(1)}, f32[136,128]{1,0:T(8,128)S(1)}, u32[]{:S(2)}, u32[]{:S(2)}) collective-permute-start(f32[136,128]{1,0:T(8,128)S(1)} %get-tuple-element.29), channel_id=1, source_target_pairs={{0,1},{1,0},{2,3},{3,2},{4,5},{5,4},{6,7},{7,6},{8,9},{9,8},{10,11... | collective-permute-start | bytes 208904 | tf_op jit(solution)/shard_map/ppermute | solution.py:191
  28.4 18.3 %collective-permute-start.12 = (f32[768,128]{1,0:T(8,128)S(1)}, f32[768,128]{1,0:T(8,128)S(1)}, u32[]{:S(2)}, u32[]{:S(2)}) collective-permute-start(f32[768,128]{1,0:T(8,128)S(1)} %get-tuple-element.33), channel_id=1, source_target_pairs={{0,8},{8,16},{16,24},{24,0},{1,9},{9,17},{17,25},{25,1},{2,10},{10... | collective-permute-start | bytes 1179656 | tf_op jit(solution)/shard_map/ppermute | solution.py:180
  29.7 5.3 %collective-permute-start.10 = (f32[136,128]{1,0:T(8,128)S(1)}, f32[136,128]{1,0:T(8,128)S(1)}, u32[]{:S(2)}, u32[]{:S(2)}) collective-permute-start(f32[136,128]{1,0:T(8,128)S(1)} %add.29.refs_0_), channel_id=1, source_target_pairs={{0,6},{1,7},{2,4},{3,5},{4,2},{5,3},{6,0},{7,1},{8,14},{9,15},{10,... | collective-permute-start | bytes 208904 | tf_op jit(solution)/shard_map/ppermute | solution.py:191
  32.2 4.3 %collective-permute-start.9 = (f32[136,128]{1,0:T(8,128)S(1)}, f32[136,128]{1,0:T(8,128)S(1)}, u32[]{:S(2)}, u32[]{:S(2)}) collective-permute-start(f32[136,128]{1,0:T(8,128)S(1)} %add.29.refs_0_), channel_id=1, source_target_pairs={{0,4},{1,5},{2,6},{3,7},{4,0},{5,1},{6,2},{7,3},{8,12},{9,13},{10,... | collective-permute-start | bytes 208904 | tf_op jit(solution)/shard_map/ppermute | solution.py:191
  32.7 4.3 %collective-permute-start.8 = (f32[136,128]{1,0:T(8,128)S(1)}, f32[136,128]{1,0:T(8,128)S(1)}, u32[]{:S(2)}, u32[]{:S(2)}) collective-permute-start(f32[136,128]{1,0:T(8,128)S(1)} %add.29.refs_0_), channel_id=1, source_target_pairs={{0,2},{1,3},{2,0},{3,1},{4,6},{5,7},{6,4},{7,5},{8,10},{9,11},{10,... | collective-permute-start | bytes 208904 | tf_op jit(solution)/shard_map/ppermute | solution.py:191
  33.2 13.5 %collective-permute-start.13 = (f32[128,128]{1,0:T(8,128)S(1)}, f32[128,128]{1,0:T(8,128)S(1)}, u32[]{:S(2)}, u32[]{:S(2)}) collective-permute-start(f32[128,128]{1,0:T(8,128)S(1)} %get-tuple-element.35), channel_id=1, source_target_pairs={{0,8},{8,16},{16,24},{24,0},{1,9},{9,17},{17,25},{25,1},{2,10},{10... | collective-permute-start | bytes 196616 | tf_op jit(solution)/shard_map/ppermute | solution.py:180
  37.1 8.0 %collective-permute-start.11 = (f32[136,128]{1,0:T(8,128)S(1)}, f32[136,128]{1,0:T(8,128)S(1)}, u32[]{:S(2)}, u32[]{:S(2)}) collective-permute-start(f32[136,128]{1,0:T(8,128)S(1)} %ratio.4.s_ref), channel_id=1, source_target_pairs={{0,8},{8,16},{16,24},{24,0},{1,9},{9,17},{17,25},{25,1},{2,10},{10... | collective-permute-start | bytes 208904 | tf_op jit(solution)/shard_map/ppermute | solution.py:180
  39.8 7.9 %collective-permute-start.14 = (f32[256,128]{1,0:T(8,128)S(1)}, f32[256,128]{1,0:T(8,128)S(1)}, u32[]{:S(2)}, u32[]{:S(2)}) collective-permute-start(f32[256,128]{1,0:T(8,128)S(1)} %get-tuple-element.37), channel_id=1, source_target_pairs={{0,8},{8,16},{16,24},{24,0},{1,9},{9,17},{17,25},{25,1},{2,10},{10... | collective-permute-start | bytes 393224 | tf_op jit(solution)/shard_map/ppermute | solution.py:180
  48.2 1.3 %collective-permute-start.15 = (f32[136,128]{1,0:T(8,128)S(1)}, f32[136,128]{1,0:T(8,128)S(1)}, u32[]{:S(2)}, u32[]{:S(2)}) collective-permute-start(f32[136,128]{1,0:T(8,128)S(1)} %get-tuple-element.38), channel_id=1, source_target_pairs={{0,1},{1,0},{2,3},{3,2},{4,5},{5,4},{6,7},{7,6},{8,9},{9,8},{10,11... | collective-permute-start | bytes 208904 | tf_op jit(solution)/shard_map/ppermute | solution.py:191
  48.3 16.7 %collective-permute-start.20 = (f32[768,128]{1,0:T(8,128)S(1)}, f32[768,128]{1,0:T(8,128)S(1)}, u32[]{:S(2)}, u32[]{:S(2)}) collective-permute-start(f32[768,128]{1,0:T(8,128)S(1)} %get-tuple-element.42), channel_id=1, source_target_pairs={{0,8},{8,16},{16,24},{24,0},{1,9},{9,17},{17,25},{25,1},{2,10},{10... | collective-permute-start | bytes 1179656 | tf_op jit(solution)/shard_map/ppermute | solution.py:180
  49.6 5.3 %collective-permute-start.18 = (f32[136,128]{1,0:T(8,128)S(1)}, f32[136,128]{1,0:T(8,128)S(1)}, u32[]{:S(2)}, u32[]{:S(2)}) collective-permute-start(f32[136,128]{1,0:T(8,128)S(1)} %add.30.refs_0_), channel_id=1, source_target_pairs={{0,6},{1,7},{2,4},{3,5},{4,2},{5,3},{6,0},{7,1},{8,14},{9,15},{10,... | collective-permute-start | bytes 208904 | tf_op jit(solution)/shard_map/ppermute | solution.py:191
  52.1 4.3 %collective-permute-start.17 = (f32[136,128]{1,0:T(8,128)S(1)}, f32[136,128]{1,0:T(8,128)S(1)}, u32[]{:S(2)}, u32[]{:S(2)}) collective-permute-start(f32[136,128]{1,0:T(8,128)S(1)} %add.30.refs_0_), channel_id=1, source_target_pairs={{0,4},{1,5},{2,6},{3,7},{4,0},{5,1},{6,2},{7,3},{8,12},{9,13},{10,... | collective-permute-start | bytes 208904 | tf_op jit(solution)/shard_map/ppermute | solution.py:191
  52.6 4.3 %collective-permute-start.16 = (f32[136,128]{1,0:T(8,128)S(1)}, f32[136,128]{1,0:T(8,128)S(1)}, u32[]{:S(2)}, u32[]{:S(2)}) collective-permute-start(f32[136,128]{1,0:T(8,128)S(1)} %add.30.refs_0_), channel_id=1, source_target_pairs={{0,2},{1,3},{2,0},{3,1},{4,6},{5,7},{6,4},{7,5},{8,10},{9,11},{10,... | collective-permute-start | bytes 208904 | tf_op jit(solution)/shard_map/ppermute | solution.py:191
  57.0 6.6 %collective-permute-start.19 = (f32[136,128]{1,0:T(8,128)S(1)}, f32[136,128]{1,0:T(8,128)S(1)}, u32[]{:S(2)}, u32[]{:S(2)}) collective-permute-start(f32[136,128]{1,0:T(8,128)S(1)} %ratio.5.s_ref), channel_id=1, source_target_pairs={{0,8},{8,16},{16,24},{24,0},{1,9},{9,17},{17,25},{25,1},{2,10},{10... | collective-permute-start | bytes 208904 | tf_op jit(solution)/shard_map/ppermute | solution.py:180
  59.4 6.8 %collective-permute-start.21 = (f32[256,128]{1,0:T(8,128)S(1)}, f32[256,128]{1,0:T(8,128)S(1)}, u32[]{:S(2)}, u32[]{:S(2)}) collective-permute-start(f32[256,128]{1,0:T(8,128)S(1)} %get-tuple-element.43), channel_id=1, source_target_pairs={{0,8},{8,16},{16,24},{24,0},{1,9},{9,17},{17,25},{25,1},{2,10},{10... | collective-permute-start | bytes 393224 | tf_op jit(solution)/shard_map/ppermute | solution.py:180
  67.4 1.2 %collective-permute-start.22 = (f32[8,128]{1,0:T(8,128)S(1)}, f32[8,128]{1,0:T(8,128)S(1)}, u32[]{:S(2)}, u32[]{:S(2)}) collective-permute-start(f32[8,128]{1,0:T(8,128)S(1)} %get-tuple-element.45), channel_id=1, source_target_pairs={{0,1},{1,0},{2,3},{3,2},{4,5},{5,4},{6,7},{7,6},{8,9},{9,8},{10,11... | collective-permute-start | bytes 12296 | tf_op jit(solution)/shard_map/ppermute | solution.py:191
  68.5 4.5 %collective-permute-start.25 = (f32[8,128]{1,0:T(8,128)S(1)}, f32[8,128]{1,0:T(8,128)S(1)}, u32[]{:S(2)}, u32[]{:S(2)}) collective-permute-start(f32[8,128]{1,0:T(8,128)S(1)} %add.31), channel_id=1, source_target_pairs={{0,6},{1,7},{2,4},{3,5},{4,2},{5,3},{6,0},{7,1},{8,14},{9,15},{10,... | collective-permute-start | bytes 12296 | tf_op jit(solution)/shard_map/ppermute | solution.py:191
  70.7 3.6 %collective-permute-start.24 = (f32[8,128]{1,0:T(8,128)S(1)}, f32[8,128]{1,0:T(8,128)S(1)}, u32[]{:S(2)}, u32[]{:S(2)}) collective-permute-start(f32[8,128]{1,0:T(8,128)S(1)} %add.31), channel_id=1, source_target_pairs={{0,4},{1,5},{2,6},{3,7},{4,0},{5,1},{6,2},{7,3},{8,12},{9,13},{10,... | collective-permute-start | bytes 12296 | tf_op jit(solution)/shard_map/ppermute | solution.py:191
  71.3 3.6 %collective-permute-start.23 = (f32[8,128]{1,0:T(8,128)S(1)}, f32[8,128]{1,0:T(8,128)S(1)}, u32[]{:S(2)}, u32[]{:S(2)}) collective-permute-start(f32[8,128]{1,0:T(8,128)S(1)} %add.31), channel_id=1, source_target_pairs={{0,2},{1,3},{2,0},{3,1},{4,6},{5,7},{6,4},{7,5},{8,10},{9,11},{10,... | collective-permute-start | bytes 12296 | tf_op jit(solution)/shard_map/ppermute | solution.py:191

commit v2 on v1

v2 whole, which is shorter than its diff:
```python
import functools
import jax
import jax.numpy as jnp
from jax import lax
from jax.experimental import pallas as pl
from jax.experimental.pallas import tpu as pltpu
from jax.sharding import PartitionSpec as P

epsilon = 1e-06
MICROS = {"own": 1.0, "inverse": 2.0, "turn": 1.0, "join": 0.5}
F32 = jnp.float32
BF16 = jnp.bfloat16
NN = (((1,), (0,)), ((), ()))
NT = (((1,), (1,)), ((), ()))
TN = (((0,), (0,)), ((), ()))
VMEM = pl.BlockSpec(memory_space=pltpu.VMEM)


def split(x):
    high = x.astype(BF16)
    return high, (x - high.astype(F32)).astype(BF16)


def product(a, b, dims):
    return lax.dot_general(a, b, dims, preferred_element_type=F32)


def right(b, transposed=False):
    high, low = split(b)
    zeros = jnp.zeros_like(low)
    if transposed:
        return jnp.concatenate([jnp.concatenate([high, high], axis=1), jnp.concatenate([low, zeros], axis=1)], axis=0)
    return jnp.concatenate([jnp.concatenate([high, low], axis=1), jnp.concatenate([high, zeros], axis=1)], axis=0)


def times(a, b, transposed=False):
    both = product(jnp.concatenate(split(a), axis=1), b, NT if transposed else NN)
    half = both.shape[1] // 2
    return both[:, :half] + both[:, half:]


def across(a, b):
    both = product(jnp.concatenate(split(a), axis=1), jnp.concatenate(split(b), axis=1), TN)
    width = a.shape[1]
    return both[:width, :width] + (both[:width, width:] + both[width:, :width])


def identity_of(width):
    shape = (width, width)
    return (lax.broadcasted_iota(jnp.int32, shape, 0) == lax.broadcasted_iota(jnp.int32, shape, 1)).astype(F32)


def gram_of(first, second, whole):
    width = first.shape[1]
    parts = [
        across(first, second),
        jnp.sum(first * first, axis=0, keepdims=True),
        jnp.sum(second * second, axis=0, keepdims=True),
        jnp.zeros((6, width), F32),
    ]
    if whole:
        above, below = triangles(width)
        parts.append(
            jnp.where(above, across(first, first), 0.0)
            + jnp.where(below, across(second, second), 0.0)
        )
    return jnp.concatenate(parts, axis=0)


def triangles(width):
    row = lax.broadcasted_iota(jnp.int32, (width, width), 0)
    column = lax.broadcasted_iota(jnp.int32, (width, width), 1)
    return row < column, row > column


def whole_gram(gram):
    width = gram.shape[1]
    above, below = triangles(width)
    identity = identity_of(width)
    cross, packed = gram[:width], gram[width + 8 :]
    blocks = []
    for triangle, diagonal in ((above, gram[width : width + 1]), (below, gram[width + 1 : width + 2])):
        half = jnp.where(triangle, packed, 0.0)
        blocks.append(half + half.T + identity * diagonal)
    return jnp.concatenate([blocks[0], cross.T], axis=0), jnp.concatenate([cross, blocks[1]], axis=0)


def inverse(skew, error_ref, total_ref):
    width = skew.shape[0]
    identity = identity_of(width)
    square = times(skew, right(skew, True), True)
    bound = jnp.minimum(
        jnp.max(jnp.sum(jnp.abs(square), axis=0, keepdims=True), axis=1, keepdims=True),
        jnp.sqrt(jnp.sum(jnp.sum(square * square, axis=0, keepdims=True), axis=1, keepdims=True)),
    )
    scale = 2.0 / (bound + 2.0)
    error_bound = bound / (bound + 2.0)
    error = (1.0 - scale) * identity - scale * square
    total = scale * identity
    for step in range(4):
        grow = 2.0 / (2.0 - error_bound * error_bound)
        if step == 0:
            total, error = (grow * scale) * (identity + error), times(error, right(error))
        else:
            both = times(jnp.concatenate([error, total], axis=0), right(error))
            total, error = grow * (total + both[width:]), both[:width]
        error = (1.0 - grow) * identity + grow * error
        error_bound = error_bound * error_bound / (2.0 - error_bound * error_bound)
    total_ref[...] = total + times(total, right(identity - total - times(square, right(total))))

    @pl.when(error_bound[0, 0] > 1e-3)
    def _():
        exact = functools.partial(lax.dot_general, precision=lax.Precision.HIGHEST, preferred_element_type=F32)
        square = exact(skew, skew, NT)
        error_ref[...] = (1.0 - scale) * identity - scale * square
        total_ref[...] = scale * identity

        def more(error_bound):
            grow = 2.0 / (2.0 - error_bound * error_bound)
            error, total = error_ref[...], total_ref[...]
            total_ref[...] = grow * (total + exact(total, error, NN))
            error_ref[...] = (1.0 - grow) * identity + grow * exact(error, error, NN)
            return error_bound * error_bound / (2.0 - error_bound * error_bound)

        lax.while_loop(lambda error_bound: error_bound > 1e-4, more, (bound / (bound + 2.0))[0, 0])
        for _ in range(2):
            total = total_ref[...]
            total_ref[...] = total + exact(total, identity - total - exact(square, total, NN), NN)

    return total_ref[...]


def rotated_halves(skew, inner, first, second):
    mixed = times(first + times(second, right(skew, True), True), right(inner))
    return 2.0 * mixed - first, second - 2.0 * times(mixed, right(skew))


def gram_kernel(pair_ref, gram_ref, head_ref):
    width = pair_ref.shape[1] // 2
    gram_ref[...] = gram_of(pair_ref[:, :width], pair_ref[:, width:], gram_ref.shape[0] > width + 8)
    head_ref[...] = pair_ref[: head_ref.shape[0]]


def ratio_kernel(row, count, plan_ref, *refs):
    parts, (s_ref, *sum_ref) = refs[:count], refs[count:]
    gram = functools.reduce(lambda x, y: x + y, [ref[...] for ref in parts])
    if sum_ref:
        sum_ref[0][...] = gram
    width = gram.shape[1]
    cross, second_diag = gram[:width], gram[width + 1 : width + 2]
    first_diag = jnp.sum(identity_of(width) * gram[width : width + 1], axis=1, keepdims=True)
    difference = first_diag - second_diag
    s_ref[:width] = (
        cross * difference / (2.0 * (difference * difference + 4.0 * cross * cross + 0.01 * first_diag * second_diag))
    )
    s_ref[width:] = plan_ref[row : row + 8]


def own_kernel(known, kept, last, s_ref, pair_ref, *refs):
    *refs, error_ref, total_ref = refs
    width = s_ref.shape[1]
    rows = pair_ref.shape[0]
    skew = s_ref[:width]
    inner = inverse(skew, error_ref, total_ref)
    moves_second = s_ref[width : width + 1] > 0.5
    first, second = pair_ref[:, :width], pair_ref[:, width:]
    if last:
        gram_ref, *refs = refs
        identity, zeros = identity_of(width), jnp.zeros((width, width), F32)
        left, right = whole_gram(gram_ref[...])
        first = jnp.concatenate([first, left, identity, zeros], axis=0)
        second = jnp.concatenate([second, right, zeros, identity], axis=0)
    first, second = rotated_halves(skew, inner, first, second)
    staying = jnp.where(moves_second, first, second)
    moving = jnp.where(moves_second, second, first)
    staying_ref, *outs = refs
    staying_ref[...] = staying[:rows]
    if last:
        energies = [
            jnp.sum(half[rows : rows + 2 * width] * half[rows + 2 * width :], axis=0, keepdims=True)
            for half in (staying, moving)
        ]
        outs[-1][...] = jnp.concatenate(energies + [jnp.zeros((6, width), F32)], axis=0)
    if known < rows:
        outs[0][...] = moving[known:rows]
    if known < kept:
        outs[1 if known < rows else 0][...] = staying[known:kept]


def inverse_kernel(s_ref, inner_ref, error_ref, total_ref):
    inner_ref[...] = inverse(s_ref[: s_ref.shape[1]], error_ref, total_ref)


def turned(s_ref, inner_ref, refs):
    width = s_ref.shape[1]
    if len(refs) == 1:
        first, second = refs[0][:, :width], refs[0][:, width:]
    else:
        second = refs[1][...]
        first = jnp.concatenate([refs[0][...]] + [ref[...] for ref in refs[2:]], axis=0)
    first, second = rotated_halves(s_ref[:width], inner_ref[...], first, second)
    moves_second = s_ref[width : width + 1] > 0.5
    return jnp.where(moves_second, second, first), jnp.where(moves_second, first, second)


def joined(staying, moving, pair_ref, *gram_ref):
    width = staying.shape[1]
    pair_ref[:, :width] = staying
    pair_ref[:, width:] = moving
    for ref in gram_ref:
        ref[...] = gram_of(staying, moving, ref.shape[0] > width + 8)


def turn_kernel(parts, s_ref, inner_ref, *refs):
    moving, staying = turned(s_ref, inner_ref, refs[:parts])
    refs[parts][...] = moving
    if len(refs) > parts + 1:
        refs[parts + 1][...] = staying[: refs[parts + 1].shape[0]]


def join_kernel(kept, staying_ref, moving_ref, tail_ref, pair_ref, *outs):
    moving = jnp.concatenate([moving_ref[...], tail_ref[...]], axis=0)
    joined(staying_ref[...], moving, pair_ref, *outs[:1])
    if kept:
        outs[1][...] = moving[:kept]


def turn_join_kernel(kept, parts, s_ref, inner_ref, staying_ref, *refs):
    moving, neighbour_staying = turned(s_ref, inner_ref, refs[:parts])
    pair_ref, *outs = refs[parts:]
    joined(staying_ref[...], moving, pair_ref, *outs[:1])
    if kept:
        outs[1][...] = moving[:kept]
        outs[2][...] = neighbour_staying[: outs[2].shape[0]]


def call(kernel, operands, outs, scratch=(), name="", last=False):
    micros = 0.0 if last else MICROS.get(name, 0.0)
    return pl.pallas_call(
        kernel,
        out_shape=[jax.ShapeDtypeStruct(shape, F32) for shape in outs],
        in_specs=[VMEM] * len(operands),
        out_specs=[VMEM] * len(outs),
        scratch_shapes=list(scratch),
        compiler_params=pltpu.CompilerParams(vmem_limit_bytes=48 * 1024 * 1024),
        cost_estimate=pl.CostEstimate(flops=int(micros * 1e9) + 1, bytes_accessed=int(micros * 3.5e6) + 1, transcendentals=0),
        name=name,
    )(*operands)


def passed_along(block, axis):
    size = lax.axis_size(axis)
    return lax.ppermute(block, axis, [(i, (i + 1) % size) for i in range(size)])


def parts_of_sum(term, axis):
    size = lax.axis_size(axis)
    if size & (size - 1):
        return [lax.psum(term, axis)]
    parts, bit = [term], 1
    while bit < size:
        term = functools.reduce(lambda x, y: x + y, parts)
        masks = [bit] if bit == 1 or 2 * bit >= size else [bit, 2 * bit, 3 * bit]
        parts = [term] + [lax.ppermute(term, axis, [(i, i ^ mask) for i in range(size)]) for mask in masks]
        bit *= 2 if len(masks) == 1 else 4
    return parts


def known_rows(rows, rounds):
    sixteenths = [9, 12] + [14] * rounds
    return [rows * part // 256 * 16 for part in sixteenths[:rounds]] + [0]


def body(record, plan):
    rows, width = record.shape[0], record.shape[1] // 2
    rounds = plan.shape[0]
    total_rows = rows * lax.axis_size("tm")
    square, ratios = (width, width), (width + 8, width)
    grams = [ratios] * (rounds - 1) + [(2 * width + 8, width)]
    scratch = [pltpu.VMEM(square, F32)] * 2
    heads = known_rows(rows, rounds)
    pair = record
    terms, raw_head = call(gram_kernel, [pair], [grams[0], (heads[0], 2 * width)], name="gram")
    neighbour = [passed_along(raw_head, "col")]
    plan_rows = jnp.repeat(jnp.broadcast_to(plan.astype(F32), (rounds, width)), 8, axis=0)
    for step in range(rounds):
        known, kept, last = heads[step], heads[step + 1], step + 1 == rounds
        parts = parts_of_sum(terms, "tm")
        kernel = functools.partial(ratio_kernel, 8 * step, len(parts))
        ratio, *gram = call(kernel, [plan_rows] + parts, [ratios] + [grams[step]] * last, name="ratio", last=last)
        neighbour_ratio = passed_along(ratio, "col")
        outs = [(rows, width)] + [(rows - known, width)] * (known < rows) + [(kept - known, width)] * (known < kept)
        kernel = functools.partial(own_kernel, known, kept, last)
        staying, *sent = call(kernel, [ratio, pair] + gram, outs + [(8, width)] * last, scratch, name="own", last=last)
        (inner,) = call(inverse_kernel, [neighbour_ratio], [square], scratch, name="inverse", last=last)
        turn = [neighbour_ratio, inner]
        sums = [] if last else [grams[step + 1]]
        kept_outs = [(kept, width)] * (kept > 0)
        known_outs = [(min(known, kept), width)] * (kept > 0)
        if known < rows:
            tail = passed_along(sent[0], "col")
            kernel = functools.partial(turn_kernel, len(neighbour))
            moving, *kept_staying = call(kernel, turn + neighbour, [(known, width)] + known_outs, name="turn", last=last)
            if last:
                passed = passed_along(sent[-1], "col")
                moving, passed = lax.optimization_barrier((moving, passed))
            kernel = functools.partial(join_kernel, kept)
            pair, *rest = call(kernel, [staying, moving, tail], [record.shape] + sums + kept_outs, name="join", last=last)
        else:
            tail = None
            if last:
                passed = passed_along(sent[-1], "col")
            kernel = functools.partial(turn_join_kernel, kept, len(neighbour))
            pair, *rest = call(kernel, turn + [staying] + neighbour, [record.shape] + sums + kept_outs + known_outs, name="both", last=last)
            rest, kept_staying = rest[:2], rest[2:]
        if last:
            energy = jnp.concatenate([sent[-1][0], passed[1]])
            return (pair, jnp.sqrt(jnp.maximum(energy, 0.0) / total_rows + epsilon))
        terms, moving = rest
        neighbour = kept_staying + [passed_along(moving, "col")]
        if known < kept:
            more = sent[-1]
            if tail is not None:
                more, _ = lax.optimization_barrier((more, tail))
            neighbour.append(passed_along(more, "col"))


def solution(mesh):
    in_specs = (P("tm", "col"), P(None, "col"))
    out_specs = (P("tm", "col"), P("col"))
    return jax.shard_map(body, mesh=mesh, in_specs=in_specs, out_specs=out_specs, check_vma=False)
```

time: 75.7 us -> 69.8 us (0.922)
  waiting for transfers between devices: 31.7 us -> 27.3 us
  Pallas kernels: 17.9 us -> 16.5 us
    ppermute x16 -> x12, starting transfers between devices: 14.3 us -> 10.8 us  [parts_of_sum(): lax.ppermute(term, axis, [(i, i ^ mask) for i in range(size)])]
    ppermute x10 -> x12, starting transfers between devices: 8.7 us -> 12.1 us  [passed_along(): return lax.ppermute(block, axis, [(i, (i + 1) % size) for i in range(size)])]
    ppermute x10 -> x12, waiting for transfers between devices: 13 us -> 10.3 us  [passed_along(): return lax.ppermute(block, axis, [(i, (i + 1) % size) for i in range(size)])]
    ppermute x16 -> x12, waiting for transfers between devices: 18.7 us -> 17 us  [parts_of_sum(): lax.ppermute(term, axis, [(i, i ^ mask) for i in range(size)])]
    pallas_call x16, Pallas kernels: 17.9 us -> 16.5 us  [call(): pl.pallas_call(kernel, out_shape=[jax.ShapeDtypeStruct(shape, F32) for sh...]
  transfers between devices with their start and end apart: 26 -> 24, of which waited for: 21 -> 16; matrix products, arithmetic and copies ran while one was open for 0% -> 1% of each run, Pallas kernels for 20% -> 20%
where the time goes in v2:
time: 69.8 us; the launch traced here: 69.7 us
  waiting for transfers between devices  27.3 us (39%)
  starting transfers between devices  22.9 us (33%)
  Pallas kernels  16.5 us (24%)
  local copies, waits for them, and re-layouts  1.46 us (2%)
  between operations  0.84 us (1%)
    ppermute x12, waiting for transfers between devices, parts_of_sum(): lax.ppermute(term, axis, [(i, i ^ mask) for i in range(size)])  17 us
    pallas_call x16, Pallas kernels, call(): pl.pallas_call(kernel, out_shape=[jax.ShapeDtypeStruct(shape, F32) for sh...  16.5 us
    ppermute x12, starting transfers between devices, passed_along(): return lax.ppermute(block, axis, [(i, (i + 1) % size) for i in range(size)])  12.1 us
    ppermute x12, starting transfers between devices, parts_of_sum(): lax.ppermute(term, axis, [(i, i ^ mask) for i in range(size)])  10.8 us
    ppermute x12, waiting for transfers between devices, passed_along(): return lax.ppermute(block, axis, [(i, (i + 1) % size) for i in range(size)])  10.3 us
  transfers between devices with their start and end apart: 24, of which 16 were waited for; matrix products, arithmetic and copies ran while one was open for 1% of the time, Pallas kernels for 20%

profile of v2, /device:TPU:0, one launch (start us, length us, event | category | flops | bytes accessed | tf_op | source)
XLA Modules:
  0.0 69.7 jit_solution(5402786434526142121)
XLA Ops:
  0.6 1.2 %copy-done = f32[1024,256]{1,0:T(8,128)S(1)} copy-done((f32[1024,256]{1,0:T(8,128)S(1)}, f32[1024,256]{1,0:T(8,128)}, u32[]{:S(2)}) %copy-start) | copy-done | bytes 1048600
  1.9 0.4 gram.1
  2.2 3.1 %collective-permute-start.5 = (f32[576,256]{1,0:T(8,128)S(1)}, f32[576,256]{1,0:T(8,128)S(1)}, u32[]{:S(2)}, u32[]{:S(2)}) collective-permute-start(f32[576,256]{1,0:T(8,128)S(1)} %get-tuple-element.31), channel_id=1, source_target_pairs={{0,8},{8,16},{16,24},{24,0},{1,9},{9,17},{17,25},{25,1},{2,10},{10... | collective-permute-start | bytes 1769480 | tf_op jit(solution)/shard_map/ppermute | solution.py:253
  5.3 1.3 %collective-permute-done = f32[136,128]{1,0:T(8,128)S(1)} collective-permute-done((f32[136,128]{1,0:T(8,128)S(1)}, f32[136,128]{1,0:T(8,128)S(1)}, u32[]{:S(2)}, u32[]{:S(2)}) %collective-permute-start) | collective-permute-done | bytes 69664 | tf_op jit(solution)/shard_map/ppermute | solution.py:264
  6.6 2.5 %collective-permute-start.3 = (f32[136,128]{1,0:T(8,128)S(1)}, f32[136,128]{1,0:T(8,128)S(1)}, u32[]{:S(2)}, u32[]{:S(2)}) collective-permute-start(f32[136,128]{1,0:T(8,128)S(1)} %add.15.refs_0_), channel_id=1, source_target_pairs={{0,6},{1,7},{2,4},{3,5},{4,2},{5,3},{6,0},{7,1},{8,14},{9,15},{10,... | collective-permute-start | bytes 208904 | tf_op jit(solution)/shard_map/ppermute | solution.py:264
  9.1 0.5 collective-permute-start.2
  9.6 0.5 collective-permute-start.1
  10.3 1.6 %collective-permute-done.3.refs_3_ = f32[136,128]{1,0:T(8,128)S(1)} collective-permute-done((f32[136,128]{1,0:T(8,128)S(1)}, f32[136,128]{1,0:T(8,128)S(1)}, u32[]{:S(2)}, u32[]{:S(2)}) %collective-permute-start.3) | collective-permute-done | bytes 69664 | tf_op jit(solution)/shard_map/ppermute | solution.py:264
  11.9 1.5 %collective-permute-done.2.refs_2_ = f32[136,128]{1,0:T(8,128)S(1)} collective-permute-done((f32[136,128]{1,0:T(8,128)S(1)}, f32[136,128]{1,0:T(8,128)S(1)}, u32[]{:S(2)}, u32[]{:S(2)}) %collective-permute-start.2) | collective-permute-done | bytes 69664 | tf_op jit(solution)/shard_map/ppermute | solution.py:264
  13.4 0.5 collective-permute-done.1.refs_1_
  14.0 0.1 ratio.3.s_ref
  14.1 1.6 %collective-permute-start.4 = (f32[136,128]{1,0:T(8,128)S(1)}, f32[136,128]{1,0:T(8,128)S(1)}, u32[]{:S(2)}, u32[]{:S(2)}) collective-permute-start(f32[136,128]{1,0:T(8,128)S(1)} %ratio.3.s_ref), channel_id=1, source_target_pairs={{0,8},{8,16},{16,24},{24,0},{1,9},{9,17},{17,25},{25,1},{2,10},{10... | collective-permute-start | bytes 208904 | tf_op jit(solution)/shard_map/ppermute | solution.py:253
  15.7 2.2 %own.3 = (f32[1024,128]{1,0:T(8,128)S(1)}, f32[448,128]{1,0:T(8,128)S(1)}, f32[192,128]{1,0:T(8,128)S(1)}) custom-call(f32[136,128]{1,0:T(8,128)S(1)} %ratio.3.s_ref, f32[1024,256]{1,0:T(8,128)S(1)} %copy-done.1), custom_call_target="tpu_custom_call" | custom-call | flops 1000000000 | bytes 3500001 | tf_op jit(solution)/shard_map/own/pallas_call | solution.py:239
  18.0 1.6 %collective-permute-start.6 = (f32[448,128]{1,0:T(8,128)S(1)}, f32[448,128]{1,0:T(8,128)S(1)}, u32[]{:S(2)}, u32[]{:S(2)}) collective-permute-start(f32[448,128]{1,0:T(8,128)S(1)} %get-tuple-element.33), channel_id=1, source_target_pairs={{0,8},{8,16},{16,24},{24,0},{1,9},{9,17},{17,25},{25,1},{2,10},{10... | collective-permute-start | bytes 688136 | tf_op jit(solution)/shard_map/ppermute | solution.py:253
  19.6 3.4 %collective-permute-done.4.s_ref = f32[136,128]{1,0:T(8,128)S(1)} collective-permute-done((f32[136,128]{1,0:T(8,128)S(1)}, f32[136,128]{1,0:T(8,128)S(1)}, u32[]{:S(2)}, u32[]{:S(2)}) %collective-permute-start.4) | collective-permute-done | bytes 69664 | tf_op jit(solution)/shard_map/ppermute | solution.py:253
  23.0 1.4 %inverse.3.inner_ref = f32[128,128]{1,0:T(8,128)S(1)} custom-call(f32[136,128]{1,0:T(8,128)S(1)} %collective-permute-done.4.s_ref), custom_call_target="tpu_custom_call" | custom-call | flops 2000000000 | bytes 7000001 | tf_op jit(solution)/shard_map/inverse/pallas_call | solution.py:239
  24.4 0.6 turn.3
  25.0 2.1 %collective-permute-done.6.tail_ref = f32[448,128]{1,0:T(8,128)S(1)} collective-permute-done((f32[448,128]{1,0:T(8,128)S(1)}, f32[448,128]{1,0:T(8,128)S(1)}, u32[]{:S(2)}, u32[]{:S(2)}) %collective-permute-start.6) | collective-permute-done | bytes 229408 | tf_op jit(solution)/shard_map/ppermute | solution.py:253
  27.1 0.5 join.3
  27.7 1.2 %collective-permute-done.7 = f32[136,128]{1,0:T(8,128)S(1)} collective-permute-done((f32[136,128]{1,0:T(8,128)S(1)}, f32[136,128]{1,0:T(8,128)S(1)}, u32[]{:S(2)}, u32[]{:S(2)}) %collective-permute-start.7) | collective-permute-done | bytes 69664 | tf_op jit(solution)/shard_map/ppermute | solution.py:264
  28.9 2.5 %collective-permute-start.10 = (f32[136,128]{1,0:T(8,128)S(1)}, f32[136,128]{1,0:T(8,128)S(1)}, u32[]{:S(2)}, u32[]{:S(2)}) collective-permute-start(f32[136,128]{1,0:T(8,128)S(1)} %add.16.refs_0_), channel_id=1, source_target_pairs={{0,6},{1,7},{2,4},{3,5},{4,2},{5,3},{6,0},{7,1},{8,14},{9,15},{10,... | collective-permute-start | bytes 208904 | tf_op jit(solution)/shard_map/ppermute | solution.py:264
  31.4 0.5 collective-permute-start.9
  31.9 0.5 collective-permute-start.8
  32.5 1.6 %collective-permute-done.10.refs_3_ = f32[136,128]{1,0:T(8,128)S(1)} collective-permute-done((f32[136,128]{1,0:T(8,128)S(1)}, f32[136,128]{1,0:T(8,128)S(1)}, u32[]{:S(2)}, u32[]{:S(2)}) %collective-permute-start.10) | collective-permute-done | bytes 69664 | tf_op jit(solution)/shard_map/ppermute | solution.py:264
  34.2 1.5 %collective-permute-done.9.refs_2_ = f32[136,128]{1,0:T(8,128)S(1)} collective-permute-done((f32[136,128]{1,0:T(8,128)S(1)}, f32[136,128]{1,0:T(8,128)S(1)}, u32[]{:S(2)}, u32[]{:S(2)}) %collective-permute-start.9) | collective-permute-done | bytes 69664 | tf_op jit(solution)/shard_map/ppermute | solution.py:264
  35.7 0.5 collective-permute-done.8.refs_1_
  36.3 0.2 collective-permute-start.11
  36.5 2.3 %own.4 = (f32[1024,128]{1,0:T(8,128)S(1)}, f32[256,128]{1,0:T(8,128)S(1)}, f32[128,128]{1,0:T(8,128)S(1)}) custom-call(f32[136,128]{1,0:T(8,128)S(1)} %ratio.4.s_ref, f32[1024,256]{1,0:T(8,128)S(1)} %get-tuple-element.35.pair_ref), custom_call_target="tpu_custom_call" | custom-call | flops 1000000000 | bytes 3500001 | tf_op jit(solution)/shard_map/own/pallas_call | solution.py:239
  38.7 1.6 %collective-permute-start.14 = (f32[256,128]{1,0:T(8,128)S(1)}, f32[256,128]{1,0:T(8,128)S(1)}, u32[]{:S(2)}, u32[]{:S(2)}) collective-permute-start(f32[256,128]{1,0:T(8,128)S(1)} %get-tuple-element.42), channel_id=1, source_target_pairs={{0,8},{8,16},{16,24},{24,0},{1,9},{9,17},{17,25},{25,1},{2,10},{10... | collective-permute-start | bytes 393224 | tf_op jit(solution)/shard_map/ppermute | solution.py:253
  40.4 4.6 %collective-permute-done.11.s_ref = f32[136,128]{1,0:T(8,128)S(1)} collective-permute-done((f32[136,128]{1,0:T(8,128)S(1)}, f32[136,128]{1,0:T(8,128)S(1)}, u32[]{:S(2)}, u32[]{:S(2)}) %collective-permute-start.11) | collective-permute-done | bytes 69664 | tf_op jit(solution)/shard_map/ppermute | solution.py:253
  45.0 1.4 %inverse.4.inner_ref = f32[128,128]{1,0:T(8,128)S(1)} custom-call(f32[136,128]{1,0:T(8,128)S(1)} %collective-permute-done.11.s_ref), custom_call_target="tpu_custom_call" | custom-call | flops 2000000000 | bytes 7000001 | tf_op jit(solution)/shard_map/inverse/pallas_call | solution.py:239
  46.4 0.7 %turn.4 = (f32[768,128]{1,0:T(8,128)S(1)}, f32[768,128]{1,0:T(8,128)S(1)}) custom-call(f32[136,128]{1,0:T(8,128)S(1)} %collective-permute-done.11.s_ref, f32[128,128]{1,0:T(8,128)S(1)} %inverse.4.inner_ref, f32[576,128]{1,0:T(8,128)S(1)} %get-tuple-element.37.refs_0_, f32[768,128]{1,0:T(8,128)S(1)} %collective-permute-done.12.refs_1_, ...), custom_call_target="tpu_custom_call" | custom-call | flops 1000000000 | bytes 3500001 | tf_op jit(solution)/shard_map/turn/pallas_call | solution.py:239
  47.1 0.2 collective-permute-done.14.tail_ref
  47.3 0.8 %join.4 = (f32[1024,256]{1,0:T(8,128)S(1)}, f32[264,128]{1,0:T(8,128)S(1)}, f32[896,128]{1,0:T(8,128)S(1)}) custom-call(f32[1024,128]{1,0:T(8,128)S(1)} %get-tuple-element.36.staying_ref, f32[768,128]{1,0:T(8,128)S(1)} %get-tuple-element.41.moving_ref, f32[256,128]{1,0:T(8,128)S(1)} %collective-permute-done.14.tail_ref), custom_call_target="tpu_custom_call" | custom-call | flops 500000000 | bytes 1750001 | tf_op jit(solution)/shard_map/join/pallas_call | solution.py:239
  48.2 1.3 %collective-permute-done.15 = f32[264,128]{1,0:T(8,128)S(1)} collective-permute-done((f32[264,128]{1,0:T(8,128)S(1)}, f32[264,128]{1,0:T(8,128)S(1)}, u32[]{:S(2)}, u32[]{:S(2)}) %collective-permute-start.15) | collective-permute-done | bytes 135200 | tf_op jit(solution)/shard_map/ppermute | solution.py:264
  49.5 2.5 %collective-permute-start.18 = (f32[264,128]{1,0:T(8,128)S(1)}, f32[264,128]{1,0:T(8,128)S(1)}, u32[]{:S(2)}, u32[]{:S(2)}) collective-permute-start(f32[264,128]{1,0:T(8,128)S(1)} %add.17.refs_0_), channel_id=1, source_target_pairs={{0,6},{1,7},{2,4},{3,5},{4,2},{5,3},{6,0},{7,1},{8,14},{9,15},{10,... | collective-permute-start | bytes 405512 | tf_op jit(solution)/shard_map/ppermute | solution.py:264
  52.0 0.5 collective-permute-start.17
  52.6 0.5 collective-permute-start.16
  53.1 3.4 %collective-permute-done.18.refs_3_ = f32[264,128]{1,0:T(8,128)S(1)} collective-permute-done((f32[264,128]{1,0:T(8,128)S(1)}, f32[264,128]{1,0:T(8,128)S(1)}, u32[]{:S(2)}, u32[]{:S(2)}) %collective-permute-start.18) | collective-permute-done | bytes 135200 | tf_op jit(solution)/shard_map/ppermute | solution.py:264
  56.5 2.5 %collective-permute-done.17.refs_2_ = f32[264,128]{1,0:T(8,128)S(1)} collective-permute-done((f32[264,128]{1,0:T(8,128)S(1)}, f32[264,128]{1,0:T(8,128)S(1)}, u32[]{:S(2)}, u32[]{:S(2)}) %collective-permute-start.17) | collective-permute-done | bytes 135200 | tf_op jit(solution)/shard_map/ppermute | solution.py:264
  59.1 0.1 ratio.5
  59.3 2.7 %own.5 = (f32[1024,128]{1,0:T(8,128)S(1)}, f32[128,128]{1,0:T(8,128)S(1)}, f32[8,128]{1,0:T(8,128)S(1)}) custom-call(f32[136,128]{1,0:T(8,128)S(1)} %get-tuple-element.44.s_ref, f32[1024,256]{1,0:T(8,128)S(1)} %get-tuple-element.45.pair_ref, f32[264,128]{1,0:T(8,128)S(1)} %get-tuple-element.46.refs_0_), custom_call_target="tpu_custom_call" | custom-call | flops 1 | bytes 1 | tf_op jit(solution)/shard_map/own/pallas_call | solution.py:239
  62.0 0.1 collective-permute-start.22
  62.2 3.6 %collective-permute-start.23 = (f32[128,128]{1,0:T(8,128)S(1)}, f32[128,128]{1,0:T(8,128)S(1)}, u32[]{:S(2)}, u32[]{:S(2)}) collective-permute-start(f32[128,128]{1,0:T(8,128)S(1)} %get-tuple-element.54), channel_id=1, source_target_pairs={{0,8},{8,16},{16,24},{24,0},{1,9},{9,17},{17,25},{25,1},{2,10},{10... | collective-permute-start | bytes 196616 | tf_op jit(solution)/shard_map/ppermute | solution.py:253
  65.8 1.4 %inverse.5.inner_ref = f32[128,128]{1,0:T(8,128)S(1)} custom-call(f32[136,128]{1,0:T(8,128)S(1)} %collective-permute-done.19.s_ref), custom_call_target="tpu_custom_call" | custom-call | flops 1 | bytes 1 | tf_op jit(solution)/shard_map/inverse/pallas_call | solution.py:239
  67.2 0.8 %turn.5.moving_ref = f32[896,128]{1,0:T(8,128)S(1)} custom-call(f32[136,128]{1,0:T(8,128)S(1)} %collective-permute-done.19.s_ref, f32[128,128]{1,0:T(8,128)S(1)} %inverse.5.inner_ref, f32[768,128]{1,0:T(8,128)S(1)} %get-tuple-element.48.refs_0_, f32[896,128]{1,0:T(8,128)S(1)} %collective-permute-done.20.refs_1_, f32[128,128]{1,0:T(8,128)S(1)} %collective-permute-done.21.refs_2_), custom_call_target="tpu_custom_call" | custom-call | flops 1 | bytes 1 | tf_op jit(solution)/shard_map/turn/pallas_call | solution.py:239
  68.0 0.6 fusion.2
  68.6 1.1 %join.5 = f32[1024,256]{1,0:T(8,128)} custom-call(f32[1024,128]{1,0:T(8,128)S(1)} %get-tuple-element.47.staying_ref, f32[896,128]{1,0:T(8,128)S(1)} %turn.5.moving_ref, f32[128,128]{1,0:T(8,128)S(1)} %collective-permute-done.23.tail_ref), custom_call_target="tpu_custom_call" | custom-call | flops 1 | bytes 1 | tf_op jit(solution)/shard_map/join/pallas_call | solution.py:239
  (32 shorter events, 1.0 us)
Async XLA Ops:
  0.6 1.2 %copy-start = (f32[1024,256]{1,0:T(8,128)S(1)}, f32[1024,256]{1,0:T(8,128)}, u32[]{:S(2)}) copy-start(f32[1024,256]{1,0:T(8,128)} %pair_ref.3) | copy-start | bytes 3145732
  1.9 13.9 %copy-start.1 = (f32[1024,256]{1,0:T(8,128)S(1)}, f32[1024,256]{1,0:T(8,128)}, u32[]{:S(2)}) copy-start(f32[1024,256]{1,0:T(8,128)} %pair_ref.3) | copy-start | bytes 3145732
  2.2 22.1 %collective-permute-start.5 = (f32[576,256]{1,0:T(8,128)S(1)}, f32[576,256]{1,0:T(8,128)S(1)}, u32[]{:S(2)}, u32[]{:S(2)}) collective-permute-start(f32[576,256]{1,0:T(8,128)S(1)} %get-tuple-element.31), channel_id=1, source_target_pairs={{0,8},{8,16},{16,24},{24,0},{1,9},{9,17},{17,25},{25,1},{2,10},{10... | collective-permute-start | bytes 1769480 | tf_op jit(solution)/shard_map/ppermute | solution.py:253
  5.3 4.8 %copy-start.2 = (s32[3,1]{0,1:T(1,128)S(1)}, s32[3,1]{0,1:T(1,128)}, u32[]{:S(2)}) copy-start(s32[3,1]{0,1:T(1,128)} %param.3) | copy-start | bytes 40
  5.3 1.3 %collective-permute-start = (f32[136,128]{1,0:T(8,128)S(1)}, f32[136,128]{1,0:T(8,128)S(1)}, u32[]{:S(2)}, u32[]{:S(2)}) collective-permute-start(f32[136,128]{1,0:T(8,128)S(1)} %get-tuple-element.29), channel_id=1, source_target_pairs={{0,1},{1,0},{2,3},{3,2},{4,5},{5,4},{6,7},{7,6},{8,9},{9,8},{10,11... | collective-permute-start | bytes 208904 | tf_op jit(solution)/shard_map/ppermute | solution.py:264
  6.6 5.3 %collective-permute-start.3 = (f32[136,128]{1,0:T(8,128)S(1)}, f32[136,128]{1,0:T(8,128)S(1)}, u32[]{:S(2)}, u32[]{:S(2)}) collective-permute-start(f32[136,128]{1,0:T(8,128)S(1)} %add.15.refs_0_), channel_id=1, source_target_pairs={{0,6},{1,7},{2,4},{3,5},{4,2},{5,3},{6,0},{7,1},{8,14},{9,15},{10,... | collective-permute-start | bytes 208904 | tf_op jit(solution)/shard_map/ppermute | solution.py:264
  9.1 4.3 %collective-permute-start.2 = (f32[136,128]{1,0:T(8,128)S(1)}, f32[136,128]{1,0:T(8,128)S(1)}, u32[]{:S(2)}, u32[]{:S(2)}) collective-permute-start(f32[136,128]{1,0:T(8,128)S(1)} %add.15.refs_0_), channel_id=1, source_target_pairs={{0,4},{1,5},{2,6},{3,7},{4,0},{5,1},{6,2},{7,3},{8,12},{9,13},{10,... | collective-permute-start | bytes 208904 | tf_op jit(solution)/shard_map/ppermute | solution.py:264
  9.6 4.3 %collective-permute-start.1 = (f32[136,128]{1,0:T(8,128)S(1)}, f32[136,128]{1,0:T(8,128)S(1)}, u32[]{:S(2)}, u32[]{:S(2)}) collective-permute-start(f32[136,128]{1,0:T(8,128)S(1)} %add.15.refs_0_), channel_id=1, source_target_pairs={{0,2},{1,3},{2,0},{3,1},{4,6},{5,7},{6,4},{7,5},{8,10},{9,11},{10,... | collective-permute-start | bytes 208904 | tf_op jit(solution)/shard_map/ppermute | solution.py:264
  14.1 8.9 %collective-permute-start.4 = (f32[136,128]{1,0:T(8,128)S(1)}, f32[136,128]{1,0:T(8,128)S(1)}, u32[]{:S(2)}, u32[]{:S(2)}) collective-permute-start(f32[136,128]{1,0:T(8,128)S(1)} %ratio.3.s_ref), channel_id=1, source_target_pairs={{0,8},{8,16},{16,24},{24,0},{1,9},{9,17},{17,25},{25,1},{2,10},{10... | collective-permute-start | bytes 208904 | tf_op jit(solution)/shard_map/ppermute | solution.py:253
  18.0 9.1 %collective-permute-start.6 = (f32[448,128]{1,0:T(8,128)S(1)}, f32[448,128]{1,0:T(8,128)S(1)}, u32[]{:S(2)}, u32[]{:S(2)}) collective-permute-start(f32[448,128]{1,0:T(8,128)S(1)} %get-tuple-element.33), channel_id=1, source_target_pairs={{0,8},{8,16},{16,24},{24,0},{1,9},{9,17},{17,25},{25,1},{2,10},{10... | collective-permute-start | bytes 688136 | tf_op jit(solution)/shard_map/ppermute | solution.py:253
  27.5 1.3 %collective-permute-start.7 = (f32[136,128]{1,0:T(8,128)S(1)}, f32[136,128]{1,0:T(8,128)S(1)}, u32[]{:S(2)}, u32[]{:S(2)}) collective-permute-start(f32[136,128]{1,0:T(8,128)S(1)} %get-tuple-element.34), channel_id=1, source_target_pairs={{0,1},{1,0},{2,3},{3,2},{4,5},{5,4},{6,7},{7,6},{8,9},{9,8},{10,11... | collective-permute-start | bytes 208904 | tf_op jit(solution)/shard_map/ppermute | solution.py:264
  27.6 18.8 %collective-permute-start.12 = (f32[768,128]{1,0:T(8,128)S(1)}, f32[768,128]{1,0:T(8,128)S(1)}, u32[]{:S(2)}, u32[]{:S(2)}) collective-permute-start(f32[768,128]{1,0:T(8,128)S(1)} %get-tuple-element.38), channel_id=1, source_target_pairs={{0,8},{8,16},{16,24},{24,0},{1,9},{9,17},{17,25},{25,1},{2,10},{10... | collective-permute-start | bytes 1179656 | tf_op jit(solution)/shard_map/ppermute | solution.py:253
  28.9 5.3 %collective-permute-start.10 = (f32[136,128]{1,0:T(8,128)S(1)}, f32[136,128]{1,0:T(8,128)S(1)}, u32[]{:S(2)}, u32[]{:S(2)}) collective-permute-start(f32[136,128]{1,0:T(8,128)S(1)} %add.16.refs_0_), channel_id=1, source_target_pairs={{0,6},{1,7},{2,4},{3,5},{4,2},{5,3},{6,0},{7,1},{8,14},{9,15},{10,... | collective-permute-start | bytes 208904 | tf_op jit(solution)/shard_map/ppermute | solution.py:264
  31.4 4.3 %collective-permute-start.9 = (f32[136,128]{1,0:T(8,128)S(1)}, f32[136,128]{1,0:T(8,128)S(1)}, u32[]{:S(2)}, u32[]{:S(2)}) collective-permute-start(f32[136,128]{1,0:T(8,128)S(1)} %add.16.refs_0_), channel_id=1, source_target_pairs={{0,4},{1,5},{2,6},{3,7},{4,0},{5,1},{6,2},{7,3},{8,12},{9,13},{10,... | collective-permute-start | bytes 208904 | tf_op jit(solution)/shard_map/ppermute | solution.py:264
  31.9 4.3 %collective-permute-start.8 = (f32[136,128]{1,0:T(8,128)S(1)}, f32[136,128]{1,0:T(8,128)S(1)}, u32[]{:S(2)}, u32[]{:S(2)}) collective-permute-start(f32[136,128]{1,0:T(8,128)S(1)} %add.16.refs_0_), channel_id=1, source_target_pairs={{0,2},{1,3},{2,0},{3,1},{4,6},{5,7},{6,4},{7,5},{8,10},{9,11},{10,... | collective-permute-start | bytes 208904 | tf_op jit(solution)/shard_map/ppermute | solution.py:264
  32.4 13.9 %collective-permute-start.13 = (f32[192,128]{1,0:T(8,128)S(1)}, f32[192,128]{1,0:T(8,128)S(1)}, u32[]{:S(2)}, u32[]{:S(2)}) collective-permute-start(f32[192,128]{1,0:T(8,128)S(1)} %get-tuple-element.40), channel_id=1, source_target_pairs={{0,8},{8,16},{16,24},{24,0},{1,9},{9,17},{17,25},{25,1},{2,10},{10... | collective-permute-start | bytes 294920 | tf_op jit(solution)/shard_map/ppermute | solution.py:253
  36.3 8.7 %collective-permute-start.11 = (f32[136,128]{1,0:T(8,128)S(1)}, f32[136,128]{1,0:T(8,128)S(1)}, u32[]{:S(2)}, u32[]{:S(2)}) collective-permute-start(f32[136,128]{1,0:T(8,128)S(1)} %ratio.4.s_ref), channel_id=1, source_target_pairs={{0,8},{8,16},{16,24},{24,0},{1,9},{9,17},{17,25},{25,1},{2,10},{10... | collective-permute-start | bytes 208904 | tf_op jit(solution)/shard_map/ppermute | solution.py:253
  38.7 8.6 %collective-permute-start.14 = (f32[256,128]{1,0:T(8,128)S(1)}, f32[256,128]{1,0:T(8,128)S(1)}, u32[]{:S(2)}, u32[]{:S(2)}) collective-permute-start(f32[256,128]{1,0:T(8,128)S(1)} %get-tuple-element.42), channel_id=1, source_target_pairs={{0,8},{8,16},{16,24},{24,0},{1,9},{9,17},{17,25},{25,1},{2,10},{10... | collective-permute-start | bytes 393224 | tf_op jit(solution)/shard_map/ppermute | solution.py:253
  48.1 1.4 %collective-permute-start.15 = (f32[264,128]{1,0:T(8,128)S(1)}, f32[264,128]{1,0:T(8,128)S(1)}, u32[]{:S(2)}, u32[]{:S(2)}) collective-permute-start(f32[264,128]{1,0:T(8,128)S(1)} %get-tuple-element.43), channel_id=1, source_target_pairs={{0,1},{1,0},{2,3},{3,2},{4,5},{5,4},{6,7},{7,6},{8,9},{9,8},{10,11... | collective-permute-start | bytes 405512 | tf_op jit(solution)/shard_map/ppermute | solution.py:264
  48.2 19.0 %collective-permute-start.20 = (f32[896,128]{1,0:T(8,128)S(1)}, f32[896,128]{1,0:T(8,128)S(1)}, u32[]{:S(2)}, u32[]{:S(2)}) collective-permute-start(f32[896,128]{1,0:T(8,128)S(1)} %get-tuple-element.49), channel_id=1, source_target_pairs={{0,8},{8,16},{16,24},{24,0},{1,9},{9,17},{17,25},{25,1},{2,10},{10... | collective-permute-start | bytes 1376264 | tf_op jit(solution)/shard_map/ppermute | solution.py:253
  49.5 7.0 %collective-permute-start.18 = (f32[264,128]{1,0:T(8,128)S(1)}, f32[264,128]{1,0:T(8,128)S(1)}, u32[]{:S(2)}, u32[]{:S(2)}) collective-permute-start(f32[264,128]{1,0:T(8,128)S(1)} %add.17.refs_0_), channel_id=1, source_target_pairs={{0,6},{1,7},{2,4},{3,5},{4,2},{5,3},{6,0},{7,1},{8,14},{9,15},{10,... | collective-permute-start | bytes 405512 | tf_op jit(solution)/shard_map/ppermute | solution.py:264
  52.0 7.0 %collective-permute-start.17 = (f32[264,128]{1,0:T(8,128)S(1)}, f32[264,128]{1,0:T(8,128)S(1)}, u32[]{:S(2)}, u32[]{:S(2)}) collective-permute-start(f32[264,128]{1,0:T(8,128)S(1)} %add.17.refs_0_), channel_id=1, source_target_pairs={{0,4},{1,5},{2,6},{3,7},{4,0},{5,1},{6,2},{7,3},{8,12},{9,13},{10,... | collective-permute-start | bytes 405512 | tf_op jit(solution)/shard_map/ppermute | solution.py:264
  52.6 6.6 %collective-permute-start.16 = (f32[264,128]{1,0:T(8,128)S(1)}, f32[264,128]{1,0:T(8,128)S(1)}, u32[]{:S(2)}, u32[]{:S(2)}) collective-permute-start(f32[264,128]{1,0:T(8,128)S(1)} %add.17.refs_0_), channel_id=1, source_target_pairs={{0,2},{1,3},{2,0},{3,1},{4,6},{5,7},{6,4},{7,5},{8,10},{9,11},{10,... | collective-permute-start | bytes 405512 | tf_op jit(solution)/shard_map/ppermute | solution.py:264
  53.1 14.1 %collective-permute-start.21 = (f32[128,128]{1,0:T(8,128)S(1)}, f32[128,128]{1,0:T(8,128)S(1)}, u32[]{:S(2)}, u32[]{:S(2)}) collective-permute-start(f32[128,128]{1,0:T(8,128)S(1)} %get-tuple-element.51), channel_id=1, source_target_pairs={{0,8},{8,16},{16,24},{24,0},{1,9},{9,17},{17,25},{25,1},{2,10},{10... | collective-permute-start | bytes 196616 | tf_op jit(solution)/shard_map/ppermute | solution.py:253
  59.3 6.5 %collective-permute-start.19 = (f32[136,128]{1,0:T(8,128)S(1)}, f32[136,128]{1,0:T(8,128)S(1)}, u32[]{:S(2)}, u32[]{:S(2)}) collective-permute-start(f32[136,128]{1,0:T(8,128)S(1)} %get-tuple-element.44.s_ref), channel_id=1, source_target_pairs={{0,8},{8,16},{16,24},{24,0},{1,9},{9,17},{17,25},{25,1},{2,10},{10... | collective-permute-start | bytes 208904 | tf_op jit(solution)/shard_map/ppermute | solution.py:253
  62.0 6.0 %collective-permute-start.22 = (f32[8,128]{1,0:T(8,128)S(1)}, f32[8,128]{1,0:T(8,128)S(1)}, u32[]{:S(2)}, u32[]{:S(2)}) collective-permute-start(f32[8,128]{1,0:T(8,128)S(1)} %get-tuple-element.52), channel_id=1, source_target_pairs={{0,8},{8,16},{16,24},{24,0},{1,9},{9,17},{17,25},{25,1},{2,10},{10... | collective-permute-start | bytes 12296 | tf_op jit(solution)/shard_map/ppermute | solution.py:253
  62.2 6.4 %collective-permute-start.23 = (f32[128,128]{1,0:T(8,128)S(1)}, f32[128,128]{1,0:T(8,128)S(1)}, u32[]{:S(2)}, u32[]{:S(2)}) collective-permute-start(f32[128,128]{1,0:T(8,128)S(1)} %get-tuple-element.54), channel_id=1, source_target_pairs={{0,8},{8,16},{16,24},{24,0},{1,9},{9,17},{17,25},{25,1},{2,10},{10... | collective-permute-start | bytes 196616 | tf_op jit(solution)/shard_map/ppermute | solution.py:253

commit v3 on v2

--- a/solution.py
+++ b/solution.py
@@ -7,7 +7,11 @@
 from jax.sharding import PartitionSpec as P
 
 epsilon = 1e-06
-MICROS = {"own": 1.0, "inverse": 2.0, "turn": 1.0, "join": 0.5}
+MICROS = (
+    {"own": 1.0, "turn": 4.0},
+    {"ratio": 2.0, "own": 0.5, "turn": 1.0, "join": 2.0},
+    {"ratio": 1.5, "own": 0.8, "turn": 1.0, "join": 0.5, "both": 2.0},
+)
 F32 = jnp.float32
 BF16 = jnp.bfloat16
 NN = (((1,), (0,)), ((), ()))
@@ -130,15 +134,15 @@
     return total_ref[...]
 
 
-def rotated_halves(skew, inner, first, second):
-    mixed = times(first + times(second, right(skew, True), True), right(inner))
+def rotated_halves(skew, first, second, error_ref, total_ref):
+    mixed = first + times(second, right(skew, True), True)
+    mixed = times(mixed, right(inverse(skew, error_ref, total_ref)))
     return 2.0 * mixed - first, second - 2.0 * times(mixed, right(skew))
 
 
-def gram_kernel(pair_ref, gram_ref, head_ref):
+def gram_kernel(pair_ref, gram_ref):
     width = pair_ref.shape[1] // 2
     gram_ref[...] = gram_of(pair_ref[:, :width], pair_ref[:, width:], gram_ref.shape[0] > width + 8)
-    head_ref[...] = pair_ref[: head_ref.shape[0]]
 
 
 def ratio_kernel(row, count, plan_ref, *refs):
@@ -161,7 +165,6 @@
     width = s_ref.shape[1]
     rows = pair_ref.shape[0]
     skew = s_ref[:width]
-    inner = inverse(skew, error_ref, total_ref)
     moves_second = s_ref[width : width + 1] > 0.5
     first, second = pair_ref[:, :width], pair_ref[:, width:]
     if last:
@@ -170,7 +173,7 @@
         left, right = whole_gram(gram_ref[...])
         first = jnp.concatenate([first, left, identity, zeros], axis=0)
         second = jnp.concatenate([second, right, zeros, identity], axis=0)
-    first, second = rotated_halves(skew, inner, first, second)
+    first, second = rotated_halves(skew, first, second, error_ref, total_ref)
     staying = jnp.where(moves_second, first, second)
     moving = jnp.where(moves_second, second, first)
     staying_ref, *outs = refs
@@ -180,25 +183,23 @@
             jnp.sum(half[rows : rows + 2 * width] * half[rows + 2 * width :], axis=0, keepdims=True)
             for half in (staying, moving)
         ]
-        outs[-1][...] = jnp.concatenate(energies + [jnp.zeros((6, width), F32)], axis=0)
-    if known < rows:
+        energies = jnp.concatenate(energies + [jnp.zeros((6, width), F32)], axis=0)
+        outs[-1][...] = energies
+        outs[0][...] = jnp.concatenate([moving[known:rows], energies], axis=0) if known < rows else energies
+    elif known < rows:
         outs[0][...] = moving[known:rows]
     if known < kept:
         outs[1 if known < rows else 0][...] = staying[known:kept]
 
 
-def inverse_kernel(s_ref, inner_ref, error_ref, total_ref):
-    inner_ref[...] = inverse(s_ref[: s_ref.shape[1]], error_ref, total_ref)
-
-
-def turned(s_ref, inner_ref, refs):
+def turned(s_ref, refs, error_ref, total_ref):
     width = s_ref.shape[1]
     if len(refs) == 1:
         first, second = refs[0][:, :width], refs[0][:, width:]
     else:
         second = refs[1][...]
         first = jnp.concatenate([refs[0][...]] + [ref[...] for ref in refs[2:]], axis=0)
-    first, second = rotated_halves(s_ref[:width], inner_ref[...], first, second)
+    first, second = rotated_halves(s_ref[:width], first, second, error_ref, total_ref)
     moves_second = s_ref[width : width + 1] > 0.5
     return jnp.where(moves_second, second, first), jnp.where(moves_second, first, second)
 
@@ -211,31 +212,49 @@
         ref[...] = gram_of(staying, moving, ref.shape[0] > width + 8)
 
 
-def turn_kernel(parts, s_ref, inner_ref, *refs):
-    moving, staying = turned(s_ref, inner_ref, refs[:parts])
+def turn_kernel(parts, s_ref, *refs):
+    *refs, error_ref, total_ref = refs
+    moving, staying = turned(s_ref, refs[:parts], error_ref, total_ref)
     refs[parts][...] = moving
     if len(refs) > parts + 1:
         refs[parts + 1][...] = staying[: refs[parts + 1].shape[0]]
 
 
-def join_kernel(kept, staying_ref, moving_ref, tail_ref, pair_ref, *outs):
-    moving = jnp.concatenate([moving_ref[...], tail_ref[...]], axis=0)
-    joined(staying_ref[...], moving, pair_ref, *outs[:1])
+def column_rms(total_rows, own, passed, rms_ref):
+    energy = jnp.concatenate([own[:1], passed[1:2]], axis=1)
+    rms_ref[...] = jnp.sqrt(jnp.maximum(energy, 0.0) / total_rows + epsilon)
+
+
+def join_kernel(kept, total_rows, staying_ref, moving_ref, tail_ref, *refs):
+    rows = staying_ref.shape[0]
+    known = moving_ref.shape[0]
+    moving = jnp.concatenate([moving_ref[...], tail_ref[: rows - known]], axis=0)
     if kept:
-        outs[1][...] = moving[:kept]
-
-
-def turn_join_kernel(kept, parts, s_ref, inner_ref, staying_ref, *refs):
-    moving, neighbour_staying = turned(s_ref, inner_ref, refs[:parts])
-    pair_ref, *outs = refs[parts:]
+        pair_ref, gram_ref, moving_out_ref = refs
+        joined(staying_ref[...], moving, pair_ref, gram_ref)
+        moving_out_ref[...] = moving[:kept]
+    else:
+        energies_ref, pair_ref, rms_ref = refs
+        joined(staying_ref[...], moving, pair_ref)
+        column_rms(total_rows, energies_ref[...], tail_ref[rows - known :], rms_ref)
+
+
+def turn_join_kernel(kept, total_rows, parts, s_ref, *refs):
+    *refs, error_ref, total_ref = refs
+    moving, neighbour_staying = turned(s_ref, refs[:parts], error_ref, total_ref)
+    staying_ref, *refs = refs[parts:]
+    if not kept:
+        column_rms(total_rows, refs[0][...], refs[1][...], refs[-1])
+        refs = refs[2:-1]
+    pair_ref, *outs = refs
     joined(staying_ref[...], moving, pair_ref, *outs[:1])
     if kept:
         outs[1][...] = moving[:kept]
         outs[2][...] = neighbour_staying[: outs[2].shape[0]]
 
 
-def call(kernel, operands, outs, scratch=(), name="", last=False):
-    micros = 0.0 if last else MICROS.get(name, 0.0)
+def call(kernel, operands, outs, scratch=(), name="", place=0):
+    micros = MICROS[place].get(name, 0.0)
     return pl.pallas_call(
         kernel,
         out_shape=[jax.ShapeDtypeStruct(shape, F32) for shape in outs],
@@ -280,42 +299,37 @@
     scratch = [pltpu.VMEM(square, F32)] * 2
     heads = known_rows(rows, rounds)
     pair = record
-    terms, raw_head = call(gram_kernel, [pair], [grams[0], (heads[0], 2 * width)], name="gram")
-    neighbour = [passed_along(raw_head, "col")]
+    neighbour = [passed_along(record[: heads[0]], "col")]
+    (terms,) = call(gram_kernel, [pair], [grams[0]], name="gram")
     plan_rows = jnp.repeat(jnp.broadcast_to(plan.astype(F32), (rounds, width)), 8, axis=0)
     for step in range(rounds):
         known, kept, last = heads[step], heads[step + 1], step + 1 == rounds
+        place = 2 if last else min(step, 1)
         parts = parts_of_sum(terms, "tm")
         kernel = functools.partial(ratio_kernel, 8 * step, len(parts))
-        ratio, *gram = call(kernel, [plan_rows] + parts, [ratios] + [grams[step]] * last, name="ratio", last=last)
+        ratio, *gram = call(kernel, [plan_rows] + parts, [ratios] + [grams[step]] * last, name="ratio", place=place)
         neighbour_ratio = passed_along(ratio, "col")
-        outs = [(rows, width)] + [(rows - known, width)] * (known < rows) + [(kept - known, width)] * (known < kept)
+        sent_rows = rows - known + 8 * last
+        outs = [(rows, width)] + [(sent_rows, width)] * (sent_rows > 0) + [(kept - known, width)] * (known < kept)
         kernel = functools.partial(own_kernel, known, kept, last)
-        staying, *sent = call(kernel, [ratio, pair] + gram, outs + [(8, width)] * last, scratch, name="own", last=last)
-        (inner,) = call(inverse_kernel, [neighbour_ratio], [square], scratch, name="inverse", last=last)
-        turn = [neighbour_ratio, inner]
-        sums = [] if last else [grams[step + 1]]
-        kept_outs = [(kept, width)] * (kept > 0)
-        known_outs = [(min(known, kept), width)] * (kept > 0)
+        staying, *sent = call(kernel, [ratio, pair] + gram, outs + [(8, width)] * last, scratch, name="own", place=place)
+        tail = passed_along(sent[0], "col") if sent_rows else None
+        outs = [record.shape] + ([(1, 2 * width)] if last else [grams[step + 1], (kept, width)])
+        known_outs = [(min(known, kept), width)] * (not last)
         if known < rows:
-            tail = passed_along(sent[0], "col")
             kernel = functools.partial(turn_kernel, len(neighbour))
-            moving, *kept_staying = call(kernel, turn + neighbour, [(known, width)] + known_outs, name="turn", last=last)
-            if last:
-                passed = passed_along(sent[-1], "col")
-                moving, passed = lax.optimization_barrier((moving, passed))
-            kernel = functools.partial(join_kernel, kept)
-            pair, *rest = call(kernel, [staying, moving, tail], [record.shape] + sums + kept_outs, name="join", last=last)
+            moving, *kept_staying = call(
+                kernel, [neighbour_ratio] + neighbour, [(known, width)] + known_outs, scratch, name="turn", place=place
+            )
+            kernel = functools.partial(join_kernel, kept, total_rows)
+            pair, *rest = call(kernel, [staying, moving, tail] + [sent[-1]] * last, outs, name="join", place=place)
         else:
-            tail = None
-            if last:
-                passed = passed_along(sent[-1], "col")
-            kernel = functools.partial(turn_join_kernel, kept, len(neighbour))
-            pair, *rest = call(kernel, turn + [staying] + neighbour, [record.shape] + sums + kept_outs + known_outs, name="both", last=last)
+            kernel = functools.partial(turn_join_kernel, kept, total_rows, len(neighbour))
+            operands = [neighbour_ratio] + neighbour + [staying] + ([sent[-1], tail] if last else [])
+            pair, *rest = call(kernel, operands, outs + known_outs, scratch, name="both", place=place)
             rest, kept_staying = rest[:2], rest[2:]
         if last:
-            energy = jnp.concatenate([sent[-1][0], passed[1]])
-            return (pair, jnp.sqrt(jnp.maximum(energy, 0.0) / total_rows + epsilon))
+            return (pair, rest[0].reshape(2 * width))
         terms, moving = rest
         neighbour = kept_staying + [passed_along(moving, "col")]
         if known < kept:

time: 69.8 us -> 68.5 us (0.981)
  waiting for transfers between devices: 27.3 us -> 31.9 us
  starting transfers between devices: 22.9 us -> 19.3 us
  Pallas kernels: 16.5 us -> 14.9 us
    ppermute x12 -> x11, waiting for transfers between devices: 10.3 us -> 14.9 us  [passed_along(): return lax.ppermute(block, axis, [(i, (i + 1) % size) for i in range(size)])]
    ppermute x12 -> x11, starting transfers between devices: 12.1 us -> 8.45 us  [passed_along(): return lax.ppermute(block, axis, [(i, (i + 1) % size) for i in range(size)])]
    pallas_call x16 -> x13, Pallas kernels: 16.5 us -> 14.9 us  [call(): pl.pallas_call(kernel, out_shape=[jax.ShapeDtypeStruct(shape, F32) for sh...]
    unnamed x6 -> x4, local copies, waits for them, and re-layouts: 1.23 us -> 0.01 us
    slice x0 -> x1, local copies, waits for them, and re-layouts: none -> 1.19 us  [body(): neighbour = [passed_along(record[:heads[0]], 'col')]]
  transfers between devices with their start and end apart: 24 -> 23, of which waited for: 16 -> 19; matrix products, arithmetic and copies ran while one was open for 1% -> 0% of each run, Pallas kernels for 20% -> 19%
where the time goes in v3:
time: 68.5 us; the launch traced here: 68.4 us
  waiting for transfers between devices  31.9 us (47%)
  starting transfers between devices  19.3 us (28%)
  Pallas kernels  14.9 us (22%)
  local copies, waits for them, and re-layouts  1.43 us (2%)
  between operations  0.79 us (1%)
    ppermute x12, waiting for transfers between devices, parts_of_sum(): lax.ppermute(term, axis, [(i, i ^ mask) for i in range(size)])  17 us
    ppermute x11, waiting for transfers between devices, passed_along(): return lax.ppermute(block, axis, [(i, (i + 1) % size) for i in range(size)])  14.9 us
    pallas_call x13, Pallas kernels, call(): pl.pallas_call(kernel, out_shape=[jax.ShapeDtypeStruct(shape, F32) for sh...  14.9 us
    ppermute x12, starting transfers between devices, parts_of_sum(): lax.ppermute(term, axis, [(i, i ^ mask) for i in range(size)])  10.9 us
    ppermute x11, starting transfers between devices, passed_along(): return lax.ppermute(block, axis, [(i, (i + 1) % size) for i in range(size)])  8.45 us
  transfers between devices with their start and end apart: 23, of which 19 were waited for; matrix products, arithmetic and copies ran while one was open for 0% of the time, Pallas kernels for 19%

profile of v3, /device:TPU:0, one launch (start us, length us, event | category | flops | bytes accessed | tf_op | source)
XLA Modules:
  0.0 68.4 jit_solution(10974555371119016893)
XLA Ops:
  0.6 1.2 %slice.3 = f32[576,256]{1,0:T(8,128)S(1)} slice(f32[1024,256]{1,0:T(8,128)} %pair_ref.3), slice={[0:576], [0:256]} | slice | bytes 1179648 | tf_op jit(solution)/shard_map/slice | solution.py:302
  1.8 3.1 %collective-permute-start.5 = (f32[576,256]{1,0:T(8,128)S(1)}, f32[576,256]{1,0:T(8,128)S(1)}, u32[]{:S(2)}, u32[]{:S(2)}) collective-permute-start(f32[576,256]{1,0:T(8,128)S(1)} %slice.3), channel_id=1, source_target_pairs={{0,8},{8,16},{16,24},{24,0},{1,9},{9,17},{17,25},{25,1},{2,10},{10... | collective-permute-start | bytes 1769480 | tf_op jit(solution)/shard_map/ppermute | solution.py:272
  4.9 0.4 gram.1
  5.4 1.2 %collective-permute-done = f32[136,128]{1,0:T(8,128)S(1)} collective-permute-done((f32[136,128]{1,0:T(8,128)S(1)}, f32[136,128]{1,0:T(8,128)S(1)}, u32[]{:S(2)}, u32[]{:S(2)}) %collective-permute-start) | collective-permute-done | bytes 69664 | tf_op jit(solution)/shard_map/ppermute | solution.py:283
  6.6 2.5 %collective-permute-start.3 = (f32[136,128]{1,0:T(8,128)S(1)}, f32[136,128]{1,0:T(8,128)S(1)}, u32[]{:S(2)}, u32[]{:S(2)}) collective-permute-start(f32[136,128]{1,0:T(8,128)S(1)} %add.9.refs_0_), channel_id=1, source_target_pairs={{0,6},{1,7},{2,4},{3,5},{4,2},{5,3},{6,0},{7,1},{8,14},{9,15},{10,... | collective-permute-start | bytes 208904 | tf_op jit(solution)/shard_map/ppermute | solution.py:283
  9.2 0.5 collective-permute-start.2
  9.7 0.5 collective-permute-start.1
  10.4 1.6 %collective-permute-done.3.refs_3_ = f32[136,128]{1,0:T(8,128)S(1)} collective-permute-done((f32[136,128]{1,0:T(8,128)S(1)}, f32[136,128]{1,0:T(8,128)S(1)}, u32[]{:S(2)}, u32[]{:S(2)}) %collective-permute-start.3) | collective-permute-done | bytes 69664 | tf_op jit(solution)/shard_map/ppermute | solution.py:283
  11.9 1.5 %collective-permute-done.2.refs_2_ = f32[136,128]{1,0:T(8,128)S(1)} collective-permute-done((f32[136,128]{1,0:T(8,128)S(1)}, f32[136,128]{1,0:T(8,128)S(1)}, u32[]{:S(2)}, u32[]{:S(2)}) %collective-permute-start.2) | collective-permute-done | bytes 69664 | tf_op jit(solution)/shard_map/ppermute | solution.py:283
  13.5 0.5 collective-permute-done.1.refs_1_
  14.0 0.1 ratio.3.s_ref
  14.2 1.6 %collective-permute-start.4 = (f32[136,128]{1,0:T(8,128)S(1)}, f32[136,128]{1,0:T(8,128)S(1)}, u32[]{:S(2)}, u32[]{:S(2)}) collective-permute-start(f32[136,128]{1,0:T(8,128)S(1)} %ratio.3.s_ref), channel_id=1, source_target_pairs={{0,8},{8,16},{16,24},{24,0},{1,9},{9,17},{17,25},{25,1},{2,10},{10... | collective-permute-start | bytes 208904 | tf_op jit(solution)/shard_map/ppermute | solution.py:272
  15.8 2.0 %own.3 = (f32[1024,128]{1,0:T(8,128)S(1)}, f32[448,128]{1,0:T(8,128)S(1)}, f32[192,128]{1,0:T(8,128)S(1)}) custom-call(f32[136,128]{1,0:T(8,128)S(1)} %ratio.3.s_ref, f32[1024,256]{1,0:T(8,128)S(1)} %copy-done), custom_call_target="tpu_custom_call" | custom-call | flops 1000000000 | bytes 3500001 | tf_op jit(solution)/shard_map/own/pallas_call | solution.py:258
  17.8 1.6 %collective-permute-start.6 = (f32[448,128]{1,0:T(8,128)S(1)}, f32[448,128]{1,0:T(8,128)S(1)}, u32[]{:S(2)}, u32[]{:S(2)}) collective-permute-start(f32[448,128]{1,0:T(8,128)S(1)} %get-tuple-element.29), channel_id=1, source_target_pairs={{0,8},{8,16},{16,24},{24,0},{1,9},{9,17},{17,25},{25,1},{2,10},{10... | collective-permute-start | bytes 688136 | tf_op jit(solution)/shard_map/ppermute | solution.py:272
  19.4 3.2 %collective-permute-done.4.s_ref = f32[136,128]{1,0:T(8,128)S(1)} collective-permute-done((f32[136,128]{1,0:T(8,128)S(1)}, f32[136,128]{1,0:T(8,128)S(1)}, u32[]{:S(2)}, u32[]{:S(2)}) %collective-permute-start.4) | collective-permute-done | bytes 69664 | tf_op jit(solution)/shard_map/ppermute | solution.py:272
  22.6 1.8 %turn.3 = (f32[576,128]{1,0:T(8,128)S(1)}, f32[576,128]{1,0:T(8,128)S(1)}) custom-call(f32[136,128]{1,0:T(8,128)S(1)} %collective-permute-done.4.s_ref, f32[576,256]{1,0:T(8,128)S(1)} %collective-permute-done.5.refs_0_), custom_call_target="tpu_custom_call" | custom-call | flops 4000000000 | bytes 14000001 | tf_op jit(solution)/shard_map/turn/pallas_call | solution.py:258
  24.4 2.2 %collective-permute-done.6.tail_ref = f32[448,128]{1,0:T(8,128)S(1)} collective-permute-done((f32[448,128]{1,0:T(8,128)S(1)}, f32[448,128]{1,0:T(8,128)S(1)}, u32[]{:S(2)}, u32[]{:S(2)}) %collective-permute-start.6) | collective-permute-done | bytes 229408 | tf_op jit(solution)/shard_map/ppermute | solution.py:272
  26.7 0.4 join.3
  27.3 1.2 %collective-permute-done.7 = f32[136,128]{1,0:T(8,128)S(1)} collective-permute-done((f32[136,128]{1,0:T(8,128)S(1)}, f32[136,128]{1,0:T(8,128)S(1)}, u32[]{:S(2)}, u32[]{:S(2)}) %collective-permute-start.7) | collective-permute-done | bytes 69664 | tf_op jit(solution)/shard_map/ppermute | solution.py:283
  28.5 2.5 %collective-permute-start.10 = (f32[136,128]{1,0:T(8,128)S(1)}, f32[136,128]{1,0:T(8,128)S(1)}, u32[]{:S(2)}, u32[]{:S(2)}) collective-permute-start(f32[136,128]{1,0:T(8,128)S(1)} %add.10.refs_0_), channel_id=1, source_target_pairs={{0,6},{1,7},{2,4},{3,5},{4,2},{5,3},{6,0},{7,1},{8,14},{9,15},{10,... | collective-permute-start | bytes 208904 | tf_op jit(solution)/shard_map/ppermute | solution.py:283
  31.0 0.5 collective-permute-start.9
  31.5 0.5 collective-permute-start.8
  32.0 0.1 collective-permute-start.13
  32.1 1.6 %collective-permute-done.10.refs_3_ = f32[136,128]{1,0:T(8,128)S(1)} collective-permute-done((f32[136,128]{1,0:T(8,128)S(1)}, f32[136,128]{1,0:T(8,128)S(1)}, u32[]{:S(2)}, u32[]{:S(2)}) %collective-permute-start.10) | collective-permute-done | bytes 69664 | tf_op jit(solution)/shard_map/ppermute | solution.py:283
  33.8 1.5 %collective-permute-done.9.refs_2_ = f32[136,128]{1,0:T(8,128)S(1)} collective-permute-done((f32[136,128]{1,0:T(8,128)S(1)}, f32[136,128]{1,0:T(8,128)S(1)}, u32[]{:S(2)}, u32[]{:S(2)}) %collective-permute-start.9) | collective-permute-done | bytes 69664 | tf_op jit(solution)/shard_map/ppermute | solution.py:283
  35.3 0.5 collective-permute-done.8.refs_1_
  35.8 0.1 ratio.4.s_ref
  35.9 0.2 collective-permute-start.11
  36.1 2.0 %own.4 = (f32[1024,128]{1,0:T(8,128)S(1)}, f32[256,128]{1,0:T(8,128)S(1)}, f32[128,128]{1,0:T(8,128)S(1)}) custom-call(f32[136,128]{1,0:T(8,128)S(1)} %ratio.4.s_ref, f32[1024,256]{1,0:T(8,128)S(1)} %get-tuple-element.31.pair_ref), custom_call_target="tpu_custom_call" | custom-call | flops 500000000 | bytes 1750001 | tf_op jit(solution)/shard_map/own/pallas_call | solution.py:258
  38.0 1.6 %collective-permute-start.14 = (f32[256,128]{1,0:T(8,128)S(1)}, f32[256,128]{1,0:T(8,128)S(1)}, u32[]{:S(2)}, u32[]{:S(2)}) collective-permute-start(f32[256,128]{1,0:T(8,128)S(1)} %get-tuple-element.38), channel_id=1, source_target_pairs={{0,8},{8,16},{16,24},{24,0},{1,9},{9,17},{17,25},{25,1},{2,10},{10... | collective-permute-start | bytes 393224 | tf_op jit(solution)/shard_map/ppermute | solution.py:272
  39.7 3.4 %collective-permute-done.13.refs_2_ = f32[192,128]{1,0:T(8,128)S(1)} collective-permute-done((f32[192,128]{1,0:T(8,128)S(1)}, f32[192,128]{1,0:T(8,128)S(1)}, u32[]{:S(2)}, u32[]{:S(2)}) %collective-permute-start.13) | collective-permute-done | bytes 98336 | tf_op jit(solution)/shard_map/ppermute | solution.py:272
  43.1 1.5 %collective-permute-done.11.s_ref = f32[136,128]{1,0:T(8,128)S(1)} collective-permute-done((f32[136,128]{1,0:T(8,128)S(1)}, f32[136,128]{1,0:T(8,128)S(1)}, u32[]{:S(2)}, u32[]{:S(2)}) %collective-permute-start.11) | collective-permute-done | bytes 69664 | tf_op jit(solution)/shard_map/ppermute | solution.py:272
  44.6 1.9 %turn.4 = (f32[768,128]{1,0:T(8,128)S(1)}, f32[768,128]{1,0:T(8,128)S(1)}) custom-call(f32[136,128]{1,0:T(8,128)S(1)} %collective-permute-done.11.s_ref, f32[576,128]{1,0:T(8,128)S(1)} %get-tuple-element.33.refs_0_, f32[768,128]{1,0:T(8,128)S(1)} %collective-permute-done.12.refs_1_, f32[192,128]{1,0:T(8,128)S(1)} %collective-permute-done.13.refs_2_), custom_call_target="tpu_custom_call" | custom-call | flops 1000000000 | bytes 3500001 | tf_op jit(solution)/shard_map/turn/pallas_call | solution.py:258
  46.5 0.4 collective-permute-done.14.tail_ref
  46.9 0.7 %join.4 = (f32[1024,256]{1,0:T(8,128)S(1)}, f32[264,128]{1,0:T(8,128)S(1)}, f32[896,128]{1,0:T(8,128)S(1)}) custom-call(f32[1024,128]{1,0:T(8,128)S(1)} %get-tuple-element.32.staying_ref, f32[768,128]{1,0:T(8,128)S(1)} %get-tuple-element.37.moving_ref, f32[256,128]{1,0:T(8,128)S(1)} %collective-permute-done.14.tail_ref), custom_call_target="tpu_custom_call" | custom-call | flops 2000000000 | bytes 7000001 | tf_op jit(solution)/shard_map/join/pallas_call | solution.py:258
  47.8 1.3 %collective-permute-done.15 = f32[264,128]{1,0:T(8,128)S(1)} collective-permute-done((f32[264,128]{1,0:T(8,128)S(1)}, f32[264,128]{1,0:T(8,128)S(1)}, u32[]{:S(2)}, u32[]{:S(2)}) %collective-permute-start.15) | collective-permute-done | bytes 135200 | tf_op jit(solution)/shard_map/ppermute | solution.py:283
  49.1 2.5 %collective-permute-start.18 = (f32[264,128]{1,0:T(8,128)S(1)}, f32[264,128]{1,0:T(8,128)S(1)}, u32[]{:S(2)}, u32[]{:S(2)}) collective-permute-start(f32[264,128]{1,0:T(8,128)S(1)} %add.11.refs_0_), channel_id=1, source_target_pairs={{0,6},{1,7},{2,4},{3,5},{4,2},{5,3},{6,0},{7,1},{8,14},{9,15},{10,... | collective-permute-start | bytes 405512 | tf_op jit(solution)/shard_map/ppermute | solution.py:283
  51.6 0.5 collective-permute-start.17
  52.1 0.5 collective-permute-start.16
  52.7 3.4 %collective-permute-done.18.refs_3_ = f32[264,128]{1,0:T(8,128)S(1)} collective-permute-done((f32[264,128]{1,0:T(8,128)S(1)}, f32[264,128]{1,0:T(8,128)S(1)}, u32[]{:S(2)}, u32[]{:S(2)}) %collective-permute-start.18) | collective-permute-done | bytes 135200 | tf_op jit(solution)/shard_map/ppermute | solution.py:283
  56.1 2.5 %collective-permute-done.17.refs_2_ = f32[264,128]{1,0:T(8,128)S(1)} collective-permute-done((f32[264,128]{1,0:T(8,128)S(1)}, f32[264,128]{1,0:T(8,128)S(1)}, u32[]{:S(2)}, u32[]{:S(2)}) %collective-permute-start.17) | collective-permute-done | bytes 135200 | tf_op jit(solution)/shard_map/ppermute | solution.py:283
  58.6 0.1 collective-permute-done.16.refs_1_
  58.7 0.1 ratio.5
  58.9 2.3 %own.5 = (f32[1024,128]{1,0:T(8,128)S(1)}, f32[136,128]{1,0:T(8,128)S(1)}, f32[8,128]{1,0:T(8,128)S(1)}) custom-call(f32[136,128]{1,0:T(8,128)S(1)} %get-tuple-element.40.s_ref, f32[1024,256]{1,0:T(8,128)S(1)} %get-tuple-element.41.pair_ref, f32[264,128]{1,0:T(8,128)S(1)} %get-tuple-element.42.refs_0_), custom_call_target="tpu_custom_call" | custom-call | flops 800000000 | bytes 2800001 | tf_op jit(solution)/shard_map/own/pallas_call | solution.py:258
  61.2 3.1 %collective-permute-done.21.refs_2_ = f32[128,128]{1,0:T(8,128)S(1)} collective-permute-done((f32[128,128]{1,0:T(8,128)S(1)}, f32[128,128]{1,0:T(8,128)S(1)}, u32[]{:S(2)}, u32[]{:S(2)}) %collective-permute-start.21) | collective-permute-done | bytes 65568 | tf_op jit(solution)/shard_map/ppermute | solution.py:272
  64.3 1.0 %collective-permute-done.19.s_ref = f32[136,128]{1,0:T(8,128)S(1)} collective-permute-done((f32[136,128]{1,0:T(8,128)S(1)}, f32[136,128]{1,0:T(8,128)S(1)}, u32[]{:S(2)}, u32[]{:S(2)}) %collective-permute-start.19) | collective-permute-done | bytes 69664 | tf_op jit(solution)/shard_map/ppermute | solution.py:272
  65.4 1.9 %turn.5.moving_ref = f32[896,128]{1,0:T(8,128)S(1)} custom-call(f32[136,128]{1,0:T(8,128)S(1)} %collective-permute-done.19.s_ref, f32[768,128]{1,0:T(8,128)S(1)} %get-tuple-element.44.refs_0_, f32[896,128]{1,0:T(8,128)S(1)} %collective-permute-done.20.refs_1_, f32[128,128]{1,0:T(8,128)S(1)} %collective-permute-done.21.refs_2_), custom_call_target="tpu_custom_call" | custom-call | flops 1000000000 | bytes 3500001 | tf_op jit(solution)/shard_map/turn/pallas_call | solution.py:258
  67.3 1.1 %join.5 = (f32[1024,256]{1,0:T(8,128)}, f32[1,256]{1,0:T(1,128)}) custom-call(f32[1024,128]{1,0:T(8,128)S(1)} %get-tuple-element.43.staying_ref, f32[896,128]{1,0:T(8,128)S(1)} %turn.5.moving_ref, f32[136,128]{1,0:T(8,128)S(1)} %collective-permute-done.22.tail_ref, f32[8,128]{1,0:T(8,128)S(1)} %get-tuple-element.49.refs_0_), custom_call_target="tpu_custom_call" | custom-call | flops 500000000 | bytes 1750001 | tf_op jit(solution)/shard_map/join/pallas_call | solution.py:258
  (23 shorter events, 0.8 us)
Async XLA Ops:
  0.6 4.3 %copy-start = (f32[1024,256]{1,0:T(8,128)S(1)}, f32[1024,256]{1,0:T(8,128)}, u32[]{:S(2)}) copy-start(f32[1024,256]{1,0:T(8,128)} %pair_ref.3) | copy-start | bytes 3145732
  1.8 20.8 %collective-permute-start.5 = (f32[576,256]{1,0:T(8,128)S(1)}, f32[576,256]{1,0:T(8,128)S(1)}, u32[]{:S(2)}, u32[]{:S(2)}) collective-permute-start(f32[576,256]{1,0:T(8,128)S(1)} %slice.3), channel_id=1, source_target_pairs={{0,8},{8,16},{16,24},{24,0},{1,9},{9,17},{17,25},{25,1},{2,10},{10... | collective-permute-start | bytes 1769480 | tf_op jit(solution)/shard_map/ppermute | solution.py:272
  5.3 4.9 %copy-start.1 = (s32[3,1]{0,1:T(1,128)S(1)}, s32[3,1]{0,1:T(1,128)}, u32[]{:S(2)}) copy-start(s32[3,1]{0,1:T(1,128)} %param.3) | copy-start | bytes 40
  5.3 1.3 %collective-permute-start = (f32[136,128]{1,0:T(8,128)S(1)}, f32[136,128]{1,0:T(8,128)S(1)}, u32[]{:S(2)}, u32[]{:S(2)}) collective-permute-start(f32[136,128]{1,0:T(8,128)S(1)} %gram.1), channel_id=1, source_target_pairs={{0,1},{1,0},{2,3},{3,2},{4,5},{5,4},{6,7},{7,6},{8,9},{9,8},{10,11... | collective-permute-start | bytes 208904 | tf_op jit(solution)/shard_map/ppermute | solution.py:283
  6.6 5.3 %collective-permute-start.3 = (f32[136,128]{1,0:T(8,128)S(1)}, f32[136,128]{1,0:T(8,128)S(1)}, u32[]{:S(2)}, u32[]{:S(2)}) collective-permute-start(f32[136,128]{1,0:T(8,128)S(1)} %add.9.refs_0_), channel_id=1, source_target_pairs={{0,6},{1,7},{2,4},{3,5},{4,2},{5,3},{6,0},{7,1},{8,14},{9,15},{10,... | collective-permute-start | bytes 208904 | tf_op jit(solution)/shard_map/ppermute | solution.py:283
  9.2 4.3 %collective-permute-start.2 = (f32[136,128]{1,0:T(8,128)S(1)}, f32[136,128]{1,0:T(8,128)S(1)}, u32[]{:S(2)}, u32[]{:S(2)}) collective-permute-start(f32[136,128]{1,0:T(8,128)S(1)} %add.9.refs_0_), channel_id=1, source_target_pairs={{0,4},{1,5},{2,6},{3,7},{4,0},{5,1},{6,2},{7,3},{8,12},{9,13},{10,... | collective-permute-start | bytes 208904 | tf_op jit(solution)/shard_map/ppermute | solution.py:283
  9.7 4.3 %collective-permute-start.1 = (f32[136,128]{1,0:T(8,128)S(1)}, f32[136,128]{1,0:T(8,128)S(1)}, u32[]{:S(2)}, u32[]{:S(2)}) collective-permute-start(f32[136,128]{1,0:T(8,128)S(1)} %add.9.refs_0_), channel_id=1, source_target_pairs={{0,2},{1,3},{2,0},{3,1},{4,6},{5,7},{6,4},{7,5},{8,10},{9,11},{10,... | collective-permute-start | bytes 208904 | tf_op jit(solution)/shard_map/ppermute | solution.py:283
  14.2 8.4 %collective-permute-start.4 = (f32[136,128]{1,0:T(8,128)S(1)}, f32[136,128]{1,0:T(8,128)S(1)}, u32[]{:S(2)}, u32[]{:S(2)}) collective-permute-start(f32[136,128]{1,0:T(8,128)S(1)} %ratio.3.s_ref), channel_id=1, source_target_pairs={{0,8},{8,16},{16,24},{24,0},{1,9},{9,17},{17,25},{25,1},{2,10},{10... | collective-permute-start | bytes 208904 | tf_op jit(solution)/shard_map/ppermute | solution.py:272
  17.8 8.9 %collective-permute-start.6 = (f32[448,128]{1,0:T(8,128)S(1)}, f32[448,128]{1,0:T(8,128)S(1)}, u32[]{:S(2)}, u32[]{:S(2)}) collective-permute-start(f32[448,128]{1,0:T(8,128)S(1)} %get-tuple-element.29), channel_id=1, source_target_pairs={{0,8},{8,16},{16,24},{24,0},{1,9},{9,17},{17,25},{25,1},{2,10},{10... | collective-permute-start | bytes 688136 | tf_op jit(solution)/shard_map/ppermute | solution.py:272
  27.1 1.3 %collective-permute-start.7 = (f32[136,128]{1,0:T(8,128)S(1)}, f32[136,128]{1,0:T(8,128)S(1)}, u32[]{:S(2)}, u32[]{:S(2)}) collective-permute-start(f32[136,128]{1,0:T(8,128)S(1)} %get-tuple-element.30), channel_id=1, source_target_pairs={{0,1},{1,0},{2,3},{3,2},{4,5},{5,4},{6,7},{7,6},{8,9},{9,8},{10,11... | collective-permute-start | bytes 208904 | tf_op jit(solution)/shard_map/ppermute | solution.py:283
  27.2 17.4 %collective-permute-start.12 = (f32[768,128]{1,0:T(8,128)S(1)}, f32[768,128]{1,0:T(8,128)S(1)}, u32[]{:S(2)}, u32[]{:S(2)}) collective-permute-start(f32[768,128]{1,0:T(8,128)S(1)} %get-tuple-element.34), channel_id=1, source_target_pairs={{0,8},{8,16},{16,24},{24,0},{1,9},{9,17},{17,25},{25,1},{2,10},{10... | collective-permute-start | bytes 1179656 | tf_op jit(solution)/shard_map/ppermute | solution.py:272
  28.5 5.3 %collective-permute-start.10 = (f32[136,128]{1,0:T(8,128)S(1)}, f32[136,128]{1,0:T(8,128)S(1)}, u32[]{:S(2)}, u32[]{:S(2)}) collective-permute-start(f32[136,128]{1,0:T(8,128)S(1)} %add.10.refs_0_), channel_id=1, source_target_pairs={{0,6},{1,7},{2,4},{3,5},{4,2},{5,3},{6,0},{7,1},{8,14},{9,15},{10,... | collective-permute-start | bytes 208904 | tf_op jit(solution)/shard_map/ppermute | solution.py:283
  31.0 4.3 %collective-permute-start.9 = (f32[136,128]{1,0:T(8,128)S(1)}, f32[136,128]{1,0:T(8,128)S(1)}, u32[]{:S(2)}, u32[]{:S(2)}) collective-permute-start(f32[136,128]{1,0:T(8,128)S(1)} %add.10.refs_0_), channel_id=1, source_target_pairs={{0,4},{1,5},{2,6},{3,7},{4,0},{5,1},{6,2},{7,3},{8,12},{9,13},{10,... | collective-permute-start | bytes 208904 | tf_op jit(solution)/shard_map/ppermute | solution.py:283
  31.5 4.3 %collective-permute-start.8 = (f32[136,128]{1,0:T(8,128)S(1)}, f32[136,128]{1,0:T(8,128)S(1)}, u32[]{:S(2)}, u32[]{:S(2)}) collective-permute-start(f32[136,128]{1,0:T(8,128)S(1)} %add.10.refs_0_), channel_id=1, source_target_pairs={{0,2},{1,3},{2,0},{3,1},{4,6},{5,7},{6,4},{7,5},{8,10},{9,11},{10,... | collective-permute-start | bytes 208904 | tf_op jit(solution)/shard_map/ppermute | solution.py:283
  32.0 11.1 %collective-permute-start.13 = (f32[192,128]{1,0:T(8,128)S(1)}, f32[192,128]{1,0:T(8,128)S(1)}, u32[]{:S(2)}, u32[]{:S(2)}) collective-permute-start(f32[192,128]{1,0:T(8,128)S(1)} %get-tuple-element.36), channel_id=1, source_target_pairs={{0,8},{8,16},{16,24},{24,0},{1,9},{9,17},{17,25},{25,1},{2,10},{10... | collective-permute-start | bytes 294920 | tf_op jit(solution)/shard_map/ppermute | solution.py:272
  35.9 8.7 %collective-permute-start.11 = (f32[136,128]{1,0:T(8,128)S(1)}, f32[136,128]{1,0:T(8,128)S(1)}, u32[]{:S(2)}, u32[]{:S(2)}) collective-permute-start(f32[136,128]{1,0:T(8,128)S(1)} %ratio.4.s_ref), channel_id=1, source_target_pairs={{0,8},{8,16},{16,24},{24,0},{1,9},{9,17},{17,25},{25,1},{2,10},{10... | collective-permute-start | bytes 208904 | tf_op jit(solution)/shard_map/ppermute | solution.py:272
  38.0 8.9 %collective-permute-start.14 = (f32[256,128]{1,0:T(8,128)S(1)}, f32[256,128]{1,0:T(8,128)S(1)}, u32[]{:S(2)}, u32[]{:S(2)}) collective-permute-start(f32[256,128]{1,0:T(8,128)S(1)} %get-tuple-element.38), channel_id=1, source_target_pairs={{0,8},{8,16},{16,24},{24,0},{1,9},{9,17},{17,25},{25,1},{2,10},{10... | collective-permute-start | bytes 393224 | tf_op jit(solution)/shard_map/ppermute | solution.py:272
  47.7 1.4 %collective-permute-start.15 = (f32[264,128]{1,0:T(8,128)S(1)}, f32[264,128]{1,0:T(8,128)S(1)}, u32[]{:S(2)}, u32[]{:S(2)}) collective-permute-start(f32[264,128]{1,0:T(8,128)S(1)} %get-tuple-element.39), channel_id=1, source_target_pairs={{0,1},{1,0},{2,3},{3,2},{4,5},{5,4},{6,7},{7,6},{8,9},{9,8},{10,11... | collective-permute-start | bytes 405512 | tf_op jit(solution)/shard_map/ppermute | solution.py:283
  47.7 17.6 %collective-permute-start.20 = (f32[896,128]{1,0:T(8,128)S(1)}, f32[896,128]{1,0:T(8,128)S(1)}, u32[]{:S(2)}, u32[]{:S(2)}) collective-permute-start(f32[896,128]{1,0:T(8,128)S(1)} %get-tuple-element.45), channel_id=1, source_target_pairs={{0,8},{8,16},{16,24},{24,0},{1,9},{9,17},{17,25},{25,1},{2,10},{10... | collective-permute-start | bytes 1376264 | tf_op jit(solution)/shard_map/ppermute | solution.py:272
  49.1 7.0 %collective-permute-start.18 = (f32[264,128]{1,0:T(8,128)S(1)}, f32[264,128]{1,0:T(8,128)S(1)}, u32[]{:S(2)}, u32[]{:S(2)}) collective-permute-start(f32[264,128]{1,0:T(8,128)S(1)} %add.11.refs_0_), channel_id=1, source_target_pairs={{0,6},{1,7},{2,4},{3,5},{4,2},{5,3},{6,0},{7,1},{8,14},{9,15},{10,... | collective-permute-start | bytes 405512 | tf_op jit(solution)/shard_map/ppermute | solution.py:283
  51.6 7.0 %collective-permute-start.17 = (f32[264,128]{1,0:T(8,128)S(1)}, f32[264,128]{1,0:T(8,128)S(1)}, u32[]{:S(2)}, u32[]{:S(2)}) collective-permute-start(f32[264,128]{1,0:T(8,128)S(1)} %add.11.refs_0_), channel_id=1, source_target_pairs={{0,4},{1,5},{2,6},{3,7},{4,0},{5,1},{6,2},{7,3},{8,12},{9,13},{10,... | collective-permute-start | bytes 405512 | tf_op jit(solution)/shard_map/ppermute | solution.py:283
  52.1 6.6 %collective-permute-start.16 = (f32[264,128]{1,0:T(8,128)S(1)}, f32[264,128]{1,0:T(8,128)S(1)}, u32[]{:S(2)}, u32[]{:S(2)}) collective-permute-start(f32[264,128]{1,0:T(8,128)S(1)} %add.11.refs_0_), channel_id=1, source_target_pairs={{0,2},{1,3},{2,0},{3,1},{4,6},{5,7},{6,4},{7,5},{8,10},{9,11},{10,... | collective-permute-start | bytes 405512 | tf_op jit(solution)/shard_map/ppermute | solution.py:283
  52.7 11.7 %collective-permute-start.21 = (f32[128,128]{1,0:T(8,128)S(1)}, f32[128,128]{1,0:T(8,128)S(1)}, u32[]{:S(2)}, u32[]{:S(2)}) collective-permute-start(f32[128,128]{1,0:T(8,128)S(1)} %get-tuple-element.47), channel_id=1, source_target_pairs={{0,8},{8,16},{16,24},{24,0},{1,9},{9,17},{17,25},{25,1},{2,10},{10... | collective-permute-start | bytes 196616 | tf_op jit(solution)/shard_map/ppermute | solution.py:272
  58.8 6.5 %collective-permute-start.19 = (f32[136,128]{1,0:T(8,128)S(1)}, f32[136,128]{1,0:T(8,128)S(1)}, u32[]{:S(2)}, u32[]{:S(2)}) collective-permute-start(f32[136,128]{1,0:T(8,128)S(1)} %get-tuple-element.40.s_ref), channel_id=1, source_target_pairs={{0,8},{8,16},{16,24},{24,0},{1,9},{9,17},{17,25},{25,1},{2,10},{10... | collective-permute-start | bytes 208904 | tf_op jit(solution)/shard_map/ppermute | solution.py:272
  61.2 6.2 %collective-permute-start.22 = (f32[136,128]{1,0:T(8,128)S(1)}, f32[136,128]{1,0:T(8,128)S(1)}, u32[]{:S(2)}, u32[]{:S(2)}) collective-permute-start(f32[136,128]{1,0:T(8,128)S(1)} %get-tuple-element.48), channel_id=1, source_target_pairs={{0,8},{8,16},{16,24},{24,0},{1,9},{9,17},{17,25},{25,1},{2,10},{10... | collective-permute-start | bytes 208904 | tf_op jit(solution)/shard_map/ppermute | solution.py:272

commit v4 on v3

--- a/solution.py
+++ b/solution.py
@@ -8,7 +8,7 @@
 
 epsilon = 1e-06
 MICROS = (
-    {"own": 1.0, "turn": 4.0},
+    {"own": 1.0, "turn": 2.0},
     {"ratio": 2.0, "own": 0.5, "turn": 1.0, "join": 2.0},
     {"ratio": 1.5, "own": 0.8, "turn": 1.0, "join": 0.5, "both": 2.0},
 )
@@ -272,17 +272,19 @@
     return lax.ppermute(block, axis, [(i, (i + 1) % size) for i in range(size)])
 
 
-def parts_of_sum(term, axis):
+def parts_of_sum(term, axis, ahead):
     size = lax.axis_size(axis)
     if size & (size - 1):
-        return [lax.psum(term, axis)]
+        return [lax.psum(term, axis)], ahead
     parts, bit = [term], 1
     while bit < size:
         term = functools.reduce(lambda x, y: x + y, parts)
+        if bit > 1:
+            term, ahead = lax.optimization_barrier((term, ahead))
         masks = [bit] if bit == 1 or 2 * bit >= size else [bit, 2 * bit, 3 * bit]
         parts = [term] + [lax.ppermute(term, axis, [(i, i ^ mask) for i in range(size)]) for mask in masks]
         bit *= 2 if len(masks) == 1 else 4
-    return parts
+    return parts, ahead
 
 
 def known_rows(rows, rounds):
@@ -302,10 +304,12 @@
     neighbour = [passed_along(record[: heads[0]], "col")]
     (terms,) = call(gram_kernel, [pair], [grams[0]], name="gram")
     plan_rows = jnp.repeat(jnp.broadcast_to(plan.astype(F32), (rounds, width)), 8, axis=0)
+    ahead = []
     for step in range(rounds):
         known, kept, last = heads[step], heads[step + 1], step + 1 == rounds
         place = 2 if last else min(step, 1)
-        parts = parts_of_sum(terms, "tm")
+        parts, ahead = parts_of_sum(terms, "tm", ahead)
+        neighbour += ahead
         kernel = functools.partial(ratio_kernel, 8 * step, len(parts))
         ratio, *gram = call(kernel, [plan_rows] + parts, [ratios] + [grams[step]] * last, name="ratio", place=place)
         neighbour_ratio = passed_along(ratio, "col")
@@ -332,7 +336,10 @@
             return (pair, rest[0].reshape(2 * width))
         terms, moving = rest
         neighbour = kept_staying + [passed_along(moving, "col")]
-        if known < kept:
+        ahead = []
+        if known < kept and step == 0:
+            ahead = [passed_along(sent[-1], "col")]
+        elif known < kept:
             more = sent[-1]
             if tail is not None:
                 more, _ = lax.optimization_barrier((more, tail))

time: 68.5 us -> 68.1 us (level)
  waiting for transfers between devices: 31.9 us -> 29 us
  starting transfers between devices: 19.3 us -> 21.9 us
    ppermute x11, starting transfers between devices: 8.45 us -> 11 us  [passed_along(): return lax.ppermute(block, axis, [(i, (i + 1) % size) for i in range(size)])]
    ppermute x11, waiting for transfers between devices: 14.9 us -> 12.4 us  [passed_along(): return lax.ppermute(block, axis, [(i, (i + 1) % size) for i in range(size)])]
where the time goes in v4:
time: 68.1 us; the launch traced here: 68 us
  waiting for transfers between devices  29 us (43%)
  starting transfers between devices  21.9 us (32%)
  Pallas kernels  14.9 us (22%)
  local copies, waits for them, and re-layouts  1.43 us (2%)
  between operations  0.78 us (1%)
    ppermute x12, waiting for transfers between devices, parts_of_sum(): lax.ppermute(term, axis, [(i, i ^ mask) for i in range(size)])  16.6 us
    pallas_call x13, Pallas kernels, call(): pl.pallas_call(kernel, out_shape=[jax.ShapeDtypeStruct(shape, F32) for sh...  14.9 us
    ppermute x11, waiting for transfers between devices, passed_along(): return lax.ppermute(block, axis, [(i, (i + 1) % size) for i in range(size)])  12.4 us
    ppermute x11, starting transfers between devices, passed_along(): return lax.ppermute(block, axis, [(i, (i + 1) % size) for i in range(size)])  11 us
    ppermute x12, starting transfers between devices, parts_of_sum(): lax.ppermute(term, axis, [(i, i ^ mask) for i in range(size)])  10.9 us
  transfers between devices with their start and end apart: 23, of which 19 were waited for; matrix products, arithmetic and copies ran while one was open for 0% of the time, Pallas kernels for 19%

profile of v4, /device:TPU:0, one launch (start us, length us, event | category | flops | bytes accessed | tf_op | source)
XLA Modules:
  0.0 68.0 jit_solution(7804365277934406035)
XLA Ops:
  0.6 1.2 %slice.3 = f32[576,256]{1,0:T(8,128)S(1)} slice(f32[1024,256]{1,0:T(8,128)} %pair_ref.3), slice={[0:576], [0:256]} | slice | bytes 1179648 | tf_op jit(solution)/shard_map/slice | solution.py:304
  1.8 3.1 %collective-permute-start.5 = (f32[576,256]{1,0:T(8,128)S(1)}, f32[576,256]{1,0:T(8,128)S(1)}, u32[]{:S(2)}, u32[]{:S(2)}) collective-permute-start(f32[576,256]{1,0:T(8,128)S(1)} %slice.3), channel_id=1, source_target_pairs={{0,8},{8,16},{16,24},{24,0},{1,9},{9,17},{17,25},{25,1},{2,10},{10... | collective-permute-start | bytes 1769480 | tf_op jit(solution)/shard_map/ppermute | solution.py:272
  4.9 0.4 gram.1
  5.4 1.2 %collective-permute-done = f32[136,128]{1,0:T(8,128)S(1)} collective-permute-done((f32[136,128]{1,0:T(8,128)S(1)}, f32[136,128]{1,0:T(8,128)S(1)}, u32[]{:S(2)}, u32[]{:S(2)}) %collective-permute-start) | collective-permute-done | bytes 69664 | tf_op jit(solution)/shard_map/ppermute | solution.py:285
  6.6 2.5 %collective-permute-start.3 = (f32[136,128]{1,0:T(8,128)S(1)}, f32[136,128]{1,0:T(8,128)S(1)}, u32[]{:S(2)}, u32[]{:S(2)}) collective-permute-start(f32[136,128]{1,0:T(8,128)S(1)} %add.9.refs_0_), channel_id=1, source_target_pairs={{0,6},{1,7},{2,4},{3,5},{4,2},{5,3},{6,0},{7,1},{8,14},{9,15},{10,... | collective-permute-start | bytes 208904 | tf_op jit(solution)/shard_map/ppermute | solution.py:285
  9.2 0.5 collective-permute-start.2
  9.7 0.5 collective-permute-start.1
  10.4 1.6 %collective-permute-done.3.refs_3_ = f32[136,128]{1,0:T(8,128)S(1)} collective-permute-done((f32[136,128]{1,0:T(8,128)S(1)}, f32[136,128]{1,0:T(8,128)S(1)}, u32[]{:S(2)}, u32[]{:S(2)}) %collective-permute-start.3) | collective-permute-done | bytes 69664 | tf_op jit(solution)/shard_map/ppermute | solution.py:285
  11.9 1.5 %collective-permute-done.2.refs_2_ = f32[136,128]{1,0:T(8,128)S(1)} collective-permute-done((f32[136,128]{1,0:T(8,128)S(1)}, f32[136,128]{1,0:T(8,128)S(1)}, u32[]{:S(2)}, u32[]{:S(2)}) %collective-permute-start.2) | collective-permute-done | bytes 69664 | tf_op jit(solution)/shard_map/ppermute | solution.py:285
  13.5 0.5 collective-permute-done.1.refs_1_
  14.2 1.6 %collective-permute-start.4 = (f32[136,128]{1,0:T(8,128)S(1)}, f32[136,128]{1,0:T(8,128)S(1)}, u32[]{:S(2)}, u32[]{:S(2)}) collective-permute-start(f32[136,128]{1,0:T(8,128)S(1)} %ratio.3.s_ref), channel_id=1, source_target_pairs={{0,8},{8,16},{16,24},{24,0},{1,9},{9,17},{17,25},{25,1},{2,10},{10... | collective-permute-start | bytes 208904 | tf_op jit(solution)/shard_map/ppermute | solution.py:272
  15.8 2.0 %own.3 = (f32[1024,128]{1,0:T(8,128)S(1)}, f32[448,128]{1,0:T(8,128)S(1)}, f32[192,128]{1,0:T(8,128)S(1)}) custom-call(f32[136,128]{1,0:T(8,128)S(1)} %ratio.3.s_ref, f32[1024,256]{1,0:T(8,128)S(1)} %copy-done), custom_call_target="tpu_custom_call" | custom-call | flops 1000000000 | bytes 3500001 | tf_op jit(solution)/shard_map/own/pallas_call | solution.py:258
  17.8 1.6 %collective-permute-start.6 = (f32[448,128]{1,0:T(8,128)S(1)}, f32[448,128]{1,0:T(8,128)S(1)}, u32[]{:S(2)}, u32[]{:S(2)}) collective-permute-start(f32[448,128]{1,0:T(8,128)S(1)} %get-tuple-element.30), channel_id=1, source_target_pairs={{0,8},{8,16},{16,24},{24,0},{1,9},{9,17},{17,25},{25,1},{2,10},{10... | collective-permute-start | bytes 688136 | tf_op jit(solution)/shard_map/ppermute | solution.py:272
  19.4 0.2 collective-permute-start.8
  19.6 3.0 %collective-permute-done.4.s_ref = f32[136,128]{1,0:T(8,128)S(1)} collective-permute-done((f32[136,128]{1,0:T(8,128)S(1)}, f32[136,128]{1,0:T(8,128)S(1)}, u32[]{:S(2)}, u32[]{:S(2)}) %collective-permute-start.4) | collective-permute-done | bytes 69664 | tf_op jit(solution)/shard_map/ppermute | solution.py:272
  22.6 1.8 %turn.3 = (f32[576,128]{1,0:T(8,128)S(1)}, f32[576,128]{1,0:T(8,128)S(1)}) custom-call(f32[136,128]{1,0:T(8,128)S(1)} %collective-permute-done.4.s_ref, f32[576,256]{1,0:T(8,128)S(1)} %collective-permute-done.5.refs_0_), custom_call_target="tpu_custom_call" | custom-call | flops 2000000000 | bytes 7000001 | tf_op jit(solution)/shard_map/turn/pallas_call | solution.py:258
  24.4 3.3 %collective-permute-done.6.tail_ref = f32[448,128]{1,0:T(8,128)S(1)} collective-permute-done((f32[448,128]{1,0:T(8,128)S(1)}, f32[448,128]{1,0:T(8,128)S(1)}, u32[]{:S(2)}, u32[]{:S(2)}) %collective-permute-start.6) | collective-permute-done | bytes 229408 | tf_op jit(solution)/shard_map/ppermute | solution.py:272
  27.7 0.4 join.3
  28.3 1.2 %collective-permute-done.7 = f32[136,128]{1,0:T(8,128)S(1)} collective-permute-done((f32[136,128]{1,0:T(8,128)S(1)}, f32[136,128]{1,0:T(8,128)S(1)}, u32[]{:S(2)}, u32[]{:S(2)}) %collective-permute-start.7) | collective-permute-done | bytes 69664 | tf_op jit(solution)/shard_map/ppermute | solution.py:285
  29.5 2.5 %collective-permute-start.11 = (f32[136,128]{1,0:T(8,128)S(1)}, f32[136,128]{1,0:T(8,128)S(1)}, u32[]{:S(2)}, u32[]{:S(2)}) collective-permute-start(f32[136,128]{1,0:T(8,128)S(1)} %add.10.refs_0_), channel_id=1, source_target_pairs={{0,6},{1,7},{2,4},{3,5},{4,2},{5,3},{6,0},{7,1},{8,14},{9,15},{10,... | collective-permute-start | bytes 208904 | tf_op jit(solution)/shard_map/ppermute | solution.py:285
  32.0 0.3 collective-permute-start.10
  32.4 0.7 %collective-permute-start.9 = (f32[136,128]{1,0:T(8,128)S(1)}, f32[136,128]{1,0:T(8,128)S(1)}, u32[]{:S(2)}, u32[]{:S(2)}) collective-permute-start(f32[136,128]{1,0:T(8,128)S(1)} %add.10.refs_0_), channel_id=1, source_target_pairs={{0,2},{1,3},{2,0},{3,1},{4,6},{5,7},{6,4},{7,5},{8,10},{9,11},{10,... | collective-permute-start | bytes 208904 | tf_op jit(solution)/shard_map/ppermute | solution.py:285
  33.1 1.7 %collective-permute-done.11.refs_3_ = f32[136,128]{1,0:T(8,128)S(1)} collective-permute-done((f32[136,128]{1,0:T(8,128)S(1)}, f32[136,128]{1,0:T(8,128)S(1)}, u32[]{:S(2)}, u32[]{:S(2)}) %collective-permute-start.11) | collective-permute-done | bytes 69664 | tf_op jit(solution)/shard_map/ppermute | solution.py:285
  34.8 1.5 %collective-permute-done.10.refs_2_ = f32[136,128]{1,0:T(8,128)S(1)} collective-permute-done((f32[136,128]{1,0:T(8,128)S(1)}, f32[136,128]{1,0:T(8,128)S(1)}, u32[]{:S(2)}, u32[]{:S(2)}) %collective-permute-start.10) | collective-permute-done | bytes 69664 | tf_op jit(solution)/shard_map/ppermute | solution.py:285
  36.3 0.3 collective-permute-done.9.refs_1_
  36.8 0.3 collective-permute-start.12
  37.1 2.0 %own.4 = (f32[1024,128]{1,0:T(8,128)S(1)}, f32[256,128]{1,0:T(8,128)S(1)}, f32[128,128]{1,0:T(8,128)S(1)}) custom-call(f32[136,128]{1,0:T(8,128)S(1)} %ratio.4.s_ref, f32[1024,256]{1,0:T(8,128)S(1)} %get-tuple-element.34.pair_ref), custom_call_target="tpu_custom_call" | custom-call | flops 500000000 | bytes 1750001 | tf_op jit(solution)/shard_map/own/pallas_call | solution.py:258
  39.1 1.6 %collective-permute-start.14 = (f32[256,128]{1,0:T(8,128)S(1)}, f32[256,128]{1,0:T(8,128)S(1)}, u32[]{:S(2)}, u32[]{:S(2)}) collective-permute-start(f32[256,128]{1,0:T(8,128)S(1)} %get-tuple-element.40), channel_id=1, source_target_pairs={{0,8},{8,16},{16,24},{24,0},{1,9},{9,17},{17,25},{25,1},{2,10},{10... | collective-permute-start | bytes 393224 | tf_op jit(solution)/shard_map/ppermute | solution.py:272
  40.7 3.1 %collective-permute-done.12.s_ref = f32[136,128]{1,0:T(8,128)S(1)} collective-permute-done((f32[136,128]{1,0:T(8,128)S(1)}, f32[136,128]{1,0:T(8,128)S(1)}, u32[]{:S(2)}, u32[]{:S(2)}) %collective-permute-start.12) | collective-permute-done | bytes 69664 | tf_op jit(solution)/shard_map/ppermute | solution.py:272
  43.8 1.9 %turn.4 = (f32[768,128]{1,0:T(8,128)S(1)}, f32[768,128]{1,0:T(8,128)S(1)}) custom-call(f32[136,128]{1,0:T(8,128)S(1)} %collective-permute-done.12.s_ref, f32[576,128]{1,0:T(8,128)S(1)} %get-tuple-element.36.refs_0_, f32[768,128]{1,0:T(8,128)S(1)} %collective-permute-done.13.refs_1_, f32[192,128]{1,0:T(8,128)S(1)} %collective-permute-done.8.refs_2_), custom_call_target="tpu_custom_call" | custom-call | flops 1000000000 | bytes 3500001 | tf_op jit(solution)/shard_map/turn/pallas_call | solution.py:258
  45.7 0.2 collective-permute-done.14.tail_ref
  45.9 0.7 %join.4 = (f32[1024,256]{1,0:T(8,128)S(1)}, f32[264,128]{1,0:T(8,128)S(1)}, f32[896,128]{1,0:T(8,128)S(1)}) custom-call(f32[1024,128]{1,0:T(8,128)S(1)} %get-tuple-element.35.staying_ref, f32[768,128]{1,0:T(8,128)S(1)} %get-tuple-element.39.moving_ref, f32[256,128]{1,0:T(8,128)S(1)} %collective-permute-done.14.tail_ref), custom_call_target="tpu_custom_call" | custom-call | flops 2000000000 | bytes 7000001 | tf_op jit(solution)/shard_map/join/pallas_call | solution.py:258
  46.8 1.3 %collective-permute-done.15 = f32[264,128]{1,0:T(8,128)S(1)} collective-permute-done((f32[264,128]{1,0:T(8,128)S(1)}, f32[264,128]{1,0:T(8,128)S(1)}, u32[]{:S(2)}, u32[]{:S(2)}) %collective-permute-start.15) | collective-permute-done | bytes 135200 | tf_op jit(solution)/shard_map/ppermute | solution.py:285
  48.1 2.5 %collective-permute-start.18 = (f32[264,128]{1,0:T(8,128)S(1)}, f32[264,128]{1,0:T(8,128)S(1)}, u32[]{:S(2)}, u32[]{:S(2)}) collective-permute-start(f32[264,128]{1,0:T(8,128)S(1)} %add.11.refs_0_), channel_id=1, source_target_pairs={{0,6},{1,7},{2,4},{3,5},{4,2},{5,3},{6,0},{7,1},{8,14},{9,15},{10,... | collective-permute-start | bytes 405512 | tf_op jit(solution)/shard_map/ppermute | solution.py:285
  50.6 0.3 collective-permute-start.17
  50.9 0.8 %collective-permute-start.16 = (f32[264,128]{1,0:T(8,128)S(1)}, f32[264,128]{1,0:T(8,128)S(1)}, u32[]{:S(2)}, u32[]{:S(2)}) collective-permute-start(f32[264,128]{1,0:T(8,128)S(1)} %add.11.refs_0_), channel_id=1, source_target_pairs={{0,2},{1,3},{2,0},{3,1},{4,6},{5,7},{6,4},{7,5},{8,10},{9,11},{10,... | collective-permute-start | bytes 405512 | tf_op jit(solution)/shard_map/ppermute | solution.py:285
  51.7 0.4 collective-permute-start.21
  52.1 3.1 %collective-permute-done.18.refs_3_ = f32[264,128]{1,0:T(8,128)S(1)} collective-permute-done((f32[264,128]{1,0:T(8,128)S(1)}, f32[264,128]{1,0:T(8,128)S(1)}, u32[]{:S(2)}, u32[]{:S(2)}) %collective-permute-start.18) | collective-permute-done | bytes 135200 | tf_op jit(solution)/shard_map/ppermute | solution.py:285
  55.1 2.5 %collective-permute-done.17.refs_2_ = f32[264,128]{1,0:T(8,128)S(1)} collective-permute-done((f32[264,128]{1,0:T(8,128)S(1)}, f32[264,128]{1,0:T(8,128)S(1)}, u32[]{:S(2)}, u32[]{:S(2)}) %collective-permute-start.17) | collective-permute-done | bytes 135200 | tf_op jit(solution)/shard_map/ppermute | solution.py:285
  57.7 0.1 ratio.5
  57.8 0.6 collective-permute-start.19
  58.5 2.3 %own.5 = (f32[1024,128]{1,0:T(8,128)S(1)}, f32[136,128]{1,0:T(8,128)S(1)}, f32[8,128]{1,0:T(8,128)S(1)}) custom-call(f32[136,128]{1,0:T(8,128)S(1)} %get-tuple-element.42.s_ref, f32[1024,256]{1,0:T(8,128)S(1)} %get-tuple-element.43.pair_ref, f32[264,128]{1,0:T(8,128)S(1)} %get-tuple-element.44.refs_0_), custom_call_target="tpu_custom_call" | custom-call | flops 800000000 | bytes 2800001 | tf_op jit(solution)/shard_map/own/pallas_call | solution.py:258
  60.8 1.3 %collective-permute-start.22 = (f32[136,128]{1,0:T(8,128)S(1)}, f32[136,128]{1,0:T(8,128)S(1)}, u32[]{:S(2)}, u32[]{:S(2)}) collective-permute-start(f32[136,128]{1,0:T(8,128)S(1)} %get-tuple-element.50), channel_id=1, source_target_pairs={{0,8},{8,16},{16,24},{24,0},{1,9},{9,17},{17,25},{25,1},{2,10},{10... | collective-permute-start | bytes 208904 | tf_op jit(solution)/shard_map/ppermute | solution.py:272
  62.1 1.2 %collective-permute-done.21.refs_2_ = f32[128,128]{1,0:T(8,128)S(1)} collective-permute-done((f32[128,128]{1,0:T(8,128)S(1)}, f32[128,128]{1,0:T(8,128)S(1)}, u32[]{:S(2)}, u32[]{:S(2)}) %collective-permute-start.21) | collective-permute-done | bytes 65568 | tf_op jit(solution)/shard_map/ppermute | solution.py:272
  63.3 1.0 %collective-permute-done.19.s_ref = f32[136,128]{1,0:T(8,128)S(1)} collective-permute-done((f32[136,128]{1,0:T(8,128)S(1)}, f32[136,128]{1,0:T(8,128)S(1)}, u32[]{:S(2)}, u32[]{:S(2)}) %collective-permute-start.19) | collective-permute-done | bytes 69664 | tf_op jit(solution)/shard_map/ppermute | solution.py:272
  64.4 1.9 %turn.5.moving_ref = f32[896,128]{1,0:T(8,128)S(1)} custom-call(f32[136,128]{1,0:T(8,128)S(1)} %collective-permute-done.19.s_ref, f32[768,128]{1,0:T(8,128)S(1)} %get-tuple-element.46.refs_0_, f32[896,128]{1,0:T(8,128)S(1)} %collective-permute-done.20.refs_1_, f32[128,128]{1,0:T(8,128)S(1)} %collective-permute-done.21.refs_2_), custom_call_target="tpu_custom_call" | custom-call | flops 1000000000 | bytes 3500001 | tf_op jit(solution)/shard_map/turn/pallas_call | solution.py:258
  66.3 0.6 collective-permute-done.22.tail_ref
  66.9 1.1 %join.5 = (f32[1024,256]{1,0:T(8,128)}, f32[1,256]{1,0:T(1,128)}) custom-call(f32[1024,128]{1,0:T(8,128)S(1)} %get-tuple-element.45.staying_ref, f32[896,128]{1,0:T(8,128)S(1)} %turn.5.moving_ref, f32[136,128]{1,0:T(8,128)S(1)} %collective-permute-done.22.tail_ref, f32[8,128]{1,0:T(8,128)S(1)} %get-tuple-element.51.refs_0_), custom_call_target="tpu_custom_call" | custom-call | flops 500000000 | bytes 1750001 | tf_op jit(solution)/shard_map/join/pallas_call | solution.py:258
  (23 shorter events, 1.0 us)
Async XLA Ops:
  0.6 4.3 %copy-start = (f32[1024,256]{1,0:T(8,128)S(1)}, f32[1024,256]{1,0:T(8,128)}, u32[]{:S(2)}) copy-start(f32[1024,256]{1,0:T(8,128)} %pair_ref.3) | copy-start | bytes 3145732
  1.8 20.8 %collective-permute-start.5 = (f32[576,256]{1,0:T(8,128)S(1)}, f32[576,256]{1,0:T(8,128)S(1)}, u32[]{:S(2)}, u32[]{:S(2)}) collective-permute-start(f32[576,256]{1,0:T(8,128)S(1)} %slice.3), channel_id=1, source_target_pairs={{0,8},{8,16},{16,24},{24,0},{1,9},{9,17},{17,25},{25,1},{2,10},{10... | collective-permute-start | bytes 1769480 | tf_op jit(solution)/shard_map/ppermute | solution.py:272
  5.3 4.9 %copy-start.1 = (s32[3,1]{0,1:T(1,128)S(1)}, s32[3,1]{0,1:T(1,128)}, u32[]{:S(2)}) copy-start(s32[3,1]{0,1:T(1,128)} %param.3) | copy-start | bytes 40
  5.3 1.3 %collective-permute-start = (f32[136,128]{1,0:T(8,128)S(1)}, f32[136,128]{1,0:T(8,128)S(1)}, u32[]{:S(2)}, u32[]{:S(2)}) collective-permute-start(f32[136,128]{1,0:T(8,128)S(1)} %gram.1), channel_id=1, source_target_pairs={{0,1},{1,0},{2,3},{3,2},{4,5},{5,4},{6,7},{7,6},{8,9},{9,8},{10,11... | collective-permute-start | bytes 208904 | tf_op jit(solution)/shard_map/ppermute | solution.py:285
  6.6 5.3 %collective-permute-start.3 = (f32[136,128]{1,0:T(8,128)S(1)}, f32[136,128]{1,0:T(8,128)S(1)}, u32[]{:S(2)}, u32[]{:S(2)}) collective-permute-start(f32[136,128]{1,0:T(8,128)S(1)} %add.9.refs_0_), channel_id=1, source_target_pairs={{0,6},{1,7},{2,4},{3,5},{4,2},{5,3},{6,0},{7,1},{8,14},{9,15},{10,... | collective-permute-start | bytes 208904 | tf_op jit(solution)/shard_map/ppermute | solution.py:285
  9.2 4.3 %collective-permute-start.2 = (f32[136,128]{1,0:T(8,128)S(1)}, f32[136,128]{1,0:T(8,128)S(1)}, u32[]{:S(2)}, u32[]{:S(2)}) collective-permute-start(f32[136,128]{1,0:T(8,128)S(1)} %add.9.refs_0_), channel_id=1, source_target_pairs={{0,4},{1,5},{2,6},{3,7},{4,0},{5,1},{6,2},{7,3},{8,12},{9,13},{10,... | collective-permute-start | bytes 208904 | tf_op jit(solution)/shard_map/ppermute | solution.py:285
  9.7 4.3 %collective-permute-start.1 = (f32[136,128]{1,0:T(8,128)S(1)}, f32[136,128]{1,0:T(8,128)S(1)}, u32[]{:S(2)}, u32[]{:S(2)}) collective-permute-start(f32[136,128]{1,0:T(8,128)S(1)} %add.9.refs_0_), channel_id=1, source_target_pairs={{0,2},{1,3},{2,0},{3,1},{4,6},{5,7},{6,4},{7,5},{8,10},{9,11},{10,... | collective-permute-start | bytes 208904 | tf_op jit(solution)/shard_map/ppermute | solution.py:285
  14.2 8.4 %collective-permute-start.4 = (f32[136,128]{1,0:T(8,128)S(1)}, f32[136,128]{1,0:T(8,128)S(1)}, u32[]{:S(2)}, u32[]{:S(2)}) collective-permute-start(f32[136,128]{1,0:T(8,128)S(1)} %ratio.3.s_ref), channel_id=1, source_target_pairs={{0,8},{8,16},{16,24},{24,0},{1,9},{9,17},{17,25},{25,1},{2,10},{10... | collective-permute-start | bytes 208904 | tf_op jit(solution)/shard_map/ppermute | solution.py:272
  17.8 9.9 %collective-permute-start.6 = (f32[448,128]{1,0:T(8,128)S(1)}, f32[448,128]{1,0:T(8,128)S(1)}, u32[]{:S(2)}, u32[]{:S(2)}) collective-permute-start(f32[448,128]{1,0:T(8,128)S(1)} %get-tuple-element.30), channel_id=1, source_target_pairs={{0,8},{8,16},{16,24},{24,0},{1,9},{9,17},{17,25},{25,1},{2,10},{10... | collective-permute-start | bytes 688136 | tf_op jit(solution)/shard_map/ppermute | solution.py:272
  19.4 10.1 %collective-permute-start.8 = (f32[192,128]{1,0:T(8,128)S(1)}, f32[192,128]{1,0:T(8,128)S(1)}, u32[]{:S(2)}, u32[]{:S(2)}) collective-permute-start(f32[192,128]{1,0:T(8,128)S(1)} %get-tuple-element.32), channel_id=1, source_target_pairs={{0,8},{8,16},{16,24},{24,0},{1,9},{9,17},{17,25},{25,1},{2,10},{10... | collective-permute-start | bytes 294920 | tf_op jit(solution)/shard_map/ppermute | solution.py:272
  28.2 1.3 %collective-permute-start.7 = (f32[136,128]{1,0:T(8,128)S(1)}, f32[136,128]{1,0:T(8,128)S(1)}, u32[]{:S(2)}, u32[]{:S(2)}) collective-permute-start(f32[136,128]{1,0:T(8,128)S(1)} %get-tuple-element.31), channel_id=1, source_target_pairs={{0,1},{1,0},{2,3},{3,2},{4,5},{5,4},{6,7},{7,6},{8,9},{9,8},{10,11... | collective-permute-start | bytes 208904 | tf_op jit(solution)/shard_map/ppermute | solution.py:285
  28.2 15.5 %collective-permute-start.13 = (f32[768,128]{1,0:T(8,128)S(1)}, f32[768,128]{1,0:T(8,128)S(1)}, u32[]{:S(2)}, u32[]{:S(2)}) collective-permute-start(f32[768,128]{1,0:T(8,128)S(1)} %get-tuple-element.37), channel_id=1, source_target_pairs={{0,8},{8,16},{16,24},{24,0},{1,9},{9,17},{17,25},{25,1},{2,10},{10... | collective-permute-start | bytes 1179656 | tf_op jit(solution)/shard_map/ppermute | solution.py:272
  29.5 5.3 %collective-permute-start.11 = (f32[136,128]{1,0:T(8,128)S(1)}, f32[136,128]{1,0:T(8,128)S(1)}, u32[]{:S(2)}, u32[]{:S(2)}) collective-permute-start(f32[136,128]{1,0:T(8,128)S(1)} %add.10.refs_0_), channel_id=1, source_target_pairs={{0,6},{1,7},{2,4},{3,5},{4,2},{5,3},{6,0},{7,1},{8,14},{9,15},{10,... | collective-permute-start | bytes 208904 | tf_op jit(solution)/shard_map/ppermute | solution.py:285
  32.0 4.3 %collective-permute-start.10 = (f32[136,128]{1,0:T(8,128)S(1)}, f32[136,128]{1,0:T(8,128)S(1)}, u32[]{:S(2)}, u32[]{:S(2)}) collective-permute-start(f32[136,128]{1,0:T(8,128)S(1)} %add.10.refs_0_), channel_id=1, source_target_pairs={{0,4},{1,5},{2,6},{3,7},{4,0},{5,1},{6,2},{7,3},{8,12},{9,13},{10,... | collective-permute-start | bytes 208904 | tf_op jit(solution)/shard_map/ppermute | solution.py:285
  32.4 4.3 %collective-permute-start.9 = (f32[136,128]{1,0:T(8,128)S(1)}, f32[136,128]{1,0:T(8,128)S(1)}, u32[]{:S(2)}, u32[]{:S(2)}) collective-permute-start(f32[136,128]{1,0:T(8,128)S(1)} %add.10.refs_0_), channel_id=1, source_target_pairs={{0,2},{1,3},{2,0},{3,1},{4,6},{5,7},{6,4},{7,5},{8,10},{9,11},{10,... | collective-permute-start | bytes 208904 | tf_op jit(solution)/shard_map/ppermute | solution.py:285
  36.8 7.0 %collective-permute-start.12 = (f32[136,128]{1,0:T(8,128)S(1)}, f32[136,128]{1,0:T(8,128)S(1)}, u32[]{:S(2)}, u32[]{:S(2)}) collective-permute-start(f32[136,128]{1,0:T(8,128)S(1)} %ratio.4.s_ref), channel_id=1, source_target_pairs={{0,8},{8,16},{16,24},{24,0},{1,9},{9,17},{17,25},{25,1},{2,10},{10... | collective-permute-start | bytes 208904 | tf_op jit(solution)/shard_map/ppermute | solution.py:272
  39.1 6.8 %collective-permute-start.14 = (f32[256,128]{1,0:T(8,128)S(1)}, f32[256,128]{1,0:T(8,128)S(1)}, u32[]{:S(2)}, u32[]{:S(2)}) collective-permute-start(f32[256,128]{1,0:T(8,128)S(1)} %get-tuple-element.40), channel_id=1, source_target_pairs={{0,8},{8,16},{16,24},{24,0},{1,9},{9,17},{17,25},{25,1},{2,10},{10... | collective-permute-start | bytes 393224 | tf_op jit(solution)/shard_map/ppermute | solution.py:272
  46.7 1.4 %collective-permute-start.15 = (f32[264,128]{1,0:T(8,128)S(1)}, f32[264,128]{1,0:T(8,128)S(1)}, u32[]{:S(2)}, u32[]{:S(2)}) collective-permute-start(f32[264,128]{1,0:T(8,128)S(1)} %get-tuple-element.41), channel_id=1, source_target_pairs={{0,1},{1,0},{2,3},{3,2},{4,5},{5,4},{6,7},{7,6},{8,9},{9,8},{10,11... | collective-permute-start | bytes 405512 | tf_op jit(solution)/shard_map/ppermute | solution.py:285
  46.7 17.6 %collective-permute-start.20 = (f32[896,128]{1,0:T(8,128)S(1)}, f32[896,128]{1,0:T(8,128)S(1)}, u32[]{:S(2)}, u32[]{:S(2)}) collective-permute-start(f32[896,128]{1,0:T(8,128)S(1)} %get-tuple-element.47), channel_id=1, source_target_pairs={{0,8},{8,16},{16,24},{24,0},{1,9},{9,17},{17,25},{25,1},{2,10},{10... | collective-permute-start | bytes 1376264 | tf_op jit(solution)/shard_map/ppermute | solution.py:272
  48.1 7.0 %collective-permute-start.18 = (f32[264,128]{1,0:T(8,128)S(1)}, f32[264,128]{1,0:T(8,128)S(1)}, u32[]{:S(2)}, u32[]{:S(2)}) collective-permute-start(f32[264,128]{1,0:T(8,128)S(1)} %add.11.refs_0_), channel_id=1, source_target_pairs={{0,6},{1,7},{2,4},{3,5},{4,2},{5,3},{6,0},{7,1},{8,14},{9,15},{10,... | collective-permute-start | bytes 405512 | tf_op jit(solution)/shard_map/ppermute | solution.py:285
  50.6 7.0 %collective-permute-start.17 = (f32[264,128]{1,0:T(8,128)S(1)}, f32[264,128]{1,0:T(8,128)S(1)}, u32[]{:S(2)}, u32[]{:S(2)}) collective-permute-start(f32[264,128]{1,0:T(8,128)S(1)} %add.11.refs_0_), channel_id=1, source_target_pairs={{0,4},{1,5},{2,6},{3,7},{4,0},{5,1},{6,2},{7,3},{8,12},{9,13},{10,... | collective-permute-start | bytes 405512 | tf_op jit(solution)/shard_map/ppermute | solution.py:285
  50.9 6.8 %collective-permute-start.16 = (f32[264,128]{1,0:T(8,128)S(1)}, f32[264,128]{1,0:T(8,128)S(1)}, u32[]{:S(2)}, u32[]{:S(2)}) collective-permute-start(f32[264,128]{1,0:T(8,128)S(1)} %add.11.refs_0_), channel_id=1, source_target_pairs={{0,2},{1,3},{2,0},{3,1},{4,6},{5,7},{6,4},{7,5},{8,10},{9,11},{10,... | collective-permute-start | bytes 405512 | tf_op jit(solution)/shard_map/ppermute | solution.py:285
  51.7 11.7 %collective-permute-start.21 = (f32[128,128]{1,0:T(8,128)S(1)}, f32[128,128]{1,0:T(8,128)S(1)}, u32[]{:S(2)}, u32[]{:S(2)}) collective-permute-start(f32[128,128]{1,0:T(8,128)S(1)} %get-tuple-element.49), channel_id=1, source_target_pairs={{0,8},{8,16},{16,24},{24,0},{1,9},{9,17},{17,25},{25,1},{2,10},{10... | collective-permute-start | bytes 196616 | tf_op jit(solution)/shard_map/ppermute | solution.py:272
  57.8 6.5 %collective-permute-start.19 = (f32[136,128]{1,0:T(8,128)S(1)}, f32[136,128]{1,0:T(8,128)S(1)}, u32[]{:S(2)}, u32[]{:S(2)}) collective-permute-start(f32[136,128]{1,0:T(8,128)S(1)} %get-tuple-element.42.s_ref), channel_id=1, source_target_pairs={{0,8},{8,16},{16,24},{24,0},{1,9},{9,17},{17,25},{25,1},{2,10},{10... | collective-permute-start | bytes 208904 | tf_op jit(solution)/shard_map/ppermute | solution.py:272
  60.8 6.2 %collective-permute-start.22 = (f32[136,128]{1,0:T(8,128)S(1)}, f32[136,128]{1,0:T(8,128)S(1)}, u32[]{:S(2)}, u32[]{:S(2)}) collective-permute-start(f32[136,128]{1,0:T(8,128)S(1)} %get-tuple-element.50), channel_id=1, source_target_pairs={{0,8},{8,16},{16,24},{24,0},{1,9},{9,17},{17,25},{25,1},{2,10},{10... | collective-permute-start | bytes 208904 | tf_op jit(solution)/shard_map/ppermute | solution.py:272
